TPU v7x, 32 devices: a whole 2x2x4 slice. The times are simulated.
32 devices in a mesh: section: 2 (over x), ctx: 16 (over z, y, core).
Axes of the slice: x: 2, y: 2, z: 4, core: 2. Of those that a mesh axis runs over, the one named last changes fastest.
Arguments:
- stream: bfloat16 [2, 3072, 8192], P('section', 'ctx'), may hold values from -1.5 to 1.5
- queries: bfloat16 [2, 3072, 8192], P('section', 'ctx'), may hold values from -24 to 24
- keys: bfloat16 [2, 3072, 1024], P('section', 'ctx'), may hold values from -24 to 24
- values: bfloat16 [2, 3072, 1024], P('section', 'ctx'), may hold values from -6 to 6
- segments: int32 [2, 3072], P('section', 'ctx'), may hold values from 0 to 7, never falling along the last dimension, each value on 1 to 1344 neighbouring positions
Outputs:
- next_stream: bfloat16 [2, 3072, 8192], P('section', 'ctx')
Inputs may be any that keep to these rules, and one draw needn't show every extreme that they name: `segments`: along each micro-batch the numbers never fall; each document holds at most (7) * 192 tokens, and one holds exactly that many.
All inputs are finite; a program needn't handle non-finite values.
Results may differ from a plain program's by a relative error of at most 0.0095.
Values may be sent and summed in bfloat16 or wider, within the bound.
No kernel may reach another device: no remote copies, remote signals or barrier semaphores. Data moves between devices by JAX's collectives and lax.ppermute only.
A program may use at most 128 MiB of HBM per device.

v0:
```python
import jax
import jax.numpy as jnp
from jax import lax
from jax.sharding import PartitionSpec as P

HQ = 64
KVH = 8
HD = 128
WINDOW = 8


def shifted(value, axis, by):
    size = lax.axis_size(axis)
    pairs = [(i, i + by) for i in range(size) if 0 <= i + by < size]
    return lax.ppermute(value, axis, pairs)


def from_behind(value, axis, by):
    size = lax.axis_size(axis)
    return lax.ppermute(value, axis, [(i, (i + by) % size) for i in range(size)])


def attend_window(query_rows, key_rows, value_rows, seg_query, seg_key, pos_query, pos_key):
    tok_count = query_rows.shape[0]
    key_count = key_rows.shape[0]
    repeat = HQ // KVH
    query_groups = jnp.moveaxis(query_rows.reshape(tok_count, KVH, repeat, HD), 1, 0)
    key_groups = jnp.moveaxis(key_rows.reshape(key_count, KVH, HD), 1, 0)
    value_groups = jnp.moveaxis(value_rows.reshape(key_count, KVH, HD), 1, 0)
    visible = (
        (seg_query[:, None] == seg_key[None, :])
        & (pos_key[None, :] <= pos_query[:, None])
        & (pos_key[None, :] >= 0)
    )

    def one_group(group_parts):
        query_group, key_group, value_group = group_parts
        scores = jnp.einsum(
            "trd,ld->rtl", query_group, key_group, preferred_element_type=jnp.float32
        ) * HD ** (-0.5)
        scores = jnp.where(visible[None, :, :], scores, jnp.float32(-1e30))
        top_score = jnp.max(scores, axis=-1, keepdims=True)
        expo = jnp.exp(scores - top_score)
        probs = (expo / jnp.sum(expo, axis=-1, keepdims=True)).astype(jnp.bfloat16)
        return jnp.einsum("rtl,ld->trd", probs, value_group, preferred_element_type=jnp.float32)

    group_out = lax.map(one_group, (query_groups, key_groups, value_groups))
    return jnp.moveaxis(group_out, 0, 1).reshape(tok_count, HQ * HD)


def local(stream, queries, keys, values, segments):
    tok_rows = queries.shape[1]
    kv_width = keys.shape[2]
    ctx_index = lax.axis_index("ctx")
    own_pair = jnp.concatenate([keys[0], values[0]], axis=1)
    own_seg = segments[0]
    pair_list = [own_pair]
    seg_list = [own_seg]
    moving = (own_pair, own_seg)
    for back_step in range(WINDOW - 1):
        moving = shifted((moving[0], moving[1]), "ctx", 1)
        pair_list.insert(0, moving[0])
        seg_list.insert(0, moving[1])
    window_pair = jnp.concatenate(pair_list, axis=0)
    window_seg = jnp.concatenate(seg_list, axis=0)
    window_keys = window_pair[:, :kv_width]
    window_values = window_pair[:, kv_width:]
    pos_query = ctx_index * tok_rows + jnp.arange(tok_rows, dtype=jnp.int32)
    pos_key = (ctx_index - (WINDOW - 1)) * tok_rows + jnp.arange(WINDOW * tok_rows, dtype=jnp.int32)
    query_rows = queries[0]
    attended = attend_window(
        query_rows, window_keys, window_values, own_seg, window_seg, pos_query, pos_key
    )
    updated = (stream[0].astype(jnp.float32) + attended).astype(jnp.bfloat16)
    return from_behind(updated[None], "section", 1)


def solution(mesh):
    in_specs = (
        P("section", "ctx", None),
        P("section", "ctx", None),
        P("section", "ctx", None),
        P("section", "ctx", None),
        P("section", "ctx"),
    )
    out_specs = P("section", "ctx", None)
    return jax.shard_map(local, mesh=mesh, in_specs=in_specs, out_specs=out_specs, check_vma=False)
```

profile of v0, /device:TPU:18, one launch (start us, length us, event | category | flops | bytes accessed | tf_op | source)
XLA Modules:
  0.0 385.1 jit_solution(10449688966374409563)
XLA Ops:
  5.0 12.3 %collective-permute-done = bf16[192,2048]{1,0:T(8,128)(2,1)S(1)} collective-permute-done((bf16[192,2048]{1,0:T(8,128)(2,1)S(1)}, bf16[192,2048]{1,0:T(8,128)(2,1)S(1)}, u32[]{:S(2)}, u32[]{:S(2)}) %collective-permute-start) | collective-permute-done | bytes 786464 | tf_op jit(solution)/shard_map/ppermute | solution.py:15
  19.2 12.3 %collective-permute-done.1 = bf16[192,2048]{1,0:T(8,128)(2,1)S(1)} collective-permute-done((bf16[192,2048]{1,0:T(8,128)(2,1)S(1)}, bf16[192,2048]{1,0:T(8,128)(2,1)S(1)}, u32[]{:S(2)}, u32[]{:S(2)}) %collective-permute-start.1) | collective-permute-done | bytes 786464 | tf_op jit(solution)/shard_map/ppermute | solution.py:15
  33.4 12.3 %collective-permute-done.2 = bf16[192,2048]{1,0:T(8,128)(2,1)S(1)} collective-permute-done((bf16[192,2048]{1,0:T(8,128)(2,1)S(1)}, bf16[192,2048]{1,0:T(8,128)(2,1)S(1)}, u32[]{:S(2)}, u32[]{:S(2)}) %collective-permute-start.2) | collective-permute-done | bytes 786464 | tf_op jit(solution)/shard_map/ppermute | solution.py:15
  48.5 12.3 %collective-permute-done.3 = bf16[192,2048]{1,0:T(8,128)(2,1)S(1)} collective-permute-done((bf16[192,2048]{1,0:T(8,128)(2,1)S(1)}, bf16[192,2048]{1,0:T(8,128)(2,1)S(1)}, u32[]{:S(2)}, u32[]{:S(2)}) %collective-permute-start.3) | collective-permute-done | bytes 786464 | tf_op jit(solution)/shard_map/ppermute | solution.py:15
  63.7 12.3 %collective-permute-done.4 = bf16[192,2048]{1,0:T(8,128)(2,1)S(1)} collective-permute-done((bf16[192,2048]{1,0:T(8,128)(2,1)S(1)}, bf16[192,2048]{1,0:T(8,128)(2,1)S(1)}, u32[]{:S(2)}, u32[]{:S(2)}) %collective-permute-start.4) | collective-permute-done | bytes 786464 | tf_op jit(solution)/shard_map/ppermute | solution.py:15
  78.8 12.4 %collective-permute-done.5 = bf16[192,2048]{1,0:T(8,128)(2,1)} collective-permute-done((bf16[192,2048]{1,0:T(8,128)(2,1)S(1)}, bf16[192,2048]{1,0:T(8,128)(2,1)}, u32[]{:S(2)}, u32[]{:S(2)}) %collective-permute-start.5) | collective-permute-done | bytes 786464 | tf_op jit(solution)/shard_map/ppermute | solution.py:15
  95.0 10.7 %collective-permute-done.7 = s32[192]{0:T(256)S(1)} collective-permute-done((s32[192]{0:T(256)}, s32[192]{0:T(256)S(1)}, u32[]{:S(2)}, u32[]{:S(2)}) %collective-permute-start.7) | collective-permute-done | bytes 800 | tf_op jit(solution)/shard_map/ppermute | solution.py:15
  107.6 3.9 %collective-permute-done.8 = s32[192]{0:T(256)S(1)} collective-permute-done((s32[192]{0:T(256)S(1)}, s32[192]{0:T(256)S(1)}, u32[]{:S(2)}, u32[]{:S(2)}) %collective-permute-start.8) | collective-permute-done | bytes 800 | tf_op jit(solution)/shard_map/ppermute | solution.py:15
  113.4 3.9 %collective-permute-done.9 = s32[192]{0:T(256)S(1)} collective-permute-done((s32[192]{0:T(256)S(1)}, s32[192]{0:T(256)S(1)}, u32[]{:S(2)}, u32[]{:S(2)}) %collective-permute-start.9) | collective-permute-done | bytes 800 | tf_op jit(solution)/shard_map/ppermute | solution.py:15
  136.7 4.4 %copy.30 = bf16[24,8,64,128]{3,2,1,0:T(8,128)(2,1)} copy(bf16[24,8,64,128]{3,1,2,0:T(8,128)(2,1)} %bitcast.77) | data formatting | bytes 6291456
  154.3 11.8 %concatenate.10 = bf16[1536,2048]{0,1:T(8,128)(2,1)} concatenate(bf16[192,2048]{0,1:T(8,128)(2,1)} %copy.16, bf16[192,2048]{0,1:T(8,128)(2,1)} %copy.17, bf16[192,2048]{0,1:T(8,128)(2,1)} %copy.18, bf16[192,2048]{0,1:T(8,128)(2,1)} %copy.19, bf16[192,2048]{0,1:T(8,128)(2,1)} %copy.20, bf16[192,2048]{0,1:T(8,128)(2,1)S(1)} %copy.21, bf16[192,2048]{0,1:T(8,128)(2,1)S(1)} %copy.22, ...), dimensions={0} | concatenate | bytes 12582912 | tf_op jit(solution)/shard_map/concatenate | solution.py:64
  166.1 6.0 %fusion.37 = (bf16[1536,1024]{0,1:T(8,128)(2,1)}, bf16[1536,1024]{0,1:T(8,128)(2,1)}) fusion(bf16[1536,2048]{0,1:T(8,128)(2,1)} %concatenate.10), kind=kLoop, calls=%fused_computation.34 | loop fusion | bytes 12582912 | tf_op jit(solution)/shard_map/slice | solution.py:66
  172.1 124.1 %while.11 = (s32[]{:T(128)}, f32[8,192,8,128]{3,1,2,0:T(8,128)}, bf16[8,1536,128]{1,2,0:T(8,128)(2,1)}, bf16[8,1536,128]{1,2,0:T(8,128)(2,1)}, bf16[8,192,8,128]...) while((s32[]{:T(128)}, f32[8,192,8,128]{3,1,2,0:T(8,128)}, ...), condition=%wide.region_3.4_spmd.clone, body=%wide.region_0.3_spmd.clone.sunk | while | flops 1223296512 | bytes 22246000 | solution.py:47
  173.5 8.0 %fusion.44 = (f32[8,192]{1,0:T(8,128)S(1)}, f32[8,192,1536]{2,1,0:T(8,128)}) fusion(pred[192,1536]{1,0:T(8,128)(4,1)S(1)} %and_and_fusion.2, bf16[1,192,8,128]{3,2,0,1:T(8,128)(2,1)S(1)} %constant_dynamic-slice_fusion.2, bf16[8,1536,128]{1,2,0:T(8,128)(2,1)} %get-tuple-element.199, s32[]{:T(128)} %get-tuple-element.185), kind=kOutput, calls=%fused_computation.33.clone.1 | convolution fusion | flops 613418496 | bytes 10525184 | tf_op jit(solution)/shard_map/while/body/eval_jaxpr/sub | solution.py:43
  181.4 6.1 %fusion.45 = f32[8,192,8,128]{3,1,2,0:T(8,128)} fusion(f32[8,192,8,128]{3,1,2,0:T(8,128)} %get-tuple-element.186, s32[]{:T(128)} %get-tuple-element.185, f32[8,192,1536]{2,1,0:T(8,128)} %get-tuple-element.172, f32[8,192]{1,0:T(8,128)S(1)} %get-tuple-element.173, bf16[8,1536,128]{1,2,0:T(8,128)(2,1)} %get-tuple-element.198), kind=kOutput, calls=%fused_computation.11.clone.1 | convolution fusion | flops 608698368 | bytes 10624000 | tf_op jit(solution)/shard_map/while/body/eval_jaxpr/rtl,ld->trd/dot_general | solution.py:45
  188.9 8.0 %fusion.44 = (f32[8,192]{1,0:T(8,128)S(1)}, f32[8,192,1536]{2,1,0:T(8,128)}) fusion(pred[192,1536]{1,0:T(8,128)(4,1)S(1)} %and_and_fusion.2, bf16[1,192,8,128]{3,2,0,1:T(8,128)(2,1)S(1)} %constant_dynamic-slice_fusion.2, bf16[8,1536,128]{1,2,0:T(8,128)(2,1)} %get-tuple-element.199, s32[]{:T(128)} %get-tuple-element.185), kind=kOutput, calls=%fused_computation.33.clone.1 | convolution fusion | flops 613418496 | bytes 10525184 | tf_op jit(solution)/shard_map/while/body/eval_jaxpr/sub | solution.py:43
  196.9 6.2 %fusion.45 = f32[8,192,8,128]{3,1,2,0:T(8,128)} fusion(f32[8,192,8,128]{3,1,2,0:T(8,128)} %get-tuple-element.186, s32[]{:T(128)} %get-tuple-element.185, f32[8,192,1536]{2,1,0:T(8,128)} %get-tuple-element.172, f32[8,192]{1,0:T(8,128)S(1)} %get-tuple-element.173, bf16[8,1536,128]{1,2,0:T(8,128)(2,1)} %get-tuple-element.198), kind=kOutput, calls=%fused_computation.11.clone.1 | convolution fusion | flops 608698368 | bytes 10624000 | tf_op jit(solution)/shard_map/while/body/eval_jaxpr/rtl,ld->trd/dot_general | solution.py:45
  204.4 8.0 %fusion.44 = (f32[8,192]{1,0:T(8,128)S(1)}, f32[8,192,1536]{2,1,0:T(8,128)}) fusion(pred[192,1536]{1,0:T(8,128)(4,1)S(1)} %and_and_fusion.2, bf16[1,192,8,128]{3,2,0,1:T(8,128)(2,1)S(1)} %constant_dynamic-slice_fusion.2, bf16[8,1536,128]{1,2,0:T(8,128)(2,1)} %get-tuple-element.199, s32[]{:T(128)} %get-tuple-element.185), kind=kOutput, calls=%fused_computation.33.clone.1 | convolution fusion | flops 613418496 | bytes 10525184 | tf_op jit(solution)/shard_map/while/body/eval_jaxpr/sub | solution.py:43
  212.4 6.1 %fusion.45 = f32[8,192,8,128]{3,1,2,0:T(8,128)} fusion(f32[8,192,8,128]{3,1,2,0:T(8,128)} %get-tuple-element.186, s32[]{:T(128)} %get-tuple-element.185, f32[8,192,1536]{2,1,0:T(8,128)} %get-tuple-element.172, f32[8,192]{1,0:T(8,128)S(1)} %get-tuple-element.173, bf16[8,1536,128]{1,2,0:T(8,128)(2,1)} %get-tuple-element.198), kind=kOutput, calls=%fused_computation.11.clone.1 | convolution fusion | flops 608698368 | bytes 10624000 | tf_op jit(solution)/shard_map/while/body/eval_jaxpr/rtl,ld->trd/dot_general | solution.py:45
  219.9 8.0 %fusion.44 = (f32[8,192]{1,0:T(8,128)S(1)}, f32[8,192,1536]{2,1,0:T(8,128)}) fusion(pred[192,1536]{1,0:T(8,128)(4,1)S(1)} %and_and_fusion.2, bf16[1,192,8,128]{3,2,0,1:T(8,128)(2,1)S(1)} %constant_dynamic-slice_fusion.2, bf16[8,1536,128]{1,2,0:T(8,128)(2,1)} %get-tuple-element.199, s32[]{:T(128)} %get-tuple-element.185), kind=kOutput, calls=%fused_computation.33.clone.1 | convolution fusion | flops 613418496 | bytes 10525184 | tf_op jit(solution)/shard_map/while/body/eval_jaxpr/sub | solution.py:43
  227.9 6.2 %fusion.45 = f32[8,192,8,128]{3,1,2,0:T(8,128)} fusion(f32[8,192,8,128]{3,1,2,0:T(8,128)} %get-tuple-element.186, s32[]{:T(128)} %get-tuple-element.185, f32[8,192,1536]{2,1,0:T(8,128)} %get-tuple-element.172, f32[8,192]{1,0:T(8,128)S(1)} %get-tuple-element.173, bf16[8,1536,128]{1,2,0:T(8,128)(2,1)} %get-tuple-element.198), kind=kOutput, calls=%fused_computation.11.clone.1 | convolution fusion | flops 608698368 | bytes 10624000 | tf_op jit(solution)/shard_map/while/body/eval_jaxpr/rtl,ld->trd/dot_general | solution.py:45
  235.4 8.0 %fusion.44 = (f32[8,192]{1,0:T(8,128)S(1)}, f32[8,192,1536]{2,1,0:T(8,128)}) fusion(pred[192,1536]{1,0:T(8,128)(4,1)S(1)} %and_and_fusion.2, bf16[1,192,8,128]{3,2,0,1:T(8,128)(2,1)S(1)} %constant_dynamic-slice_fusion.2, bf16[8,1536,128]{1,2,0:T(8,128)(2,1)} %get-tuple-element.199, s32[]{:T(128)} %get-tuple-element.185), kind=kOutput, calls=%fused_computation.33.clone.1 | convolution fusion | flops 613418496 | bytes 10525184 | tf_op jit(solution)/shard_map/while/body/eval_jaxpr/sub | solution.py:43
  243.4 6.2 %fusion.45 = f32[8,192,8,128]{3,1,2,0:T(8,128)} fusion(f32[8,192,8,128]{3,1,2,0:T(8,128)} %get-tuple-element.186, s32[]{:T(128)} %get-tuple-element.185, f32[8,192,1536]{2,1,0:T(8,128)} %get-tuple-element.172, f32[8,192]{1,0:T(8,128)S(1)} %get-tuple-element.173, bf16[8,1536,128]{1,2,0:T(8,128)(2,1)} %get-tuple-element.198), kind=kOutput, calls=%fused_computation.11.clone.1 | convolution fusion | flops 608698368 | bytes 10624000 | tf_op jit(solution)/shard_map/while/body/eval_jaxpr/rtl,ld->trd/dot_general | solution.py:45
  251.0 8.0 %fusion.44 = (f32[8,192]{1,0:T(8,128)S(1)}, f32[8,192,1536]{2,1,0:T(8,128)}) fusion(pred[192,1536]{1,0:T(8,128)(4,1)S(1)} %and_and_fusion.2, bf16[1,192,8,128]{3,2,0,1:T(8,128)(2,1)S(1)} %constant_dynamic-slice_fusion.2, bf16[8,1536,128]{1,2,0:T(8,128)(2,1)} %get-tuple-element.199, s32[]{:T(128)} %get-tuple-element.185), kind=kOutput, calls=%fused_computation.33.clone.1 | convolution fusion | flops 613418496 | bytes 10525184 | tf_op jit(solution)/shard_map/while/body/eval_jaxpr/sub | solution.py:43
  259.0 6.2 %fusion.45 = f32[8,192,8,128]{3,1,2,0:T(8,128)} fusion(f32[8,192,8,128]{3,1,2,0:T(8,128)} %get-tuple-element.186, s32[]{:T(128)} %get-tuple-element.185, f32[8,192,1536]{2,1,0:T(8,128)} %get-tuple-element.172, f32[8,192]{1,0:T(8,128)S(1)} %get-tuple-element.173, bf16[8,1536,128]{1,2,0:T(8,128)(2,1)} %get-tuple-element.198), kind=kOutput, calls=%fused_computation.11.clone.1 | convolution fusion | flops 608698368 | bytes 10624000 | tf_op jit(solution)/shard_map/while/body/eval_jaxpr/rtl,ld->trd/dot_general | solution.py:45
  266.5 8.0 %fusion.44 = (f32[8,192]{1,0:T(8,128)S(1)}, f32[8,192,1536]{2,1,0:T(8,128)}) fusion(pred[192,1536]{1,0:T(8,128)(4,1)S(1)} %and_and_fusion.2, bf16[1,192,8,128]{3,2,0,1:T(8,128)(2,1)S(1)} %constant_dynamic-slice_fusion.2, bf16[8,1536,128]{1,2,0:T(8,128)(2,1)} %get-tuple-element.199, s32[]{:T(128)} %get-tuple-element.185), kind=kOutput, calls=%fused_computation.33.clone.1 | convolution fusion | flops 613418496 | bytes 10525184 | tf_op jit(solution)/shard_map/while/body/eval_jaxpr/sub | solution.py:43
  274.5 6.2 %fusion.45 = f32[8,192,8,128]{3,1,2,0:T(8,128)} fusion(f32[8,192,8,128]{3,1,2,0:T(8,128)} %get-tuple-element.186, s32[]{:T(128)} %get-tuple-element.185, f32[8,192,1536]{2,1,0:T(8,128)} %get-tuple-element.172, f32[8,192]{1,0:T(8,128)S(1)} %get-tuple-element.173, bf16[8,1536,128]{1,2,0:T(8,128)(2,1)} %get-tuple-element.198), kind=kOutput, calls=%fused_computation.11.clone.1 | convolution fusion | flops 608698368 | bytes 10624000 | tf_op jit(solution)/shard_map/while/body/eval_jaxpr/rtl,ld->trd/dot_general | solution.py:45
  282.0 8.0 %fusion.44 = (f32[8,192]{1,0:T(8,128)S(1)}, f32[8,192,1536]{2,1,0:T(8,128)}) fusion(pred[192,1536]{1,0:T(8,128)(4,1)S(1)} %and_and_fusion.2, bf16[1,192,8,128]{3,2,0,1:T(8,128)(2,1)S(1)} %constant_dynamic-slice_fusion.2, bf16[8,1536,128]{1,2,0:T(8,128)(2,1)} %get-tuple-element.199, s32[]{:T(128)} %get-tuple-element.185), kind=kOutput, calls=%fused_computation.33.clone.1 | convolution fusion | flops 613418496 | bytes 10525184 | tf_op jit(solution)/shard_map/while/body/eval_jaxpr/sub | solution.py:43
  290.0 6.2 %fusion.45 = f32[8,192,8,128]{3,1,2,0:T(8,128)} fusion(f32[8,192,8,128]{3,1,2,0:T(8,128)} %get-tuple-element.186, s32[]{:T(128)} %get-tuple-element.185, f32[8,192,1536]{2,1,0:T(8,128)} %get-tuple-element.172, f32[8,192]{1,0:T(8,128)S(1)} %get-tuple-element.173, bf16[8,1536,128]{1,2,0:T(8,128)(2,1)} %get-tuple-element.198), kind=kOutput, calls=%fused_computation.11.clone.1 | convolution fusion | flops 608698368 | bytes 10624000 | tf_op jit(solution)/shard_map/while/body/eval_jaxpr/rtl,ld->trd/dot_general | solution.py:45
  296.2 9.1 %copy.26 = f32[192,8,8,128]{3,2,1,0:T(8,128)} copy(f32[192,8,8,128]{3,0,2,1:T(8,128)} %bitcast.76) | data formatting | bytes 12582912 | tf_op jit(solution)/shard_map/transpose | solution.py:48
  305.3 7.3 %reshape.29 = f32[1,192,8192]{2,1,0:T(8,128)} reshape(f32[192,8,8,128]{3,2,1,0:T(8,128)} %copy.26) | data formatting | bytes 12582912 | tf_op jit(solution)/shard_map/reshape | solution.py:48
  316.7 66.7 %collective-permute-done.14 = bf16[1,192,8192]{2,1,0:T(8,128)(2,1)S(1)} collective-permute-done((bf16[1,192,8192]{2,1,0:T(8,128)(2,1)S(1)}, bf16[1,192,8192]{2,1,0:T(8,128)(2,1)S(1)}, u32[]{:S(2)}, u32[]{:S(2)}) %collective-permute-start.14) | collective-permute-done | bytes 3145760 | tf_op jit(solution)/shard_map/ppermute | solution.py:20
  (66 shorter events, 74.4 us)
Async XLA Ops:
  0.0 141.1 %copy-start.5 = (s32[1,192]{1,0:T(1,128)S(1)}, s32[1,192]{1,0:T(1,128)}, u32[]{:S(2)}) copy-start(s32[1,192]{1,0:T(1,128)} %param.11) | copy-start | bytes 2308
  3.1 14.2 %collective-permute-start = (bf16[192,2048]{1,0:T(8,128)(2,1)S(1)}, bf16[192,2048]{1,0:T(8,128)(2,1)S(1)}, u32[]{:S(2)}, u32[]{:S(2)}) collective-permute-start(bf16[192,2048]{1,0:T(8,128)(2,1)S(1)} %copy.15), channel_id=1, source_target_pairs={{0,1},{1,2},{2,3},{3,4},{4,5},{5,6},{6,7},{7,8},{8,9},{9,10},{10,1... | collective-permute-start | bytes 2359304 | tf_op jit(solution)/shard_map/ppermute | solution.py:15
  17.3 14.2 %collective-permute-start.1 = (bf16[192,2048]{1,0:T(8,128)(2,1)S(1)}, bf16[192,2048]{1,0:T(8,128)(2,1)S(1)}, u32[]{:S(2)}, u32[]{:S(2)}) collective-permute-start(bf16[192,2048]{1,0:T(8,128)(2,1)S(1)} %collective-permute-done), channel_id=1, source_target_pairs={{0,1},{1,2},{2,3},{3,4},{4,5},{5,6},{6,7},{7,8},{8,9},{9,10},{10,1... | collective-permute-start | bytes 2359304 | tf_op jit(solution)/shard_map/ppermute | solution.py:15
  31.5 109.6 %copy-start.1 = (bf16[192,2048]{1,0:T(8,128)(2,1)}, bf16[192,2048]{1,0:T(8,128)(2,1)S(1)}, u32[]{:S(2)}) copy-start(bf16[192,2048]{1,0:T(8,128)(2,1)S(1)} %collective-permute-done.1) | copy-start | bytes 2359300
  31.5 14.2 %collective-permute-start.2 = (bf16[192,2048]{1,0:T(8,128)(2,1)S(1)}, bf16[192,2048]{1,0:T(8,128)(2,1)S(1)}, u32[]{:S(2)}, u32[]{:S(2)}) collective-permute-start(bf16[192,2048]{1,0:T(8,128)(2,1)S(1)} %collective-permute-done.1), channel_id=1, source_target_pairs={{0,1},{1,2},{2,3},{3,4},{4,5},{5,6},{6,7},{7,8},{8,9},{9,10},{10,1... | collective-permute-start | bytes 2359304 | tf_op jit(solution)/shard_map/ppermute | solution.py:15
  45.7 0.9 copy-start.2
  46.6 14.2 %collective-permute-start.3 = (bf16[192,2048]{1,0:T(8,128)(2,1)S(1)}, bf16[192,2048]{1,0:T(8,128)(2,1)S(1)}, u32[]{:S(2)}, u32[]{:S(2)}) collective-permute-start(bf16[192,2048]{1,0:T(8,128)(2,1)S(1)} %collective-permute-done.2), channel_id=1, source_target_pairs={{0,1},{1,2},{2,3},{3,4},{4,5},{5,6},{6,7},{7,8},{8,9},{9,10},{10,1... | collective-permute-start | bytes 2359304 | tf_op jit(solution)/shard_map/ppermute | solution.py:15
  60.8 1.0 copy-start.3
  61.8 14.2 %collective-permute-start.4 = (bf16[192,2048]{1,0:T(8,128)(2,1)S(1)}, bf16[192,2048]{1,0:T(8,128)(2,1)S(1)}, u32[]{:S(2)}, u32[]{:S(2)}) collective-permute-start(bf16[192,2048]{1,0:T(8,128)(2,1)S(1)} %collective-permute-done.3), channel_id=1, source_target_pairs={{0,1},{1,2},{2,3},{3,4},{4,5},{5,6},{6,7},{7,8},{8,9},{9,10},{10,1... | collective-permute-start | bytes 2359304 | tf_op jit(solution)/shard_map/ppermute | solution.py:15
  76.0 0.9 copy-start.4
  76.9 14.3 %collective-permute-start.5 = (bf16[192,2048]{1,0:T(8,128)(2,1)S(1)}, bf16[192,2048]{1,0:T(8,128)(2,1)}, u32[]{:S(2)}, u32[]{:S(2)}) collective-permute-start(bf16[192,2048]{1,0:T(8,128)(2,1)S(1)} %collective-permute-done.4), channel_id=1, source_target_pairs={{0,1},{1,2},{2,3},{3,4},{4,5},{5,6},{6,7},{7,8},{8,9},{9,10},{10,1... | collective-permute-start | bytes 2359304 | tf_op jit(solution)/shard_map/ppermute | solution.py:15
  91.2 60.9 %collective-permute-start.6 = (bf16[192,2048]{1,0:T(8,128)(2,1)}, bf16[192,2048]{1,0:T(8,128)(2,1)}, u32[]{:S(2)}, u32[]{:S(2)}) collective-permute-start(bf16[192,2048]{1,0:T(8,128)(2,1)} %collective-permute-done.5), channel_id=1, source_target_pairs={{0,1},{1,2},{2,3},{3,4},{4,5},{5,6},{6,7},{7,8},{8,9},{9,10},{10,1... | collective-permute-start | bytes 2359304 | tf_op jit(solution)/shard_map/ppermute | solution.py:15
  93.1 12.6 %collective-permute-start.7 = (s32[192]{0:T(256)}, s32[192]{0:T(256)S(1)}, u32[]{:S(2)}, u32[]{:S(2)}) collective-permute-start(s32[192]{0:T(256)} %bitcast.82), channel_id=1, source_target_pairs={{0,1},{1,2},{2,3},{3,4},{4,5},{5,6},{6,7},{7,8},{8,9},{9,10},{10,1... | collective-permute-start | bytes 2312 | tf_op jit(solution)/shard_map/ppermute | solution.py:15
  105.7 5.8 %collective-permute-start.8 = (s32[192]{0:T(256)S(1)}, s32[192]{0:T(256)S(1)}, u32[]{:S(2)}, u32[]{:S(2)}) collective-permute-start(s32[192]{0:T(256)S(1)} %collective-permute-done.7), channel_id=1, source_target_pairs={{0,1},{1,2},{2,3},{3,4},{4,5},{5,6},{6,7},{7,8},{8,9},{9,10},{10,1... | collective-permute-start | bytes 2312 | tf_op jit(solution)/shard_map/ppermute | solution.py:15
  111.5 5.8 %collective-permute-start.9 = (s32[192]{0:T(256)S(1)}, s32[192]{0:T(256)S(1)}, u32[]{:S(2)}, u32[]{:S(2)}) collective-permute-start(s32[192]{0:T(256)S(1)} %collective-permute-done.8), channel_id=1, source_target_pairs={{0,1},{1,2},{2,3},{3,4},{4,5},{5,6},{6,7},{7,8},{8,9},{9,10},{10,1... | collective-permute-start | bytes 2312 | tf_op jit(solution)/shard_map/ppermute | solution.py:15
  117.2 5.8 %collective-permute-start.10 = (s32[192]{0:T(256)S(1)}, s32[192]{0:T(256)S(1)}, u32[]{:S(2)}, u32[]{:S(2)}) collective-permute-start(s32[192]{0:T(256)S(1)} %collective-permute-done.9), channel_id=1, source_target_pairs={{0,1},{1,2},{2,3},{3,4},{4,5},{5,6},{6,7},{7,8},{8,9},{9,10},{10,1... | collective-permute-start | bytes 2312 | tf_op jit(solution)/shard_map/ppermute | solution.py:15
  123.0 5.8 %collective-permute-start.11 = (s32[192]{0:T(256)S(1)}, s32[192]{0:T(256)S(1)}, u32[]{:S(2)}, u32[]{:S(2)}) collective-permute-start(s32[192]{0:T(256)S(1)} %collective-permute-done.10), channel_id=1, source_target_pairs={{0,1},{1,2},{2,3},{3,4},{4,5},{5,6},{6,7},{7,8},{8,9},{9,10},{10,1... | collective-permute-start | bytes 2312 | tf_op jit(solution)/shard_map/ppermute | solution.py:15
  128.8 5.8 %collective-permute-start.12 = (s32[192]{0:T(256)S(1)}, s32[192]{0:T(256)S(1)}, u32[]{:S(2)}, u32[]{:S(2)}) collective-permute-start(s32[192]{0:T(256)S(1)} %collective-permute-done.11), channel_id=1, source_target_pairs={{0,1},{1,2},{2,3},{3,4},{4,5},{5,6},{6,7},{7,8},{8,9},{9,10},{10,1... | collective-permute-start | bytes 2312 | tf_op jit(solution)/shard_map/ppermute | solution.py:15
  134.6 6.6 %collective-permute-start.13 = (s32[192]{0:T(256)S(1)}, s32[192]{0:T(256)S(1)}, u32[]{:S(2)}, u32[]{:S(2)}) collective-permute-start(s32[192]{0:T(256)S(1)} %collective-permute-done.12), channel_id=1, source_target_pairs={{0,1},{1,2},{2,3},{3,4},{4,5},{5,6},{6,7},{7,8},{8,9},{9,10},{10,1... | collective-permute-start | bytes 2312 | tf_op jit(solution)/shard_map/ppermute | solution.py:15
  305.3 7.3 %copy-start = (bf16[1,192,8192]{2,1,0:T(8,128)(2,1)S(1)}, bf16[1,192,8192]{2,1,0:T(8,128)(2,1)}, u32[]{:S(2)}) copy-start(bf16[1,192,8192]{2,1,0:T(8,128)(2,1)} %param.7) | copy-start | bytes 9437188
  316.1 67.3 %collective-permute-start.14 = (bf16[1,192,8192]{2,1,0:T(8,128)(2,1)S(1)}, bf16[1,192,8192]{2,1,0:T(8,128)(2,1)S(1)}, u32[]{:S(2)}, u32[]{:S(2)}) collective-permute-start(bf16[1,192,8192]{2,1,0:T(8,128)(2,1)S(1)} %add_convert_fusion), channel_id=1, source_target_pairs={{0,16},{16,0},{1,17},{17,1},{2,18},{18,2},{3,19},{19,3},{4,20},{20... | collective-permute-start | bytes 9437192 | tf_op jit(solution)/shard_map/ppermute | solution.py:20
where the time goes:
time: 390 us; the launch traced here: 385 us
  waiting for transfers between devices  170 us (44%)
  matrix products  113 us (29%)
  local copies, waits for them, and re-layouts  67.3 us (17%)
  starting transfers between devices  27.6 us (7%)
  other arithmetic  6.51 us (2%)
    ppermute x14, waiting for transfers between devices, shifted(): return lax.ppermute(value, axis, pairs)  104 us
    ppermute x1, waiting for transfers between devices, from_behind(): lax.ppermute(value, axis, [(i, (i + by) % size) for i in range(size)])  66.7 us
    sub x8, matrix products, one_group(): expo = jnp.exp(scores - top_score)  63.6 us
    dot_general x8, matrix products, one_group(): jnp.einsum('rtl,ld->trd', probs, value_group, preferred_element_type=jnp....  49.3 us
    ppermute x14, starting transfers between devices, shifted(): return lax.ppermute(value, axis, pairs)  26.9 us
    ppermute x7, local copies, waits for them, and re-layouts, shifted(): return lax.ppermute(value, axis, pairs)  13.1 us
    concatenate x1, local copies, waits for them, and re-layouts, local(): window_pair = jnp.concatenate(pair_list, axis=0)  11.8 us
    unnamed x16, local copies, waits for them, and re-layouts  11.3 us
  transfers between devices with their start and end apart: 15, of which 13 were waited for; matrix products, arithmetic and copies ran while one was open for 4% of the time, Pallas kernels for 0%

commit v1 on v0

v1 whole, which is shorter than its diff:
```python
import functools
import math

import jax
import jax.numpy as jnp
from jax import lax
from jax.experimental import pallas as pl
from jax.experimental.pallas import tpu as pltpu
from jax.sharding import PartitionSpec as P

HQ = 64
KVH = 8
HD = 128
WINDOW = 8
REPEAT = HQ // KVH
PAIR = 2 * HD
SEG_ROWS = 16
PENALTY = float(2**20)
LOG2_SCALE = HD**-0.5 * math.log2(math.e)
CHUNKS = (1, 2, 2, 3)
SLOTS = (
    (7, 3, 5, 1, 4, 6, 2, 0),
    (7, 3, 5, 1, 2, 4, 0, 6),
    (7, 3, 1, 5, 4, 2, 6, 0),
    (7, 3, 1, 5, 2, 0, 4, 6),
)


def swap(value, axis, pairs):
    return lax.ppermute(value, axis, pairs + [(b, a) for a, b in pairs])


def exchange(value, axis, bit):
    return lax.ppermute(value, axis, [(i, i ^ bit) for i in range(lax.axis_size(axis))])


def from_groups_behind(value, groups):
    size = lax.axis_size("ctx")
    count = size // 4
    parity = (lax.axis_index("ctx") // 4 // groups) % 2
    halves = []
    for odd in (0, 1):
        pairs = [
            (4 * g + r, 4 * (g + groups) + r)
            for g in range(count - groups)
            if (g // groups) % 2 == odd
            for r in range(4)
        ]
        halves.append(swap(value, "ctx", pairs) if pairs else None)
    if halves[1] is None:
        return jnp.where(parity == 1, halves[0], jnp.zeros_like(value))
    return jnp.where(parity == 1, halves[0], halves[1])


def gather_window(block):
    index = lax.axis_index("ctx")
    in_y, in_core = (index // 2) % 2, index % 2
    behind_two = from_groups_behind(block, 2)
    behind = from_groups_behind(block, 1)
    y_behind = exchange(behind, "ctx", 2)
    y_other = exchange(jnp.where(in_y == 0, block, behind_two), "ctx", 2)
    core_four = exchange(
        jnp.concatenate(
            [behind, y_behind, y_other, jnp.where(in_core == 0, block, behind_two)]
        ),
        "ctx",
        1,
    )
    return (block, behind, y_behind, y_other, core_four)


def attend_kernel(first, tokens, meta, *refs):
    window = tokens * WINDOW
    if first:
        blocks, (query, stream, out, seg_out) = refs[:8], refs[8:12]
        keys, values, bias, extra = refs[12:]
        for n, block in enumerate(blocks):
            slot = meta[n]
            row = block[tokens : tokens + 1, :].astype(jnp.float32)
            seg_out[pl.ds(slot, 1), :] = jnp.where(slot + meta[8] >= WINDOW - 1, row, -1.0)
        segs = seg_out[...]
    else:
        seg_in, blocks, (query, stream, out) = refs[0], refs[1:9], refs[9:12]
        keys, values, bias, extra = refs[12:]
        segs = seg_in[...]
    own_row = segs[WINDOW - 1 :, :tokens]
    seg_zero = segs[WINDOW - 1 :, 0:1]
    own_column = segs.T[:tokens, WINDOW - 1 :]
    before = jnp.sum(jnp.where(segs[: WINDOW - 1, :tokens] != seg_zero, 1.0, 0.0))
    lane = lax.broadcasted_iota(jnp.int32, (tokens, HD), 1)
    extra[...] = jnp.where(
        lane == 0,
        jnp.where(own_column == seg_zero, 0.0, -PENALTY),
        jnp.where(lane == 1, -PENALTY, 0.0),
    ).astype(jnp.bfloat16)
    row_id = lax.broadcasted_iota(jnp.int32, (tokens, tokens), 0)
    column_id = lax.broadcasted_iota(jnp.int32, (tokens, tokens), 1)
    tail = bias.shape[1]
    bias[:, : tail - tokens] = jnp.zeros((tokens, tail - tokens), jnp.float32)
    bias[:, tail - tokens :] = jnp.where(
        (own_column == own_row) & (column_id <= row_id), 0.0, -PENALTY
    )
    for n, block in enumerate(blocks):
        rows = pl.ds(pl.multiple_of(meta[n] * tokens, tokens), tokens)
        keys[rows, :HD] = block[:tokens, :HD]
        values[rows, :HD] = block[:tokens, HD:]
    key_row = lax.broadcasted_iota(jnp.int32, (window, HD), 0)
    key_lane = lax.broadcasted_iota(jnp.int32, (window, HD), 1)
    keys[:, HD:] = jnp.where(
        ((key_lane == 0) & (key_row < window - tokens))
        | ((key_lane == 1) & (key_row.astype(jnp.float32) < before)),
        1.0,
        0.0,
    ).astype(jnp.bfloat16)
    values[:, HD:] = jnp.ones((window, HD), jnp.bfloat16)

    def columns(head):
        return slice(head * HD, (head + 1) * HD)

    def score(head):
        marks = extra[...]
        rows = jnp.concatenate(
            [
                jnp.concatenate([query[:, columns(h)], marks], axis=1)
                for h in (head, head + 1)
            ],
            axis=0,
        )
        scores = lax.dot_general(
            rows, keys[...], (((1,), (1,)), ((), ())), preferred_element_type=jnp.float32
        )
        own = scores[:, window - tail :] + jnp.concatenate([bias[...]] * 2, axis=0)
        return jnp.concatenate([scores[:, : window - tail], own], axis=1)

    def finish(head, scores):
        top = jnp.max(scores, axis=1, keepdims=True)
        weights = jnp.exp2((scores - top) * LOG2_SCALE).astype(jnp.bfloat16)
        sums = jnp.dot(weights, values[...], preferred_element_type=jnp.float32)
        attended = sums[:, :HD] / sums[:, HD:]
        for n, h in enumerate((head, head + 1)):
            out[:, columns(h)] = (
                attended[n * tokens : (n + 1) * tokens]
                + stream[:, columns(h)].astype(jnp.float32)
            ).astype(jnp.bfloat16)

    scores = score(0)
    for head in range(0, REPEAT, 2):
        later = score(head + 2) if head + 2 < REPEAT else None
        finish(head, scores)
        scores = later


def attend(meta, segs, blocks, part, queries, stream, head):
    tokens = queries.shape[0]
    first = segs is None
    rows = blocks[0].shape[0]
    width = REPEAT * HD
    own = [pl.BlockSpec((rows, PAIR), lambda i, m: (0, part)) for _ in range(4)]
    mate = [pl.BlockSpec((rows, PAIR), lambda i, m, n=n: (n, part)) for n in range(4)]
    wide = pl.BlockSpec((tokens, width), lambda i, m: (0, head))
    seg_spec = pl.BlockSpec((WINDOW, PAIR), lambda i, m: (0, 0))
    out_spec = pl.BlockSpec((tokens, width), lambda i, m: (0, 0))
    out_shape = jax.ShapeDtypeStruct((tokens, width), jnp.bfloat16)
    seg_shape = jax.ShapeDtypeStruct((WINDOW, PAIR), jnp.float32)
    window = tokens * WINDOW
    return pl.pallas_call(
        functools.partial(attend_kernel, first, tokens),
        grid_spec=pltpu.PrefetchScalarGridSpec(
            num_scalar_prefetch=1,
            grid=(1,),
            in_specs=([] if first else [seg_spec]) + own + mate + [wide, wide],
            out_specs=(out_spec, seg_spec) if first else out_spec,
            scratch_shapes=[
                pltpu.VMEM((window, PAIR), jnp.bfloat16),
                pltpu.VMEM((window, PAIR), jnp.bfloat16),
                pltpu.VMEM((tokens, PAIR), jnp.float32),
                pltpu.VMEM((tokens, HD), jnp.bfloat16),
            ],
        ),
        out_shape=(out_shape, seg_shape) if first else out_shape,
        compiler_params=pltpu.CompilerParams(vmem_limit_bytes=32 * 2**20),
        cost_estimate=pl.CostEstimate(
            flops=4 * tokens * REPEAT * window * PAIR,
            bytes_accessed=3 * tokens * width * 2 + window * PAIR * 2,
            transcendentals=tokens * REPEAT * window,
        ),
        name="attend",
    )(meta, *([] if first else [segs]), *blocks[:4], *([blocks[4]] * 4), queries, stream)


def local(stream, queries, keys, values, segments):
    stream, queries, keys, values, segments = stream[0], queries[0], keys[0], values[0], segments[0]
    tokens = queries.shape[0]
    index = lax.axis_index("ctx").astype(jnp.int32)
    meta = jnp.concatenate([jnp.asarray(SLOTS, jnp.int32)[index % 4], index[None]])
    pieces, segs, head = [], None, 0
    for size in CHUNKS:
        block = jnp.concatenate(
            [
                part[:, h * HD : (h + 1) * HD]
                for h in range(head, head + size)
                for part in (keys, values)
            ],
            axis=1,
        )
        if head == 0:
            seg_tile = jnp.pad(
                segments.astype(jnp.bfloat16)[None], ((0, SEG_ROWS - 1), (0, PAIR - tokens))
            )
            block = jnp.concatenate([block, seg_tile], axis=0)
        blocks = gather_window(block)
        for part in range(size):
            if segs is None:
                piece, segs = attend(meta, None, blocks, part, queries, stream, head)
            else:
                piece = attend(meta, segs, blocks, part, queries, stream, head)
            pieces.append(exchange(piece, "section", 1))
            head += 1
    return jnp.concatenate(pieces, axis=1)[None]


def solution(mesh):
    in_specs = (
        P("section", "ctx", None),
        P("section", "ctx", None),
        P("section", "ctx", None),
        P("section", "ctx", None),
        P("section", "ctx"),
    )
    out_specs = P("section", "ctx", None)
    return jax.shard_map(local, mesh=mesh, in_specs=in_specs, out_specs=out_specs, check_vma=False)
```

time: 390 us -> 153 us (0.39); the launches traced: 385 us -> 153 us
  matrix products: 113 us -> 0 us
  waiting for transfers between devices: 170 us -> 68.4 us
  local copies, waits for them, and re-layouts: 67.3 us -> 7.75 us
  Pallas kernels: 0 us -> 32.4 us
  starting transfers between devices: 27.6 us -> 42.1 us
  other arithmetic: 6.51 us -> 1.45 us
    ppermute x15 -> x32, waiting for transfers between devices: 170 us -> 68.4 us  [the longest x20 51.6 us: exchange(): lax.ppermute(value, axis, [(i, i ^ bit) for i in range(lax.axis_size(axis...]
    sub x8 -> x0, matrix products: 63.6 us -> none  [one_group(): expo = jnp.exp(scores - top_score)]
    dot_general x8 -> x0, matrix products: 49.3 us -> none  [one_group(): jnp.einsum('rtl,ld->trd', probs, value_group, preferred_element_type=jnp....]
    pallas_call x0 -> x8, Pallas kernels: none -> 32.4 us  [attend(): pl.pallas_call(functools.partial(attend_kernel, first, tokens), grid_spec...]
    ppermute x15 -> x32, starting transfers between devices: 27.6 us -> 42.1 us  [the longest x12 23.9 us: swap(): return lax.ppermute(value, axis, pairs + [(b, a) for a, b in pairs])]
    ppermute x7 -> x0, local copies, waits for them, and re-layouts: 13.1 us -> none  [shifted(): return lax.ppermute(value, axis, pairs)]
    concatenate x3 -> x2, local copies, waits for them, and re-layouts: 12.3 us -> 0.99 us  [the longest x1 0.96 us: local(): jnp.concatenate([part[:, h * HD:(h + 1) * HD] for h in range(head, head +...]
    transpose x1 -> x0, local copies, waits for them, and re-layouts: 9.08 us -> none  [attend_window(): return jnp.moveaxis(group_out, 0, 1).reshape(tok_count, HQ * HD)]
  transfers between devices with their start and end apart: 15 -> 32, of which waited for: 13 -> 15; matrix products, arithmetic and copies ran while one was open for 4% -> 1% of each run, Pallas kernels for 0% -> 21%
where the time goes in v1:
time: 153 us
  waiting for transfers between devices  68.4 us (45%)
  starting transfers between devices  42.1 us (28%)
  Pallas kernels  32.4 us (21%)
  local copies, waits for them, and re-layouts  7.75 us (5%)
    ppermute x20, waiting for transfers between devices, exchange(): lax.ppermute(value, axis, [(i, i ^ bit) for i in range(lax.axis_size(axis...  51.6 us
    pallas_call x8, Pallas kernels, attend(): pl.pallas_call(functools.partial(attend_kernel, first, tokens), grid_spec...  32.4 us
    ppermute x12, starting transfers between devices, swap(): return lax.ppermute(value, axis, pairs + [(b, a) for a, b in pairs])  23.9 us
    ppermute x20, starting transfers between devices, exchange(): lax.ppermute(value, axis, [(i, i ^ bit) for i in range(lax.axis_size(axis...  18.2 us
    ppermute x12, waiting for transfers between devices, swap(): return lax.ppermute(value, axis, pairs + [(b, a) for a, b in pairs])  16.8 us
    unnamed x18, local copies, waits for them, and re-layouts  6.07 us
  transfers between devices with their start and end apart: 32, of which 15 were waited for; matrix products, arithmetic and copies ran while one was open for 1% of the time, Pallas kernels for 21%

profile of v1, /device:TPU:18, one launch (start us, length us, event | category | flops | bytes accessed | tf_op | source)
XLA Modules:
  0.0 152.6 jit_solution(14625384569099553025)
XLA Ops:
  6.3 4.6 %collective-permute-start.1 = (bf16[208,256]{1,0:T(8,128)(2,1)S(1)}, bf16[208,256]{1,0:T(8,128)(2,1)S(1)}, u32[]{:S(2)}, u32[]{:S(2)}) collective-permute-start(bf16[208,256]{1,0:T(8,128)(2,1)S(1)} %fusion.1.refs_0_), channel_id=1, source_target_pairs={{4,8},{5,9},{6,10},{7,11},{8,4},{9,5},{10,6},{11,7},{20,24},{21,25... | collective-permute-start | bytes 319496 | tf_op jit(solution)/shard_map/ppermute | solution.py:30
  12.5 3.9 %collective-permute-start.8 = (bf16[192,512]{1,0:T(8,128)(2,1)S(1)}, bf16[192,512]{1,0:T(8,128)(2,1)S(1)}, u32[]{:S(2)}, u32[]{:S(2)}) collective-permute-start(bf16[192,512]{1,0:T(8,128)(2,1)S(1)} %pad_maximum_fusion.4.refs_1_), channel_id=1, source_target_pairs={{4,8},{5,9},{6,10},{7,11},{8,4},{9,5},{10,6},{11,7},{20,24},{21,25... | collective-permute-start | bytes 589832 | tf_op jit(solution)/shard_map/ppermute | solution.py:30
  17.4 3.1 %collective-permute-done.1 = bf16[208,256]{1,0:T(8,128)(2,1)S(1)} collective-permute-done((bf16[208,256]{1,0:T(8,128)(2,1)S(1)}, bf16[208,256]{1,0:T(8,128)(2,1)S(1)}, u32[]{:S(2)}, u32[]{:S(2)}) %collective-permute-start.1) | collective-permute-done | bytes 106528 | tf_op jit(solution)/shard_map/ppermute | solution.py:30
  20.5 2.0 %collective-permute-start.18 = (bf16[192,512]{1,0:T(8,128)(2,1)S(1)}, bf16[192,512]{1,0:T(8,128)(2,1)S(1)}, u32[]{:S(2)}, u32[]{:S(2)}) collective-permute-start(bf16[192,512]{1,0:T(8,128)(2,1)S(1)} %pad_maximum_fusion.5.refs_1_), channel_id=1, source_target_pairs={{0,8},{1,9},{2,10},{3,11},{4,12},{5,13},{6,14},{7,15},{8,0},{9,1},... | collective-permute-start | bytes 589832 | tf_op jit(solution)/shard_map/ppermute | solution.py:30
  22.5 3.4 %collective-permute-start.16 = (bf16[192,512]{1,0:T(8,128)(2,1)S(1)}, bf16[192,512]{1,0:T(8,128)(2,1)S(1)}, u32[]{:S(2)}, u32[]{:S(2)}) collective-permute-start(bf16[192,512]{1,0:T(8,128)(2,1)S(1)} %pad_maximum_fusion.5.refs_1_), channel_id=1, source_target_pairs={{4,8},{5,9},{6,10},{7,11},{8,4},{9,5},{10,6},{11,7},{20,24},{21,25... | collective-permute-start | bytes 589832 | tf_op jit(solution)/shard_map/ppermute | solution.py:30
  26.9 8.5 %collective-permute-done.18 = bf16[192,512]{1,0:T(8,128)(2,1)S(1)} collective-permute-done((bf16[192,512]{1,0:T(8,128)(2,1)S(1)}, bf16[192,512]{1,0:T(8,128)(2,1)S(1)}, u32[]{:S(2)}, u32[]{:S(2)}) %collective-permute-start.18) | collective-permute-done | bytes 196640 | tf_op jit(solution)/shard_map/ppermute | solution.py:30
  35.4 3.4 %collective-permute-start.26 = (bf16[192,768]{1,0:T(8,128)(2,1)S(1)}, bf16[192,768]{1,0:T(8,128)(2,1)S(1)}, u32[]{:S(2)}, u32[]{:S(2)}) collective-permute-start(bf16[192,768]{1,0:T(8,128)(2,1)S(1)} %get-tuple-element.11.refs_1_), channel_id=1, source_target_pairs={{0,8},{1,9},{2,10},{3,11},{4,12},{5,13},{6,14},{7,15},{8,0},{9,1},... | collective-permute-start | bytes 884744 | tf_op jit(solution)/shard_map/ppermute | solution.py:30
  38.9 3.7 %collective-permute-start.24 = (bf16[192,768]{1,0:T(8,128)(2,1)S(1)}, bf16[192,768]{1,0:T(8,128)(2,1)S(1)}, u32[]{:S(2)}, u32[]{:S(2)}) collective-permute-start(bf16[192,768]{1,0:T(8,128)(2,1)S(1)} %get-tuple-element.11.refs_1_), channel_id=1, source_target_pairs={{4,8},{5,9},{6,10},{7,11},{8,4},{9,5},{10,6},{11,7},{20,24},{21,25... | collective-permute-start | bytes 884744 | tf_op jit(solution)/shard_map/ppermute | solution.py:30
  42.7 5.2 %collective-permute-done.16 = bf16[192,512]{1,0:T(8,128)(2,1)S(1)} collective-permute-done((bf16[192,512]{1,0:T(8,128)(2,1)S(1)}, bf16[192,512]{1,0:T(8,128)(2,1)S(1)}, u32[]{:S(2)}, u32[]{:S(2)}) %collective-permute-start.16) | collective-permute-done | bytes 196640 | tf_op jit(solution)/shard_map/ppermute | solution.py:30
  50.0 3.8 %collective-permute-done.4.refs_3_ = bf16[208,256]{1,0:T(8,128)(2,1)S(1)} collective-permute-done((bf16[208,256]{1,0:T(8,128)(2,1)S(1)}, bf16[208,256]{1,0:T(8,128)(2,1)S(1)}, u32[]{:S(2)}, u32[]{:S(2)}) %collective-permute-start.4) | collective-permute-done | bytes 106528 | tf_op jit(solution)/shard_map/ppermute | solution.py:34
  57.3 4.3 %collective-permute-done.11.refs_4_ = bf16[192,512]{1,0:T(8,128)(2,1)S(1)} collective-permute-done((bf16[192,512]{1,0:T(8,128)(2,1)S(1)}, bf16[192,512]{1,0:T(8,128)(2,1)S(1)}, u32[]{:S(2)}, u32[]{:S(2)}) %collective-permute-start.11) | collective-permute-done | bytes 196640 | tf_op jit(solution)/shard_map/ppermute | solution.py:34
  63.1 2.7 %collective-permute-done.9.refs_3_ = bf16[192,512]{1,0:T(8,128)(2,1)S(1)} collective-permute-done((bf16[192,512]{1,0:T(8,128)(2,1)S(1)}, bf16[192,512]{1,0:T(8,128)(2,1)S(1)}, u32[]{:S(2)}, u32[]{:S(2)}) %collective-permute-start.9) | collective-permute-done | bytes 196640 | tf_op jit(solution)/shard_map/ppermute | solution.py:34
  68.0 1.6 %collective-permute-start.25 = (bf16[192,768]{1,0:T(8,128)(2,1)S(1)}, bf16[192,768]{1,0:T(8,128)(2,1)S(1)}, u32[]{:S(2)}, u32[]{:S(2)}) collective-permute-start(bf16[192,768]{1,0:T(8,128)(2,1)S(1)} %broadcast_select_fusion.3.refs_2_), channel_id=1, source_target_pairs={{0,2},{1,3},{2,0},{3,1},{4,6},{5,7},{6,4},{7,5},{8,10},{9,11},{10,... | collective-permute-start | bytes 884744 | tf_op jit(solution)/shard_map/ppermute | solution.py:34
  69.6 4.0 %attend.8 = (bf16[192,1024]{1,0:T(8,128)(2,1)S(1)}, f32[8,256]{1,0:T(8,128)S(1)}) custom-call(s32[9]{0:T(128)S(1)} %pad_add_fusion.meta, bf16[208,256]{1,0:T(8,128)(2,1)S(1)} %fusion.1.refs_0_, bf16[208,256]{1,0:T(8,128)(2,1)S(1)} %broadcast_select_fusion.15.refs_1_, bf16[208,256]{1,0:T(8,128)(2,1)S(1)} %collective-permute-done.2.refs_2_, ...), custom_call_target="tpu_custom_call" | custom-call | flops 2415919104 | bytes 1966080 | tf_op jit(solution)/shard_map/attend/pallas_call | solution.py:166
  74.4 6.2 %collective-permute-done.27.refs_4_ = bf16[192,768]{1,0:T(8,128)(2,1)S(1)} collective-permute-done((bf16[192,768]{1,0:T(8,128)(2,1)S(1)}, bf16[192,768]{1,0:T(8,128)(2,1)S(1)}, u32[]{:S(2)}, u32[]{:S(2)}) %collective-permute-start.27) | collective-permute-done | bytes 294944 | tf_op jit(solution)/shard_map/ppermute | solution.py:34
  80.6 3.9 %collective-permute-done.25.refs_3_ = bf16[192,768]{1,0:T(8,128)(2,1)S(1)} collective-permute-done((bf16[192,768]{1,0:T(8,128)(2,1)S(1)}, bf16[192,768]{1,0:T(8,128)(2,1)S(1)}, u32[]{:S(2)}, u32[]{:S(2)}) %collective-permute-start.25) | collective-permute-done | bytes 294944 | tf_op jit(solution)/shard_map/ppermute | solution.py:34
  85.0 4.0 %attend.9 = bf16[192,1024]{1,0:T(8,128)(2,1)S(1)} custom-call(s32[9]{0:T(128)S(1)} %pad_add_fusion.meta, f32[8,256]{1,0:T(8,128)S(1)} %get-tuple-element.8.refs_0_, bf16[192,512]{1,0:T(8,128)(2,1)S(1)} %pad_maximum_fusion.4.refs_1_, bf16[192,512]{1,0:T(8,128)(2,1)S(1)} %broadcast_select_fusion.11.refs_2_, ...), custom_call_target="tpu_custom_call" | custom-call | flops 2415919104 | bytes 1966080 | tf_op jit(solution)/shard_map/attend/pallas_call | solution.py:166
  89.6 4.0 %attend.10 = bf16[192,1024]{1,0:T(8,128)(2,1)S(1)} custom-call(s32[9]{0:T(128)S(1)} %pad_add_fusion.meta, f32[8,256]{1,0:T(8,128)S(1)} %get-tuple-element.8.refs_0_, bf16[192,512]{1,0:T(8,128)(2,1)S(1)} %pad_maximum_fusion.4.refs_1_, bf16[192,512]{1,0:T(8,128)(2,1)S(1)} %broadcast_select_fusion.11.refs_2_, ...), custom_call_target="tpu_custom_call" | custom-call | flops 2415919104 | bytes 1966080 | tf_op jit(solution)/shard_map/attend/pallas_call | solution.py:166
  93.6 1.6 %collective-permute-start.14 = (bf16[192,1024]{1,0:T(8,128)(2,1)S(1)}, bf16[192,1024]{1,0:T(8,128)(2,1)S(1)}, u32[]{:S(2)}, u32[]{:S(2)}) collective-permute-start(bf16[192,1024]{1,0:T(8,128)(2,1)S(1)} %attend.10), channel_id=1, source_target_pairs={{0,16},{16,0},{1,17},{17,1},{2,18},{18,2},{3,19},{19,3},{4,20},{20... | collective-permute-start | bytes 1179656 | tf_op jit(solution)/shard_map/ppermute | solution.py:34
  95.2 4.2 %attend.11 = bf16[192,1024]{1,0:T(8,128)(2,1)S(1)} custom-call(s32[9]{0:T(128)S(1)} %pad_add_fusion.meta, f32[8,256]{1,0:T(8,128)S(1)} %get-tuple-element.8.refs_0_, bf16[192,512]{1,0:T(8,128)(2,1)S(1)} %pad_maximum_fusion.5.refs_1_, bf16[192,512]{1,0:T(8,128)(2,1)S(1)} %broadcast_select_fusion.10.refs_2_, ...), custom_call_target="tpu_custom_call" | custom-call | flops 2415919104 | bytes 1966080 | tf_op jit(solution)/shard_map/attend/pallas_call | solution.py:166
  100.0 4.0 %attend.12 = bf16[192,1024]{1,0:T(8,128)(2,1)S(1)} custom-call(s32[9]{0:T(128)S(1)} %pad_add_fusion.meta, f32[8,256]{1,0:T(8,128)S(1)} %get-tuple-element.8.refs_0_, bf16[192,512]{1,0:T(8,128)(2,1)S(1)} %pad_maximum_fusion.5.refs_1_, bf16[192,512]{1,0:T(8,128)(2,1)S(1)} %broadcast_select_fusion.10.refs_2_, ...), custom_call_target="tpu_custom_call" | custom-call | flops 2415919104 | bytes 1966080 | tf_op jit(solution)/shard_map/attend/pallas_call | solution.py:166
  104.0 1.5 %collective-permute-start.22 = (bf16[192,1024]{1,0:T(8,128)(2,1)S(1)}, bf16[192,1024]{1,0:T(8,128)(2,1)S(1)}, u32[]{:S(2)}, u32[]{:S(2)}) collective-permute-start(bf16[192,1024]{1,0:T(8,128)(2,1)S(1)} %attend.12), channel_id=1, source_target_pairs={{0,16},{16,0},{1,17},{17,1},{2,18},{18,2},{3,19},{19,3},{4,20},{20... | collective-permute-start | bytes 1179656 | tf_op jit(solution)/shard_map/ppermute | solution.py:34
  105.5 3.9 %collective-permute-done.14 = bf16[192,1024]{1,0:T(8,128)(2,1)S(1)} collective-permute-done((bf16[192,1024]{1,0:T(8,128)(2,1)S(1)}, bf16[192,1024]{1,0:T(8,128)(2,1)S(1)}, u32[]{:S(2)}, u32[]{:S(2)}) %collective-permute-start.14) | collective-permute-done | bytes 393248 | tf_op jit(solution)/shard_map/ppermute | solution.py:34
  109.5 4.0 %attend.13 = bf16[192,1024]{1,0:T(8,128)(2,1)S(1)} custom-call(s32[9]{0:T(128)S(1)} %pad_add_fusion.meta, f32[8,256]{1,0:T(8,128)S(1)} %get-tuple-element.8.refs_0_, bf16[192,768]{1,0:T(8,128)(2,1)S(1)} %get-tuple-element.11.refs_1_, bf16[192,768]{1,0:T(8,128)(2,1)S(1)} %broadcast_select_fusion.3.refs_2_, ...), custom_call_target="tpu_custom_call" | custom-call | flops 2415919104 | bytes 1966080 | tf_op jit(solution)/shard_map/attend/pallas_call | solution.py:166
  114.1 4.2 %attend.14 = bf16[192,1024]{1,0:T(8,128)(2,1)S(1)} custom-call(s32[9]{0:T(128)S(1)} %pad_add_fusion.meta, f32[8,256]{1,0:T(8,128)S(1)} %get-tuple-element.8.refs_0_, bf16[192,768]{1,0:T(8,128)(2,1)S(1)} %get-tuple-element.11.refs_1_, bf16[192,768]{1,0:T(8,128)(2,1)S(1)} %broadcast_select_fusion.3.refs_2_, ...), custom_call_target="tpu_custom_call" | custom-call | flops 2415919104 | bytes 1966080 | tf_op jit(solution)/shard_map/attend/pallas_call | solution.py:166
  118.3 1.5 %collective-permute-start.30 = (bf16[192,1024]{1,0:T(8,128)(2,1)S(1)}, bf16[192,1024]{1,0:T(8,128)(2,1)S(1)}, u32[]{:S(2)}, u32[]{:S(2)}) collective-permute-start(bf16[192,1024]{1,0:T(8,128)(2,1)S(1)} %attend.14), channel_id=1, source_target_pairs={{0,16},{16,0},{1,17},{17,1},{2,18},{18,2},{3,19},{19,3},{4,20},{20... | collective-permute-start | bytes 1179656 | tf_op jit(solution)/shard_map/ppermute | solution.py:34
  119.9 4.0 %attend.15 = bf16[192,1024]{1,0:T(8,128)(2,1)S(1)} custom-call(s32[9]{0:T(128)S(1)} %pad_add_fusion.meta, f32[8,256]{1,0:T(8,128)S(1)} %get-tuple-element.8.refs_0_, bf16[192,768]{1,0:T(8,128)(2,1)S(1)} %get-tuple-element.11.refs_1_, bf16[192,768]{1,0:T(8,128)(2,1)S(1)} %broadcast_select_fusion.3.refs_2_, ...), custom_call_target="tpu_custom_call" | custom-call | flops 2415919104 | bytes 1966080 | tf_op jit(solution)/shard_map/attend/pallas_call | solution.py:166
  124.5 1.8 %collective-permute-done.22 = bf16[192,1024]{1,0:T(8,128)(2,1)S(1)} collective-permute-done((bf16[192,1024]{1,0:T(8,128)(2,1)S(1)}, bf16[192,1024]{1,0:T(8,128)(2,1)S(1)}, u32[]{:S(2)}, u32[]{:S(2)}) %collective-permute-start.22) | collective-permute-done | bytes 393248 | tf_op jit(solution)/shard_map/ppermute | solution.py:34
  126.3 8.4 %collective-permute-done.29 = bf16[192,1024]{1,0:T(8,128)(2,1)S(1)} collective-permute-done((bf16[192,1024]{1,0:T(8,128)(2,1)S(1)}, bf16[192,1024]{1,0:T(8,128)(2,1)S(1)}, u32[]{:S(2)}, u32[]{:S(2)}) %collective-permute-start.29) | collective-permute-done | bytes 393248 | tf_op jit(solution)/shard_map/ppermute | solution.py:34
  134.8 8.4 %collective-permute-done.30 = bf16[192,1024]{1,0:T(8,128)(2,1)S(1)} collective-permute-done((bf16[192,1024]{1,0:T(8,128)(2,1)S(1)}, bf16[192,1024]{1,0:T(8,128)(2,1)S(1)}, u32[]{:S(2)}, u32[]{:S(2)}) %collective-permute-start.30) | collective-permute-done | bytes 393248 | tf_op jit(solution)/shard_map/ppermute | solution.py:34
  143.2 7.6 %collective-permute-done.31 = bf16[192,1024]{1,0:T(8,128)(2,1)S(1)} collective-permute-done((bf16[192,1024]{1,0:T(8,128)(2,1)S(1)}, bf16[192,1024]{1,0:T(8,128)(2,1)S(1)}, u32[]{:S(2)}, u32[]{:S(2)}) %collective-permute-start.31) | collective-permute-done | bytes 393248 | tf_op jit(solution)/shard_map/ppermute | solution.py:34
  150.9 1.7 %copy-done.2 = bf16[192,8192]{1,0:T(8,128)(2,1)} copy-done((bf16[192,8192]{1,0:T(8,128)(2,1)}, bf16[192,8192]{1,0:T(8,128)(2,1)S(1)}, u32[]{:S(2)}) %copy-start.2) | copy-done | bytes 3145752
  (78 shorter events, 23.0 us)
Async XLA Ops:
  5.9 16.6 %collective-permute-start.3 = (bf16[208,256]{1,0:T(8,128)(2,1)S(1)}, bf16[208,256]{1,0:T(8,128)(2,1)S(1)}, u32[]{:S(2)}, u32[]{:S(2)}) collective-permute-start(bf16[208,256]{1,0:T(8,128)(2,1)S(1)} %fusion.1.refs_0_), channel_id=1, source_target_pairs={{0,8},{1,9},{2,10},{3,11},{4,12},{5,13},{6,14},{7,15},{8,0},{9,1},... | collective-permute-start | bytes 319496 | tf_op jit(solution)/shard_map/ppermute | solution.py:30
  6.3 14.2 %collective-permute-start.1 = (bf16[208,256]{1,0:T(8,128)(2,1)S(1)}, bf16[208,256]{1,0:T(8,128)(2,1)S(1)}, u32[]{:S(2)}, u32[]{:S(2)}) collective-permute-start(bf16[208,256]{1,0:T(8,128)(2,1)S(1)} %fusion.1.refs_0_), channel_id=1, source_target_pairs={{4,8},{5,9},{6,10},{7,11},{8,4},{9,5},{10,6},{11,7},{20,24},{21,25... | collective-permute-start | bytes 319496 | tf_op jit(solution)/shard_map/ppermute | solution.py:30
  10.9 9.6 %collective-permute-start = (bf16[208,256]{1,0:T(8,128)(2,1)S(1)}, bf16[208,256]{1,0:T(8,128)(2,1)S(1)}, u32[]{:S(2)}, u32[]{:S(2)}) collective-permute-start(bf16[208,256]{1,0:T(8,128)(2,1)S(1)} %fusion.1.refs_0_), channel_id=1, source_target_pairs={{0,4},{1,5},{2,6},{3,7},{8,12},{9,13},{10,14},{11,15},{4,0},{5,1},... | collective-permute-start | bytes 319496 | tf_op jit(solution)/shard_map/ppermute | solution.py:30
  11.0 15.0 %collective-permute-start.10 = (bf16[192,512]{1,0:T(8,128)(2,1)S(1)}, bf16[192,512]{1,0:T(8,128)(2,1)S(1)}, u32[]{:S(2)}, u32[]{:S(2)}) collective-permute-start(bf16[192,512]{1,0:T(8,128)(2,1)S(1)} %pad_maximum_fusion.4.refs_1_), channel_id=1, source_target_pairs={{0,8},{1,9},{2,10},{3,11},{4,12},{5,13},{6,14},{7,15},{8,0},{9,1},... | collective-permute-start | bytes 589832 | tf_op jit(solution)/shard_map/ppermute | solution.py:30
  12.5 26.3 %collective-permute-start.8 = (bf16[192,512]{1,0:T(8,128)(2,1)S(1)}, bf16[192,512]{1,0:T(8,128)(2,1)S(1)}, u32[]{:S(2)}, u32[]{:S(2)}) collective-permute-start(bf16[192,512]{1,0:T(8,128)(2,1)S(1)} %pad_maximum_fusion.4.refs_1_), channel_id=1, source_target_pairs={{4,8},{5,9},{6,10},{7,11},{8,4},{9,5},{10,6},{11,7},{20,24},{21,25... | collective-permute-start | bytes 589832 | tf_op jit(solution)/shard_map/ppermute | solution.py:30
  20.5 22.1 %collective-permute-start.7 = (bf16[192,512]{1,0:T(8,128)(2,1)S(1)}, bf16[192,512]{1,0:T(8,128)(2,1)S(1)}, u32[]{:S(2)}, u32[]{:S(2)}) collective-permute-start(bf16[192,512]{1,0:T(8,128)(2,1)S(1)} %pad_maximum_fusion.4.refs_1_), channel_id=1, source_target_pairs={{0,4},{1,5},{2,6},{3,7},{8,12},{9,13},{10,14},{11,15},{4,0},{5,1},... | collective-permute-start | bytes 589832 | tf_op jit(solution)/shard_map/ppermute | solution.py:30
  20.5 14.9 %collective-permute-start.18 = (bf16[192,512]{1,0:T(8,128)(2,1)S(1)}, bf16[192,512]{1,0:T(8,128)(2,1)S(1)}, u32[]{:S(2)}, u32[]{:S(2)}) collective-permute-start(bf16[192,512]{1,0:T(8,128)(2,1)S(1)} %pad_maximum_fusion.5.refs_1_), channel_id=1, source_target_pairs={{0,8},{1,9},{2,10},{3,11},{4,12},{5,13},{6,14},{7,15},{8,0},{9,1},... | collective-permute-start | bytes 589832 | tf_op jit(solution)/shard_map/ppermute | solution.py:30
  22.5 25.4 %collective-permute-start.16 = (bf16[192,512]{1,0:T(8,128)(2,1)S(1)}, bf16[192,512]{1,0:T(8,128)(2,1)S(1)}, u32[]{:S(2)}, u32[]{:S(2)}) collective-permute-start(bf16[192,512]{1,0:T(8,128)(2,1)S(1)} %pad_maximum_fusion.5.refs_1_), channel_id=1, source_target_pairs={{4,8},{5,9},{6,10},{7,11},{8,4},{9,5},{10,6},{11,7},{20,24},{21,25... | collective-permute-start | bytes 589832 | tf_op jit(solution)/shard_map/ppermute | solution.py:30
  26.0 23.4 %collective-permute-start.15 = (bf16[192,512]{1,0:T(8,128)(2,1)S(1)}, bf16[192,512]{1,0:T(8,128)(2,1)S(1)}, u32[]{:S(2)}, u32[]{:S(2)}) collective-permute-start(bf16[192,512]{1,0:T(8,128)(2,1)S(1)} %pad_maximum_fusion.5.refs_1_), channel_id=1, source_target_pairs={{0,4},{1,5},{2,6},{3,7},{8,12},{9,13},{10,14},{11,15},{4,0},{5,1},... | collective-permute-start | bytes 589832 | tf_op jit(solution)/shard_map/ppermute | solution.py:30
  35.4 21.7 %collective-permute-start.26 = (bf16[192,768]{1,0:T(8,128)(2,1)S(1)}, bf16[192,768]{1,0:T(8,128)(2,1)S(1)}, u32[]{:S(2)}, u32[]{:S(2)}) collective-permute-start(bf16[192,768]{1,0:T(8,128)(2,1)S(1)} %get-tuple-element.11.refs_1_), channel_id=1, source_target_pairs={{0,8},{1,9},{2,10},{3,11},{4,12},{5,13},{6,14},{7,15},{8,0},{9,1},... | collective-permute-start | bytes 884744 | tf_op jit(solution)/shard_map/ppermute | solution.py:30
  38.9 28.5 %collective-permute-start.24 = (bf16[192,768]{1,0:T(8,128)(2,1)S(1)}, bf16[192,768]{1,0:T(8,128)(2,1)S(1)}, u32[]{:S(2)}, u32[]{:S(2)}) collective-permute-start(bf16[192,768]{1,0:T(8,128)(2,1)S(1)} %get-tuple-element.11.refs_1_), channel_id=1, source_target_pairs={{4,8},{5,9},{6,10},{7,11},{8,4},{9,5},{10,6},{11,7},{20,24},{21,25... | collective-permute-start | bytes 884744 | tf_op jit(solution)/shard_map/ppermute | solution.py:30
  42.6 25.3 %collective-permute-start.23 = (bf16[192,768]{1,0:T(8,128)(2,1)S(1)}, bf16[192,768]{1,0:T(8,128)(2,1)S(1)}, u32[]{:S(2)}, u32[]{:S(2)}) collective-permute-start(bf16[192,768]{1,0:T(8,128)(2,1)S(1)} %get-tuple-element.11.refs_1_), channel_id=1, source_target_pairs={{0,4},{1,5},{2,6},{3,7},{8,12},{9,13},{10,14},{11,15},{4,0},{5,1},... | collective-permute-start | bytes 884744 | tf_op jit(solution)/shard_map/ppermute | solution.py:30
  47.9 5.8 %collective-permute-start.4 = (bf16[208,256]{1,0:T(8,128)(2,1)S(1)}, bf16[208,256]{1,0:T(8,128)(2,1)S(1)}, u32[]{:S(2)}, u32[]{:S(2)}) collective-permute-start(bf16[208,256]{1,0:T(8,128)(2,1)S(1)} %get-tuple-element.28), channel_id=1, source_target_pairs={{0,2},{1,3},{2,0},{3,1},{4,6},{5,7},{6,4},{7,5},{8,10},{9,11},{10,... | collective-permute-start | bytes 319496 | tf_op jit(solution)/shard_map/ppermute | solution.py:34
  49.4 6.1 %collective-permute-start.2 = (bf16[208,256]{1,0:T(8,128)(2,1)S(1)}, bf16[208,256]{1,0:T(8,128)(2,1)S(1)}, u32[]{:S(2)}, u32[]{:S(2)}) collective-permute-start(bf16[208,256]{1,0:T(8,128)(2,1)S(1)} %broadcast_select_fusion.15.refs_1_), channel_id=1, source_target_pairs={{0,2},{1,3},{2,0},{3,1},{4,6},{5,7},{6,4},{7,5},{8,10},{9,11},{10,... | collective-permute-start | bytes 319496 | tf_op jit(solution)/shard_map/ppermute | solution.py:34
  53.8 7.8 %collective-permute-start.11 = (bf16[192,512]{1,0:T(8,128)(2,1)S(1)}, bf16[192,512]{1,0:T(8,128)(2,1)S(1)}, u32[]{:S(2)}, u32[]{:S(2)}) collective-permute-start(bf16[192,512]{1,0:T(8,128)(2,1)S(1)} %get-tuple-element.26), channel_id=1, source_target_pairs={{0,2},{1,3},{2,0},{3,1},{4,6},{5,7},{6,4},{7,5},{8,10},{9,11},{10,... | collective-permute-start | bytes 589832 | tf_op jit(solution)/shard_map/ppermute | solution.py:34
  55.6 10.2 %collective-permute-start.9 = (bf16[192,512]{1,0:T(8,128)(2,1)S(1)}, bf16[192,512]{1,0:T(8,128)(2,1)S(1)}, u32[]{:S(2)}, u32[]{:S(2)}) collective-permute-start(bf16[192,512]{1,0:T(8,128)(2,1)S(1)} %broadcast_select_fusion.11.refs_2_), channel_id=1, source_target_pairs={{0,2},{1,3},{2,0},{3,1},{4,6},{5,7},{6,4},{7,5},{8,10},{9,11},{10,... | collective-permute-start | bytes 589832 | tf_op jit(solution)/shard_map/ppermute | solution.py:34
  57.1 10.9 %collective-permute-start.5 = (bf16[832,256]{1,0:T(8,128)(2,1)S(1)}, bf16[832,256]{1,0:T(8,128)(2,1)S(1)}, u32[]{:S(2)}, u32[]{:S(2)}) collective-permute-start(bf16[832,256]{1,0:T(8,128)(2,1)S(1)} %pad_maximum_fusion.3), channel_id=1, source_target_pairs={{0,1},{1,0},{2,3},{3,2},{4,5},{5,4},{6,7},{7,6},{8,9},{9,8},{10,11... | collective-permute-start | bytes 1277960 | tf_op jit(solution)/shard_map/ppermute | solution.py:34
  61.6 12.1 %collective-permute-start.19 = (bf16[192,512]{1,0:T(8,128)(2,1)S(1)}, bf16[192,512]{1,0:T(8,128)(2,1)S(1)}, u32[]{:S(2)}, u32[]{:S(2)}) collective-permute-start(bf16[192,512]{1,0:T(8,128)(2,1)S(1)} %get-tuple-element.24), channel_id=1, source_target_pairs={{0,2},{1,3},{2,0},{3,1},{4,6},{5,7},{6,4},{7,5},{8,10},{9,11},{10,... | collective-permute-start | bytes 589832 | tf_op jit(solution)/shard_map/ppermute | solution.py:34
  65.8 8.4 %collective-permute-start.17 = (bf16[192,512]{1,0:T(8,128)(2,1)S(1)}, bf16[192,512]{1,0:T(8,128)(2,1)S(1)}, u32[]{:S(2)}, u32[]{:S(2)}) collective-permute-start(bf16[192,512]{1,0:T(8,128)(2,1)S(1)} %broadcast_select_fusion.10.refs_2_), channel_id=1, source_target_pairs={{0,2},{1,3},{2,0},{3,1},{4,6},{5,7},{6,4},{7,5},{8,10},{9,11},{10,... | collective-permute-start | bytes 589832 | tf_op jit(solution)/shard_map/ppermute | solution.py:34
  67.4 13.1 %collective-permute-start.27 = (bf16[192,768]{1,0:T(8,128)(2,1)S(1)}, bf16[192,768]{1,0:T(8,128)(2,1)S(1)}, u32[]{:S(2)}, u32[]{:S(2)}) collective-permute-start(bf16[192,768]{1,0:T(8,128)(2,1)S(1)} %get-tuple-element.10), channel_id=1, source_target_pairs={{0,2},{1,3},{2,0},{3,1},{4,6},{5,7},{6,4},{7,5},{8,10},{9,11},{10,... | collective-permute-start | bytes 884744 | tf_op jit(solution)/shard_map/ppermute | solution.py:34
  68.0 17.0 %collective-permute-start.12 = (bf16[768,512]{1,0:T(8,128)(2,1)S(1)}, bf16[768,512]{1,0:T(8,128)(2,1)S(1)}, u32[]{:S(2)}, u32[]{:S(2)}) collective-permute-start(bf16[768,512]{1,0:T(8,128)(2,1)S(1)} %pad_maximum_fusion.1), channel_id=1, source_target_pairs={{0,1},{1,0},{2,3},{3,2},{4,5},{5,4},{6,7},{7,6},{8,9},{9,8},{10,11... | collective-permute-start | bytes 2359304 | tf_op jit(solution)/shard_map/ppermute | solution.py:34
  68.0 16.5 %collective-permute-start.25 = (bf16[192,768]{1,0:T(8,128)(2,1)S(1)}, bf16[192,768]{1,0:T(8,128)(2,1)S(1)}, u32[]{:S(2)}, u32[]{:S(2)}) collective-permute-start(bf16[192,768]{1,0:T(8,128)(2,1)S(1)} %broadcast_select_fusion.3.refs_2_), channel_id=1, source_target_pairs={{0,2},{1,3},{2,0},{3,1},{4,6},{5,7},{6,4},{7,5},{8,10},{9,11},{10,... | collective-permute-start | bytes 884744 | tf_op jit(solution)/shard_map/ppermute | solution.py:34
  73.7 11.3 %collective-permute-start.6 = (bf16[192,1024]{1,0:T(8,128)(2,1)S(1)}, bf16[192,1024]{1,0:T(8,128)(2,1)S(1)}, u32[]{:S(2)}, u32[]{:S(2)}) collective-permute-start(bf16[192,1024]{1,0:T(8,128)(2,1)S(1)} %get-tuple-element.7), channel_id=1, source_target_pairs={{0,16},{16,0},{1,17},{17,1},{2,18},{18,2},{3,19},{19,3},{4,20},{20... | collective-permute-start | bytes 1179656 | tf_op jit(solution)/shard_map/ppermute | solution.py:34
  74.3 20.9 %collective-permute-start.20 = (bf16[768,512]{1,0:T(8,128)(2,1)S(1)}, bf16[768,512]{1,0:T(8,128)(2,1)S(1)}, u32[]{:S(2)}, u32[]{:S(2)}) collective-permute-start(bf16[768,512]{1,0:T(8,128)(2,1)S(1)} %pad_maximum_fusion.2), channel_id=1, source_target_pairs={{0,1},{1,0},{2,3},{3,2},{4,5},{5,4},{6,7},{7,6},{8,9},{9,8},{10,11... | collective-permute-start | bytes 2359304 | tf_op jit(solution)/shard_map/ppermute | solution.py:34
  84.6 24.9 %collective-permute-start.28 = (bf16[768,768]{1,0:T(8,128)(2,1)S(1)}, bf16[768,768]{1,0:T(8,128)(2,1)S(1)}, u32[]{:S(2)}, u32[]{:S(2)}) collective-permute-start(bf16[768,768]{1,0:T(8,128)(2,1)S(1)} %pad_maximum_fusion), channel_id=1, source_target_pairs={{0,1},{1,0},{2,3},{3,2},{4,5},{5,4},{6,7},{7,6},{8,9},{9,8},{10,11... | collective-permute-start | bytes 3538952 | tf_op jit(solution)/shard_map/ppermute | solution.py:34
  89.0 16.5 %collective-permute-start.13 = (bf16[192,1024]{1,0:T(8,128)(2,1)S(1)}, bf16[192,1024]{1,0:T(8,128)(2,1)S(1)}, u32[]{:S(2)}, u32[]{:S(2)}) collective-permute-start(bf16[192,1024]{1,0:T(8,128)(2,1)S(1)} %attend.9), channel_id=1, source_target_pairs={{0,16},{16,0},{1,17},{17,1},{2,18},{18,2},{3,19},{19,3},{4,20},{20... | collective-permute-start | bytes 1179656 | tf_op jit(solution)/shard_map/ppermute | solution.py:34
  93.6 15.8 %collective-permute-start.14 = (bf16[192,1024]{1,0:T(8,128)(2,1)S(1)}, bf16[192,1024]{1,0:T(8,128)(2,1)S(1)}, u32[]{:S(2)}, u32[]{:S(2)}) collective-permute-start(bf16[192,1024]{1,0:T(8,128)(2,1)S(1)} %attend.10), channel_id=1, source_target_pairs={{0,16},{16,0},{1,17},{17,1},{2,18},{18,2},{3,19},{19,3},{4,20},{20... | collective-permute-start | bytes 1179656 | tf_op jit(solution)/shard_map/ppermute | solution.py:34
  99.3 25.2 %collective-permute-start.21 = (bf16[192,1024]{1,0:T(8,128)(2,1)S(1)}, bf16[192,1024]{1,0:T(8,128)(2,1)S(1)}, u32[]{:S(2)}, u32[]{:S(2)}) collective-permute-start(bf16[192,1024]{1,0:T(8,128)(2,1)S(1)} %attend.11), channel_id=1, source_target_pairs={{0,16},{16,0},{1,17},{17,1},{2,18},{18,2},{3,19},{19,3},{4,20},{20... | collective-permute-start | bytes 1179656 | tf_op jit(solution)/shard_map/ppermute | solution.py:34
  104.0 22.3 %collective-permute-start.22 = (bf16[192,1024]{1,0:T(8,128)(2,1)S(1)}, bf16[192,1024]{1,0:T(8,128)(2,1)S(1)}, u32[]{:S(2)}, u32[]{:S(2)}) collective-permute-start(bf16[192,1024]{1,0:T(8,128)(2,1)S(1)} %attend.12), channel_id=1, source_target_pairs={{0,16},{16,0},{1,17},{17,1},{2,18},{18,2},{3,19},{19,3},{4,20},{20... | collective-permute-start | bytes 1179656 | tf_op jit(solution)/shard_map/ppermute | solution.py:34
  113.5 21.2 %collective-permute-start.29 = (bf16[192,1024]{1,0:T(8,128)(2,1)S(1)}, bf16[192,1024]{1,0:T(8,128)(2,1)S(1)}, u32[]{:S(2)}, u32[]{:S(2)}) collective-permute-start(bf16[192,1024]{1,0:T(8,128)(2,1)S(1)} %attend.13), channel_id=1, source_target_pairs={{0,16},{16,0},{1,17},{17,1},{2,18},{18,2},{3,19},{19,3},{4,20},{20... | collective-permute-start | bytes 1179656 | tf_op jit(solution)/shard_map/ppermute | solution.py:34
  118.3 24.8 %collective-permute-start.30 = (bf16[192,1024]{1,0:T(8,128)(2,1)S(1)}, bf16[192,1024]{1,0:T(8,128)(2,1)S(1)}, u32[]{:S(2)}, u32[]{:S(2)}) collective-permute-start(bf16[192,1024]{1,0:T(8,128)(2,1)S(1)} %attend.14), channel_id=1, source_target_pairs={{0,16},{16,0},{1,17},{17,1},{2,18},{18,2},{3,19},{19,3},{4,20},{20... | collective-permute-start | bytes 1179656 | tf_op jit(solution)/shard_map/ppermute | solution.py:34
  123.9 27.0 %collective-permute-start.31 = (bf16[192,1024]{1,0:T(8,128)(2,1)S(1)}, bf16[192,1024]{1,0:T(8,128)(2,1)S(1)}, u32[]{:S(2)}, u32[]{:S(2)}) collective-permute-start(bf16[192,1024]{1,0:T(8,128)(2,1)S(1)} %attend.15), channel_id=1, source_target_pairs={{0,16},{16,0},{1,17},{17,1},{2,18},{18,2},{3,19},{19,3},{4,20},{20... | collective-permute-start | bytes 1179656 | tf_op jit(solution)/shard_map/ppermute | solution.py:34
  (3 other events, 52.2 us)

commit v2 on v1

v2 whole, which is shorter than its diff:
```python
import functools
import math

import jax
import jax.numpy as jnp
from jax import lax
from jax.experimental import pallas as pl
from jax.experimental.pallas import tpu as pltpu
from jax.sharding import PartitionSpec as P

HQ = 64
KVH = 8
HD = 128
WINDOW = 8
REPEAT = HQ // KVH
PAIR = 2 * HD
WIDTH = REPEAT * HD
SEG_ROWS = 16
PENALTY = float(2**20)
LOG2_SCALE = HD**-0.5 * math.log2(math.e)
LIGHT = pl.CostEstimate(flops=1, bytes_accessed=1, transcendentals=0)
HEAVY = pl.CostEstimate(flops=10**11, bytes_accessed=10**6, transcendentals=0)
SLOTS = (
    (7, 3, 5, 1, 4, 6, 2, 0),
    (7, 3, 5, 1, 2, 4, 0, 6),
    (7, 3, 1, 5, 4, 2, 6, 0),
    (7, 3, 1, 5, 2, 0, 4, 6),
)


def gate(value, *ahead):
    return lax.optimization_barrier((value, ahead))[0]


def exchange(value, axis, bit):
    return lax.ppermute(value, axis, [(i, i ^ bit) for i in range(lax.axis_size(axis))])


def from_groups_behind(value, groups):
    size = lax.axis_size("ctx")
    pairs = [(i, i + 4 * groups) for i in range(size - 4 * groups)]
    if not {a for a, _ in pairs} & {b for _, b in pairs}:
        pairs = pairs + [(b, a) for a, b in pairs]
    return lax.ppermute(value, "ctx", pairs)


def gather_behind(block):
    return from_groups_behind(block, 1), from_groups_behind(block, 2)


def join_kernel(bit, column, *refs):
    *parts, own, two, out = refs
    width = out.shape[1]
    row = 0
    for part in parts:
        start = column if part.shape[1] > width else 0
        out[row : row + part.shape[0], :] = part[:, start : start + width]
        row += part.shape[0]
    first = (lax.axis_index("ctx") // bit) % 2 == 0

    @pl.when(first)
    def _():
        out[row:, :] = own[:, column : column + width]

    @pl.when(jnp.logical_not(first))
    def _():
        out[row:, :] = two[:, column : column + width]


def join(parts, own, two, bit, chunk):
    first, size = chunk
    rows = sum(part.shape[0] for part in parts) + own.shape[0]
    vmem = pl.BlockSpec(memory_space=pltpu.VMEM)
    return pl.pallas_call(
        functools.partial(join_kernel, bit, first * PAIR),
        in_specs=[vmem] * (len(parts) + 2),
        out_specs=vmem,
        out_shape=jax.ShapeDtypeStruct((rows, size * PAIR), jnp.bfloat16),
        cost_estimate=LIGHT,
        compiler_params=pltpu.CompilerParams(vmem_limit_bytes=12 * 2**20),
        name="join",
    )(*parts, own, two)


def over_y(block, behind, chunk):
    one, two = behind
    return exchange(join([one], block, two, 2, chunk), "ctx", 2)


def over_core(block, behind, mates, chunk):
    one, two = behind
    return exchange(join([one, mates], block, two, 1, chunk), "ctx", 1)


def fill_block(out, tokens, chunk, keys, values, seg):
    first, size = chunk
    for n in range(size):
        source = slice((first + n) * HD, (first + n + 1) * HD)
        out[:tokens, n * PAIR : n * PAIR + HD] = keys[:, source]
        out[:tokens, n * PAIR + HD : (n + 1) * PAIR] = values[:, source]
    out[tokens:, :] = jnp.zeros((out.shape[0] - tokens, size * PAIR), jnp.bfloat16)
    row = seg[...].astype(jnp.float32).astype(jnp.bfloat16)
    for n in range(size):
        out[tokens : tokens + 1, n * PAIR : n * PAIR + tokens] = row


def pack_blocks_kernel(tokens, chunks, keys, values, seg, *outs):
    for out, chunk in zip(outs, chunks):
        fill_block(out, tokens, chunk, keys, values, seg)


def pack_blocks(keys, values, segments, chunks):
    tokens = keys.shape[0]
    shapes = [(tokens + SEG_ROWS, size * PAIR) for _, size in chunks]
    one = lambda i: (0, 0)
    return pl.pallas_call(
        functools.partial(pack_blocks_kernel, tokens, chunks),
        grid=(1,),
        in_specs=[pl.BlockSpec(keys.shape, one)] * 2 + [pl.BlockSpec((1, tokens), one)],
        out_specs=[pl.BlockSpec(shape, one) for shape in shapes],
        out_shape=[jax.ShapeDtypeStruct(shape, jnp.bfloat16) for shape in shapes],
        cost_estimate=LIGHT,
        compiler_params=pltpu.CompilerParams(vmem_limit_bytes=56 * 2**20),
        name="pack_blocks",
    )(keys, values, segments)


def fold_places(rows, size):
    per_row = WIDTH // PAIR
    tiles = [(n, r) for n in range(size) for r in range(rows // SEG_ROWS)]
    return [
        (r * SEG_ROWS, n * PAIR, t // per_row * SEG_ROWS, t % per_row * PAIR)
        for t, (n, r) in enumerate(tiles)
    ]


def pack_wide_kernel(parts, chunk, queries, stream, *refs):
    keys, values, seg, out, block, sems = refs if chunk else (None,) * 3 + refs[:1] + (None,) + refs[1:]
    tokens = queries.shape[0]
    copies = [
        pltpu.make_async_copy(
            source.at[:, pl.ds(head * WIDTH, WIDTH)],
            out.at[pl.ds(n * tokens, tokens)],
            sems.at[n],
        )
        for n, (source, head) in enumerate(((queries, stream)[m], head) for m, head in parts)
    ]
    for copy in copies:
        copy.start()
    if chunk:
        fill_block(block, tokens, chunk, keys, values, seg)
        base = len(parts) * tokens
        for row, column, to_row, to_column in fold_places(block.shape[0], chunk[1]):
            out[base + to_row : base + to_row + SEG_ROWS, to_column : to_column + PAIR] = block[
                row : row + SEG_ROWS, column : column + PAIR
            ]
    for copy in copies:
        copy.wait()


def pack_wide(queries, stream, parts, chunk=None, others=()):
    tokens = queries.shape[0]
    rows = len(parts) * tokens
    vmem = pl.BlockSpec(memory_space=pltpu.VMEM)
    scratch = [pltpu.SemaphoreType.DMA((len(parts),))]
    if chunk:
        block = (tokens + SEG_ROWS, chunk[1] * PAIR)
        rows += max(place[2] for place in fold_places(*block[:1], chunk[1])) + SEG_ROWS
        scratch = [pltpu.VMEM(block, jnp.bfloat16)] + scratch
    return pl.pallas_call(
        functools.partial(pack_wide_kernel, parts, chunk),
        in_specs=[pl.BlockSpec(memory_space=pltpu.HBM)] * 2 + [vmem] * len(others),
        out_specs=vmem,
        out_shape=jax.ShapeDtypeStruct((rows, WIDTH), jnp.bfloat16),
        scratch_shapes=scratch,
        cost_estimate=LIGHT,
        compiler_params=pltpu.CompilerParams(vmem_limit_bytes=56 * 2**20),
        name="pack_wide",
    )(queries, stream, *others)


def unfold_kernel(base, size, wide, out):
    for row, column, at_row, at_column in fold_places(out.shape[0], size):
        out[row : row + SEG_ROWS, column : column + PAIR] = wide[
            base + at_row : base + at_row + SEG_ROWS, at_column : at_column + PAIR
        ]


def unfold(wide, base, tokens, chunk):
    vmem = pl.BlockSpec(memory_space=pltpu.VMEM)
    return pl.pallas_call(
        functools.partial(unfold_kernel, base, chunk[1]),
        in_specs=[vmem],
        out_specs=vmem,
        out_shape=jax.ShapeDtypeStruct((tokens + SEG_ROWS, chunk[1] * PAIR), jnp.bfloat16),
        cost_estimate=LIGHT,
        compiler_params=pltpu.CompilerParams(vmem_limit_bytes=8 * 2**20),
        name="unfold",
    )(wide)


def attend_kernel(tokens, column, query_row, stream_row, *refs):
    blocks, (query_in, stream_in, out) = refs[:WINDOW], refs[WINDOW : WINDOW + 3]
    keys, values, bias, extra, segs_ref, query, stream, sems = refs[WINDOW + 3 :]
    window = tokens * WINDOW
    index = lax.axis_index("ctx")
    place = index % 4
    slots = [
        jnp.where(place < 2, jnp.where(place == 0, a, b), jnp.where(place == 2, c, d))
        for a, b, c, d in zip(*SLOTS)
    ]
    copies = [
        pltpu.make_async_copy(
            source.at[pl.ds(row, tokens), pl.ds(column, WIDTH)], target, sems.at[n]
        )
        for n, (source, row, target) in enumerate(
            ((query_in, query_row, query), (stream_in, stream_row, stream))
        )
    ]

    for copy in copies:
        copy.start()
    for slot, block in zip(slots, blocks):
        row = block[tokens : tokens + 1, :].astype(jnp.float32)
        segs_ref[pl.ds(slot, 1), :] = jnp.where(slot + index >= WINDOW - 1, row, -1.0)
    segs = segs_ref[...]
    own_row = segs[WINDOW - 1 :, :tokens]
    seg_zero = segs[WINDOW - 1 :, 0:1]
    own_column = segs.T[:tokens, WINDOW - 1 :]
    before = jnp.sum(jnp.where(segs[: WINDOW - 1, :tokens] != seg_zero, 1.0, 0.0))
    lane = lax.broadcasted_iota(jnp.int32, (tokens, HD), 1)
    extra[...] = jnp.where(
        lane == 0,
        jnp.where(own_column == seg_zero, 0.0, -PENALTY),
        jnp.where(lane == 1, -PENALTY, 0.0),
    ).astype(jnp.bfloat16)
    row_id = lax.broadcasted_iota(jnp.int32, (tokens, tokens), 0)
    column_id = lax.broadcasted_iota(jnp.int32, (tokens, tokens), 1)
    tail = bias.shape[1]
    bias[:, : tail - tokens] = jnp.zeros((tokens, tail - tokens), jnp.float32)
    bias[:, tail - tokens :] = jnp.where(
        (own_column == own_row) & (column_id <= row_id), 0.0, -PENALTY
    )
    key_row = lax.broadcasted_iota(jnp.int32, (window, HD), 0)
    key_lane = lax.broadcasted_iota(jnp.int32, (window, HD), 1)
    keys[:, HD:] = jnp.where(
        ((key_lane == 0) & (key_row < window - tokens))
        | ((key_lane == 1) & (key_row.astype(jnp.float32) < before)),
        1.0,
        0.0,
    ).astype(jnp.bfloat16)
    values[:, HD:] = jnp.ones((window, HD), jnp.bfloat16)

    for copy in copies:
        copy.wait()

    for slot, block in zip(slots, blocks):
        rows = pl.ds(pl.multiple_of(slot * tokens, tokens), tokens)
        keys[rows, :HD] = block[:tokens, :HD]
        values[rows, :HD] = block[:tokens, HD:]

    def columns(head):
        return slice(head * HD, (head + 1) * HD)

    def score(head):
        marks = extra[...]
        rows = jnp.concatenate(
            [jnp.concatenate([query[:, columns(h)], marks], axis=1) for h in (head, head + 1)],
            axis=0,
        )
        scores = lax.dot_general(
            rows, keys[...], (((1,), (1,)), ((), ())), preferred_element_type=jnp.float32
        )
        own = scores[:, window - tail :] + jnp.concatenate([bias[...]] * 2, axis=0)
        return jnp.concatenate([scores[:, : window - tail], own], axis=1)

    def finish(head, scores):
        top = jnp.max(scores, axis=1, keepdims=True)
        weights = jnp.exp2((scores - top) * LOG2_SCALE).astype(jnp.bfloat16)
        sums = jnp.dot(weights, values[...], preferred_element_type=jnp.float32)
        attended = sums[:, :HD] / sums[:, HD:]
        for n, h in enumerate((head, head + 1)):
            out[:, columns(h)] = (
                attended[n * tokens : (n + 1) * tokens]
                + stream[:, columns(h)].astype(jnp.float32)
            ).astype(jnp.bfloat16)

    scores = score(0)
    for head in range(0, REPEAT, 2):
        later = score(head + 2) if head + 2 < REPEAT else None
        finish(head, scores)
        scores = later


def attend(blocks, queries, stream, column, query_row, stream_row, cost):
    rows = blocks[0][0].shape[0]
    tokens = rows - SEG_ROWS
    window = tokens * WINDOW
    places = [(block, part, n) for block, part in blocks for n in range(block.shape[0] // rows)]
    return pl.pallas_call(
        functools.partial(attend_kernel, tokens, column, query_row, stream_row),
        grid=(1,),
        in_specs=[
            pl.BlockSpec((rows, PAIR), lambda i, part=part, n=n: (n, part)) for _, part, n in places
        ]
        + [pl.BlockSpec(memory_space=pl.ANY)] * 2,
        out_specs=pl.BlockSpec((tokens, WIDTH), lambda i: (0, 0)),
        out_shape=jax.ShapeDtypeStruct((tokens, WIDTH), jnp.bfloat16),
        scratch_shapes=[
            pltpu.VMEM((window, PAIR), jnp.bfloat16),
            pltpu.VMEM((window, PAIR), jnp.bfloat16),
            pltpu.VMEM((tokens, PAIR), jnp.float32),
            pltpu.VMEM((tokens, HD), jnp.bfloat16),
            pltpu.VMEM((WINDOW, PAIR), jnp.float32),
            pltpu.VMEM((tokens, WIDTH), jnp.bfloat16),
            pltpu.VMEM((tokens, WIDTH), jnp.bfloat16),
            pltpu.SemaphoreType.DMA((2,)),
        ],
        compiler_params=pltpu.CompilerParams(vmem_limit_bytes=16 * 2**20),
        cost_estimate=cost,
        name="attend",
    )(*[block for block, _, _ in places], queries, stream)


def assemble_kernel(places, *refs):
    *pieces, out, sems = refs
    copies = [
        pltpu.make_async_copy(
            piece, out.at[pl.ds(row, piece.shape[0]), pl.ds(column, piece.shape[1])], sems.at[n]
        )
        for n, (piece, (row, column)) in enumerate(zip(pieces[-len(places) :], places))
    ]
    for copy in copies:
        copy.start()
    for copy in copies:
        copy.wait()


def assemble(out, pieces, shape, cost):
    places = [place for _, place in pieces]
    given = [] if out is None else [out]
    return pl.pallas_call(
        functools.partial(assemble_kernel, places),
        in_specs=[pl.BlockSpec(memory_space=pl.ANY)] * len(given)
        + [pl.BlockSpec(memory_space=pltpu.VMEM)] * len(pieces),
        out_specs=pl.BlockSpec(memory_space=pl.ANY),
        out_shape=jax.ShapeDtypeStruct(shape, jnp.bfloat16),
        scratch_shapes=[pltpu.SemaphoreType.DMA((len(pieces),))],
        input_output_aliases={0: 0} if given else {},
        cost_estimate=cost,
        compiler_params=pltpu.CompilerParams(vmem_limit_bytes=8 * 2**20),
        name="assemble",
    )(*given, *[piece for piece, _ in pieces])


def local(stream, queries, keys, values, segments):
    stream, queries, keys, values = stream[0], queries[0], keys[0], values[0]
    segments = segments.reshape(1, -1)
    tokens = queries.shape[0]
    relay = lambda value: exchange(value, "section", 1)
    def own(full, head):
        block, one, mates, core, first = full
        at = [(part, head - first) for part in (block, one, mates, core)]
        return attend(at, queries, stream, head * WIDTH, 0, 0, LIGHT)

    def passed(full, n, q, q_row, s, s_row):
        return attend([(part, n) for part in full], q, s, 0, q_row, s_row, HEAVY)

    chunk_a, chunk_b, chunk_f = (0, 2), (2, 3), (5, 3)
    cut = 3 * tokens // 4
    whole = lambda chunk: (0, chunk[1])
    block_a, block_b = pack_blocks(keys, values, segments, (chunk_a, chunk_b))
    keys = gate(keys, block_a)
    wide_a = relay(pack_wide(queries, stream, ((0, 5),), chunk_f, (keys, values, segments)))
    behind_a = gather_behind(block_a)
    wide_b = pack_wide(gate(queries, block_a), stream, ((1, 5), (0, 6), (1, 6), (0, 7), (1, 7)))
    wide_b, behind_a = gate((wide_b, behind_a), wide_a, wide_b)
    wide_b = relay(wide_b)
    block_f = unfold(wide_a, tokens, tokens, chunk_f)
    behind_b = gather_behind(gate(block_b, behind_a))
    y_a = over_y(block_a, behind_a, whole(chunk_a))
    behind_f = gather_behind(gate(block_f, behind_b, y_a))
    y_b = over_y(gate(block_b, y_a), behind_b, whole(chunk_b))
    core_a = over_core(gate(block_a, behind_b), behind_a, y_a, whole(chunk_a))
    full_a = (block_a, behind_a[0], y_a, core_a)
    piece_0 = own(full_a + (0,), 0)
    recv_0 = relay(piece_0[:cut])
    piece_1 = own(gate(full_a, piece_0) + (0,), 1)
    recv_1 = relay(jnp.concatenate([piece_0[cut:], piece_1]))
    block_b, block_f = gate((block_b, block_f), behind_f, y_b, recv_0, piece_1, wide_b)
    core_b = over_core(block_b, behind_b, y_b, whole(chunk_b))
    y_f = over_y(block_f, behind_f, whole(chunk_f))
    full_b = (block_b, behind_b[0], y_b, core_b)
    piece_2 = own(full_b + (2,), 2)
    recv_2 = relay(piece_2)
    piece_3 = own(gate(full_b, piece_2) + (2,), 3)
    recv_3 = relay(piece_3)
    piece_4 = own(gate(full_b, piece_3) + (2,), 4)
    recv_4 = relay(piece_4)
    core_f = over_core(gate(block_f, piece_4, recv_1), behind_f, y_f, whole(chunk_f))
    full_f = (block_f, behind_f[0], y_f, core_f)
    piece_5 = passed(gate(full_f, recv_2), 0, wide_a, 0, wide_b, 0)
    piece_6 = passed(gate(full_f, piece_5, recv_3), 1, wide_b, tokens, wide_b, 2 * tokens)
    piece_7 = passed(gate(full_f, piece_6), 2, wide_b, 3 * tokens, wide_b, 4 * tokens)
    pieces = [
        (recv_0, (0, 0)),
        (recv_1[: tokens - cut], (cut, 0)),
        (recv_1[tokens - cut :], (0, WIDTH)),
        (recv_2, (0, 2 * WIDTH)),
        (recv_3, (0, 3 * WIDTH)),
        (piece_5, (0, 5 * WIDTH)),
        (piece_6, (0, 6 * WIDTH)),
        (piece_7, (0, 7 * WIDTH)),
    ]
    pieces.append((recv_4, (0, 4 * WIDTH)))
    return assemble(None, pieces, queries.shape, LIGHT)[None]


def solution(mesh):
    in_specs = (
        P("section", "ctx", None),
        P("section", "ctx", None),
        P("section", "ctx", None),
        P("section", "ctx", None),
        P("section", "ctx"),
    )
    out_specs = P("section", "ctx", None)
    return jax.shard_map(local, mesh=mesh, in_specs=in_specs, out_specs=out_specs, check_vma=False)
```

time: 153 us -> 126 us (0.82); the launches traced: 153 us -> 124 us
  waiting for transfers between devices: 68.4 us -> 50.2 us
  starting transfers between devices: 42.1 us -> 26.3 us
  Pallas kernels: 32.4 us -> 45.2 us
  local copies, waits for them, and re-layouts: 7.75 us -> 1.56 us
    ppermute x20 -> x13, waiting for transfers between devices: 51.6 us -> 20.8 us  [exchange(): lax.ppermute(value, axis, [(i, i ^ bit) for i in range(lax.axis_size(axis...]
    pallas_call x8 -> x19, Pallas kernels: 32.4 us -> 45.2 us  [the longest x8 33.7 us: attend(): pl.pallas_call(functools.partial(attend_kernel, tokens, column, query_row...]
    ppermute x12 -> x6, waiting for transfers between devices: 16.8 us -> 29.4 us  [from_groups_behind(): return lax.ppermute(value, 'ctx', pairs)]
    ppermute x20 -> x13, starting transfers between devices: 18.2 us -> 9.93 us  [exchange(): lax.ppermute(value, axis, [(i, i ^ bit) for i in range(lax.axis_size(axis...]
    ppermute x12 -> x6, starting transfers between devices: 23.9 us -> 16.4 us  [from_groups_behind(): return lax.ppermute(value, 'ctx', pairs)]
    unnamed x18 -> x16, local copies, waits for them, and re-layouts: 6.07 us -> 1.49 us
  transfers between devices with their start and end apart: 32 -> 19, of which waited for: 15 -> 9; matrix products, arithmetic and copies ran while one was open for 1% -> 0% of each run, Pallas kernels for 21% -> 30%
where the time goes in v2:
time: 126 us; the launch traced here: 124 us
  waiting for transfers between devices  50.2 us (40%)
  Pallas kernels  45.2 us (36%)
  starting transfers between devices  26.3 us (21%)
  local copies, waits for them, and re-layouts  1.56 us (1%)
    pallas_call x8, Pallas kernels, attend(): pl.pallas_call(functools.partial(attend_kernel, tokens, column, query_row...  33.7 us
    ppermute x6, waiting for transfers between devices, from_groups_behind(): return lax.ppermute(value, 'ctx', pairs)  29.4 us
    ppermute x13, waiting for transfers between devices, exchange(): lax.ppermute(value, axis, [(i, i ^ bit) for i in range(lax.axis_size(axis...  20.8 us
    ppermute x6, starting transfers between devices, from_groups_behind(): return lax.ppermute(value, 'ctx', pairs)  16.4 us
    ppermute x13, starting transfers between devices, exchange(): lax.ppermute(value, axis, [(i, i ^ bit) for i in range(lax.axis_size(axis...  9.93 us
    pallas_call x2, Pallas kernels, pack_wide(): pl.pallas_call(functools.partial(pack_wide_kernel, parts, chunk), in_spec...  5.96 us
    pallas_call x1, Pallas kernels, assemble(): pl.pallas_call(functools.partial(assemble_kernel, places), in_specs=[pl.B...  2.73 us
  transfers between devices with their start and end apart: 19, of which 9 were waited for; matrix products, arithmetic and copies ran while one was open for 0% of the time, Pallas kernels for 30%

profile of v2, /device:TPU:18, one launch (start us, length us, event | category | flops | bytes accessed | tf_op | source)
XLA Modules:
  0.0 123.8 jit_solution(10812659465937193224)
XLA Ops:
  0.0 2.0 %pack_blocks.1 = (bf16[208,512]{1,0:T(8,128)(2,1)}, bf16[208,768]{1,0:T(8,128)(2,1)}) custom-call(bf16[192,1024]{1,0:T(8,128)(2,1)} %bitcast.19, bf16[192,1024]{1,0:T(8,128)(2,1)} %bitcast.21, s32[1,192]{1,0:T(1,128)} %refs_2_.1), custom_call_target="tpu_custom_call" | custom-call | flops 1 | bytes 1 | tf_op jit(solution)/shard_map/pack_blocks/pallas_call | solution.py:116
  2.0 3.0 %pack_wide.3 = bf16[352,1024]{1,0:T(8,128)(2,1)} custom-call(bf16[192,8192]{1,0:T(8,128)(2,1)} %bitcast.5, bf16[192,8192]{1,0:T(8,128)(2,1)} %bitcast.12, bf16[192,1024]{1,0:T(8,128)(2,1)} %bitcast.20, bf16[192,1024]{1,0:T(8,128)(2,1)} %bitcast.22, s32[1,192]{1,0:T(1,128)} %refs_2_.1), custom_call_target="tpu_custom_call" | custom-call | flops 1 | bytes 1 | tf_op jit(solution)/shard_map/pack_wide/pallas_call | solution.py:170
  5.0 0.6 collective-permute-start.2
  5.6 3.5 %collective-permute-start = (bf16[208,512]{1,0:T(8,128)(2,1)S(1)}, bf16[208,512]{1,0:T(8,128)(2,1)S(1)}, u32[]{:S(2)}, u32[]{:S(2)}) collective-permute-start(bf16[208,512]{1,0:T(8,128)(2,1)S(1)} %copy-done.3), channel_id=1, source_target_pairs={{0,4},{1,5},{2,6},{3,7},{4,8},{5,9},{6,10},{7,11},{8,12},{9,13},{1... | collective-permute-start | bytes 638984 | tf_op jit(solution)/shard_map/ppermute | solution.py:44
  9.5 2.9 %pack_wide.2 = bf16[960,1024]{1,0:T(8,128)(2,1)} custom-call(bf16[192,8192]{1,0:T(8,128)(2,1)} %bitcast.6, bf16[192,8192]{1,0:T(8,128)(2,1)} %bitcast.13), custom_call_target="tpu_custom_call" | custom-call | flops 1 | bytes 1 | tf_op jit(solution)/shard_map/pack_wide/pallas_call | solution.py:170
  12.5 7.8 %collective-permute-done.refs_0_.refs_1_ = bf16[208,512]{1,0:T(8,128)(2,1)S(1)} collective-permute-done((bf16[208,512]{1,0:T(8,128)(2,1)S(1)}, bf16[208,512]{1,0:T(8,128)(2,1)S(1)}, u32[]{:S(2)}, u32[]{:S(2)}) %collective-permute-start) | collective-permute-done | bytes 213024 | tf_op jit(solution)/shard_map/ppermute | solution.py:44
  20.3 2.9 %collective-permute-done.2.wide.refs_8_ = bf16[352,1024]{1,0:T(8,128)(2,1)S(1)} collective-permute-done((bf16[352,1024]{1,0:T(8,128)(2,1)}, bf16[352,1024]{1,0:T(8,128)(2,1)S(1)}, u32[]{:S(2)}, u32[]{:S(2)}) %collective-permute-start.2) | collective-permute-done | bytes 720928 | tf_op jit(solution)/shard_map/ppermute | solution.py:36
  23.8 1.6 %collective-permute-start.3 = (bf16[416,512]{1,0:T(8,128)(2,1)S(1)}, bf16[416,512]{1,0:T(8,128)(2,1)S(1)}, u32[]{:S(2)}, u32[]{:S(2)}) collective-permute-start(bf16[416,512]{1,0:T(8,128)(2,1)S(1)} %join.6), channel_id=1, source_target_pairs={{0,2},{1,3},{2,0},{3,1},{4,6},{5,7},{6,4},{7,5},{8,10},{9,11},{10,... | collective-permute-start | bytes 1277960 | tf_op jit(solution)/shard_map/ppermute | solution.py:36
  25.4 4.8 %collective-permute-start.4 = (bf16[208,768]{1,0:T(8,128)(2,1)S(1)}, bf16[208,768]{1,0:T(8,128)(2,1)S(1)}, u32[]{:S(2)}, u32[]{:S(2)}) collective-permute-start(bf16[208,768]{1,0:T(8,128)(2,1)S(1)} %copy-done.2), channel_id=1, source_target_pairs={{0,4},{1,5},{2,6},{3,7},{4,8},{5,9},{6,10},{7,11},{8,12},{9,13},{1... | collective-permute-start | bytes 958472 | tf_op jit(solution)/shard_map/ppermute | solution.py:44
  30.2 14.6 %collective-permute-done.4.refs_0_.refs_1_ = bf16[208,768]{1,0:T(8,128)(2,1)S(1)} collective-permute-done((bf16[208,768]{1,0:T(8,128)(2,1)S(1)}, bf16[208,768]{1,0:T(8,128)(2,1)S(1)}, u32[]{:S(2)}, u32[]{:S(2)}) %collective-permute-start.4) | collective-permute-done | bytes 319520 | tf_op jit(solution)/shard_map/ppermute | solution.py:44
  45.6 0.7 collective-permute-start.10
  46.3 7.0 %collective-permute-start.9 = (bf16[208,768]{1,0:T(8,128)(2,1)S(1)}, bf16[208,768]{1,0:T(8,128)(2,1)S(1)}, u32[]{:S(2)}, u32[]{:S(2)}) collective-permute-start(bf16[208,768]{1,0:T(8,128)(2,1)S(1)} %unfold.1.refs_1_.refs_2_.refs_0_), channel_id=1, source_target_pairs={{0,4},{1,5},{2,6},{3,7},{4,8},{5,9},{6,10},{7,11},{8,12},{9,13},{1... | collective-permute-start | bytes 958472 | tf_op jit(solution)/shard_map/ppermute | solution.py:44
  53.3 4.0 %attend.8 = bf16[192,1024]{1,0:T(8,128)(2,1)S(1)} custom-call(bf16[208,512]{1,0:T(8,128)(2,1)S(1)} %copy-done.3, bf16[208,512]{1,0:T(8,128)(2,1)S(1)} %collective-permute-done.refs_0_.refs_1_, bf16[416,512]{1,0:T(8,128)(2,1)S(1)} %collective-permute-done.3.refs_1_.refs_2_.refs_3_, bf16[416,512]{1,0:T(8,128)(2,1)S(1)} %collective-permute-done.3.refs_1_.refs_2_.refs_3_, ...), custom_call_target="tpu_custom_call" | custom-call | flops 1 | bytes 1 | tf_op jit(solution)/shard_map/attend/pallas_call | solution.py:300
  57.4 1.6 %collective-permute-start.7 = (bf16[144,1024]{1,0:T(8,128)(2,1)S(1)}, bf16[144,1024]{1,0:T(8,128)(2,1)S(1)}, u32[]{:S(2)}, u32[]{:S(2)}) collective-permute-start(bf16[144,1024]{1,0:T(8,128)(2,1)S(1)} %slice.16), channel_id=1, source_target_pairs={{0,16},{16,0},{1,17},{17,1},{2,18},{18,2},{3,19},{19,3},{4,20},{20... | collective-permute-start | bytes 884744 | tf_op jit(solution)/shard_map/ppermute | solution.py:36
  58.9 4.0 %attend.9 = bf16[192,1024]{1,0:T(8,128)(2,1)S(1)} custom-call(bf16[208,512]{1,0:T(8,128)(2,1)S(1)} %copy-done.3, bf16[208,512]{1,0:T(8,128)(2,1)S(1)} %collective-permute-done.refs_0_.refs_1_, bf16[416,512]{1,0:T(8,128)(2,1)S(1)} %collective-permute-done.3.refs_1_.refs_2_.refs_3_, bf16[416,512]{1,0:T(8,128)(2,1)S(1)} %collective-permute-done.3.refs_1_.refs_2_.refs_3_, ...), custom_call_target="tpu_custom_call" | custom-call | flops 1 | bytes 1 | tf_op jit(solution)/shard_map/attend/pallas_call | solution.py:300
  63.0 7.0 %collective-permute-done.9.refs_0_.refs_1_ = bf16[208,768]{1,0:T(8,128)(2,1)S(1)} collective-permute-done((bf16[208,768]{1,0:T(8,128)(2,1)S(1)}, bf16[208,768]{1,0:T(8,128)(2,1)S(1)}, u32[]{:S(2)}, u32[]{:S(2)}) %collective-permute-start.9) | collective-permute-done | bytes 319520 | tf_op jit(solution)/shard_map/ppermute | solution.py:44
  70.0 3.4 %collective-permute-done.7.refs_0_ = bf16[144,1024]{1,0:T(8,128)(2,1)S(1)} collective-permute-done((bf16[144,1024]{1,0:T(8,128)(2,1)S(1)}, bf16[144,1024]{1,0:T(8,128)(2,1)S(1)}, u32[]{:S(2)}, u32[]{:S(2)}) %collective-permute-start.7) | collective-permute-done | bytes 294944 | tf_op jit(solution)/shard_map/ppermute | solution.py:36
  73.4 0.7 copy-done.6
  74.6 1.6 %collective-permute-start.16 = (bf16[416,768]{1,0:T(8,128)(2,1)S(1)}, bf16[416,768]{1,0:T(8,128)(2,1)S(1)}, u32[]{:S(2)}, u32[]{:S(2)}) collective-permute-start(bf16[416,768]{1,0:T(8,128)(2,1)S(1)} %join.10), channel_id=1, source_target_pairs={{0,2},{1,3},{2,0},{3,1},{4,6},{5,7},{6,4},{7,5},{8,10},{9,11},{10,... | collective-permute-start | bytes 1916936 | tf_op jit(solution)/shard_map/ppermute | solution.py:36
  76.2 0.6 collective-permute-start.8
  77.3 4.0 %attend.10 = bf16[192,1024]{1,0:T(8,128)(2,1)S(1)} custom-call(bf16[208,768]{1,0:T(8,128)(2,1)S(1)} %copy-done.2, bf16[208,768]{1,0:T(8,128)(2,1)S(1)} %collective-permute-done.4.refs_0_.refs_1_, bf16[416,768]{1,0:T(8,128)(2,1)S(1)} %collective-permute-done.11.refs_1_.refs_2_.refs_3_, bf16[416,768]{1,0:T(8,128)(2,1)S(1)} %collective-permute-done.11.refs_1_.refs_2_.refs_3_, ...), custom_call_target="tpu_custom_call" | custom-call | flops 1 | bytes 1 | tf_op jit(solution)/shard_map/attend/pallas_call | solution.py:300
  81.3 4.0 %attend.11 = bf16[192,1024]{1,0:T(8,128)(2,1)S(1)} custom-call(bf16[208,768]{1,0:T(8,128)(2,1)S(1)} %copy-done.2, bf16[208,768]{1,0:T(8,128)(2,1)S(1)} %collective-permute-done.4.refs_0_.refs_1_, bf16[416,768]{1,0:T(8,128)(2,1)S(1)} %collective-permute-done.11.refs_1_.refs_2_.refs_3_, bf16[416,768]{1,0:T(8,128)(2,1)S(1)} %collective-permute-done.11.refs_1_.refs_2_.refs_3_, ...), custom_call_target="tpu_custom_call" | custom-call | flops 1 | bytes 1 | tf_op jit(solution)/shard_map/attend/pallas_call | solution.py:300
  85.3 4.8 %attend.12 = bf16[192,1024]{1,0:T(8,128)(2,1)} custom-call(bf16[208,768]{1,0:T(8,128)(2,1)S(1)} %copy-done.2, bf16[208,768]{1,0:T(8,128)(2,1)S(1)} %collective-permute-done.4.refs_0_.refs_1_, bf16[416,768]{1,0:T(8,128)(2,1)S(1)} %collective-permute-done.11.refs_1_.refs_2_.refs_3_, bf16[416,768]{1,0:T(8,128)(2,1)S(1)} %collective-permute-done.11.refs_1_.refs_2_.refs_3_, ...), custom_call_target="tpu_custom_call" | custom-call | flops 1 | bytes 1 | tf_op jit(solution)/shard_map/attend/pallas_call | solution.py:300
  90.1 1.3 %collective-permute-done.16.refs_1_.refs_2_.refs_3_ = bf16[416,768]{1,0:T(8,128)(2,1)S(1)} collective-permute-done((bf16[416,768]{1,0:T(8,128)(2,1)S(1)}, bf16[416,768]{1,0:T(8,128)(2,1)S(1)}, u32[]{:S(2)}, u32[]{:S(2)}) %collective-permute-start.16) | collective-permute-done | bytes 639008 | tf_op jit(solution)/shard_map/ppermute | solution.py:36
  92.4 1.6 %collective-permute-start.15 = (bf16[192,1024]{1,0:T(8,128)(2,1)S(1)}, bf16[192,1024]{1,0:T(8,128)(2,1)S(1)}, u32[]{:S(2)}, u32[]{:S(2)}) collective-permute-start(bf16[192,1024]{1,0:T(8,128)(2,1)S(1)} %attend.11), channel_id=1, source_target_pairs={{0,16},{16,0},{1,17},{17,1},{2,18},{18,2},{3,19},{19,3},{4,20},{20... | collective-permute-start | bytes 1179656 | tf_op jit(solution)/shard_map/ppermute | solution.py:36
  94.5 9.2 %collective-permute-done.14.refs_3_ = bf16[192,1024]{1,0:T(8,128)(2,1)S(1)} collective-permute-done((bf16[192,1024]{1,0:T(8,128)(2,1)S(1)}, bf16[192,1024]{1,0:T(8,128)(2,1)S(1)}, u32[]{:S(2)}, u32[]{:S(2)}) %collective-permute-start.14) | collective-permute-done | bytes 393248 | tf_op jit(solution)/shard_map/ppermute | solution.py:36
  103.8 0.7 copy-done.4
  104.5 4.3 %attend.13.refs_5_ = bf16[192,1024]{1,0:T(8,128)(2,1)S(1)} custom-call(bf16[208,768]{1,0:T(8,128)(2,1)S(1)} %unfold.1.refs_1_.refs_2_.refs_0_, bf16[208,768]{1,0:T(8,128)(2,1)S(1)} %collective-permute-done.9.refs_0_.refs_1_, bf16[416,768]{1,0:T(8,128)(2,1)S(1)} %collective-permute-done.16.refs_1_.refs_2_.refs_3_, ...), custom_call_target="tpu_custom_call" | custom-call | flops 99999997952 | bytes 1000000 | tf_op jit(solution)/shard_map/attend/pallas_call | solution.py:300
  108.8 3.3 %collective-permute-done.15.refs_4_ = bf16[192,1024]{1,0:T(8,128)(2,1)S(1)} collective-permute-done((bf16[192,1024]{1,0:T(8,128)(2,1)S(1)}, bf16[192,1024]{1,0:T(8,128)(2,1)S(1)}, u32[]{:S(2)}, u32[]{:S(2)}) %collective-permute-start.15) | collective-permute-done | bytes 393248 | tf_op jit(solution)/shard_map/ppermute | solution.py:36
  112.2 4.3 %attend.14.refs_6_ = bf16[192,1024]{1,0:T(8,128)(2,1)S(1)} custom-call(bf16[208,768]{1,0:T(8,128)(2,1)S(1)} %unfold.1.refs_1_.refs_2_.refs_0_, bf16[208,768]{1,0:T(8,128)(2,1)S(1)} %collective-permute-done.9.refs_0_.refs_1_, bf16[416,768]{1,0:T(8,128)(2,1)S(1)} %collective-permute-done.16.refs_1_.refs_2_.refs_3_, ...), custom_call_target="tpu_custom_call" | custom-call | flops 99999997952 | bytes 1000000 | tf_op jit(solution)/shard_map/attend/pallas_call | solution.py:300
  116.5 4.3 %attend.15.refs_7_ = bf16[192,1024]{1,0:T(8,128)(2,1)S(1)} custom-call(bf16[208,768]{1,0:T(8,128)(2,1)S(1)} %unfold.1.refs_1_.refs_2_.refs_0_, bf16[208,768]{1,0:T(8,128)(2,1)S(1)} %collective-permute-done.9.refs_0_.refs_1_, bf16[416,768]{1,0:T(8,128)(2,1)S(1)} %collective-permute-done.16.refs_1_.refs_2_.refs_3_, ...), custom_call_target="tpu_custom_call" | custom-call | flops 99999997952 | bytes 1000000 | tf_op jit(solution)/shard_map/attend/pallas_call | solution.py:300
  120.9 2.7 %assemble.1 = bf16[192,8192]{1,0:T(8,128)(2,1)} custom-call(bf16[144,1024]{1,0:T(8,128)(2,1)S(1)} %copy-done.7, bf16[48,1024]{1,0:T(8,128)(2,1)S(1)} %slice.18.refs_1_, bf16[192,1024]{1,0:T(8,128)(2,1)S(1)} %slice.19.refs_2_, bf16[192,1024]{1,0:T(8,128)(2,1)S(1)} %copy-done.5, bf16[192,1024]{1,0:T(8,128)(2,1)S(1)} %collective-permute-done.15.refs_4_, ...), custom_call_target="tpu_custom_call" | custom-call | flops 1 | bytes 1 | tf_op jit(solution)/shard_map/assemble/pallas_call | solution.py:342
  (46 shorter events, 4.4 us)
Async XLA Ops:
  2.0 3.6 %copy-start.3 = (bf16[208,512]{1,0:T(8,128)(2,1)S(1)}, bf16[208,512]{1,0:T(8,128)(2,1)}, u32[]{:S(2)}) copy-start(bf16[208,512]{1,0:T(8,128)(2,1)} %get-tuple-element.51.refs_1_.refs_2_.refs_0_) | copy-start | bytes 638980
  5.0 20.3 %copy-start.2 = (bf16[208,768]{1,0:T(8,128)(2,1)S(1)}, bf16[208,768]{1,0:T(8,128)(2,1)}, u32[]{:S(2)}) copy-start(bf16[208,768]{1,0:T(8,128)(2,1)} %get-tuple-element.64.refs_1_.refs_2_.refs_0_) | copy-start | bytes 958468
  5.0 18.2 %collective-permute-start.2 = (bf16[352,1024]{1,0:T(8,128)(2,1)}, bf16[352,1024]{1,0:T(8,128)(2,1)S(1)}, u32[]{:S(2)}, u32[]{:S(2)}) collective-permute-start(bf16[352,1024]{1,0:T(8,128)(2,1)} %pack_wide.3), channel_id=1, source_target_pairs={{0,16},{16,0},{1,17},{17,1},{2,18},{18,2},{3,19},{19,3},{4,20},{20... | collective-permute-start | bytes 2162696 | tf_op jit(solution)/shard_map/ppermute | solution.py:36
  5.6 14.6 %collective-permute-start = (bf16[208,512]{1,0:T(8,128)(2,1)S(1)}, bf16[208,512]{1,0:T(8,128)(2,1)S(1)}, u32[]{:S(2)}, u32[]{:S(2)}) collective-permute-start(bf16[208,512]{1,0:T(8,128)(2,1)S(1)} %copy-done.3), channel_id=1, source_target_pairs={{0,4},{1,5},{2,6},{3,7},{4,8},{5,9},{6,10},{7,11},{8,12},{9,13},{1... | collective-permute-start | bytes 638984 | tf_op jit(solution)/shard_map/ppermute | solution.py:44
  9.1 11.1 %collective-permute-start.1 = (bf16[208,512]{1,0:T(8,128)(2,1)S(1)}, bf16[208,512]{1,0:T(8,128)(2,1)S(1)}, u32[]{:S(2)}, u32[]{:S(2)}) collective-permute-start(bf16[208,512]{1,0:T(8,128)(2,1)S(1)} %copy-done.3), channel_id=1, source_target_pairs={{0,8},{1,9},{2,10},{3,11},{4,12},{5,13},{6,14},{7,15},{8,0},{9,1},... | collective-permute-start | bytes 638984 | tf_op jit(solution)/shard_map/ppermute | solution.py:44
  9.5 43.8 %copy-start.1 = (bf16[1,192,8192]{2,1,0:T(8,128)(2,1)S(1)}, bf16[1,192,8192]{2,1,0:T(8,128)(2,1)}, u32[]{:S(2)}) copy-start(bf16[1,192,8192]{2,1,0:T(8,128)(2,1)} %param.5) | copy-start | bytes 9437188
  23.2 50.9 %collective-permute-start.12 = (bf16[960,1024]{1,0:T(8,128)(2,1)}, bf16[960,1024]{1,0:T(8,128)(2,1)S(1)}, u32[]{:S(2)}, u32[]{:S(2)}) collective-permute-start(bf16[960,1024]{1,0:T(8,128)(2,1)} %pack_wide.2), channel_id=1, source_target_pairs={{0,16},{16,0},{1,17},{17,1},{2,18},{18,2},{3,19},{19,3},{4,20},{20... | collective-permute-start | bytes 5898248 | tf_op jit(solution)/shard_map/ppermute | solution.py:36
  23.8 21.1 %collective-permute-start.3 = (bf16[416,512]{1,0:T(8,128)(2,1)S(1)}, bf16[416,512]{1,0:T(8,128)(2,1)S(1)}, u32[]{:S(2)}, u32[]{:S(2)}) collective-permute-start(bf16[416,512]{1,0:T(8,128)(2,1)S(1)} %join.6), channel_id=1, source_target_pairs={{0,2},{1,3},{2,0},{3,1},{4,6},{5,7},{6,4},{7,5},{8,10},{9,11},{10,... | collective-permute-start | bytes 1277960 | tf_op jit(solution)/shard_map/ppermute | solution.py:36
  25.4 28.0 %copy-start = (bf16[1,192,8192]{2,1,0:T(8,128)(2,1)S(1)}, bf16[1,192,8192]{2,1,0:T(8,128)(2,1)}, u32[]{:S(2)}) copy-start(bf16[1,192,8192]{2,1,0:T(8,128)(2,1)} %param.6) | copy-start | bytes 9437188
  25.4 19.5 %collective-permute-start.4 = (bf16[208,768]{1,0:T(8,128)(2,1)S(1)}, bf16[208,768]{1,0:T(8,128)(2,1)S(1)}, u32[]{:S(2)}, u32[]{:S(2)}) collective-permute-start(bf16[208,768]{1,0:T(8,128)(2,1)S(1)} %copy-done.2), channel_id=1, source_target_pairs={{0,4},{1,5},{2,6},{3,7},{4,8},{5,9},{6,10},{7,11},{8,12},{9,13},{1... | collective-permute-start | bytes 958472 | tf_op jit(solution)/shard_map/ppermute | solution.py:44
  30.1 14.7 %collective-permute-start.5 = (bf16[208,768]{1,0:T(8,128)(2,1)S(1)}, bf16[208,768]{1,0:T(8,128)(2,1)S(1)}, u32[]{:S(2)}, u32[]{:S(2)}) collective-permute-start(bf16[208,768]{1,0:T(8,128)(2,1)S(1)} %copy-done.2), channel_id=1, source_target_pairs={{0,8},{1,9},{2,10},{3,11},{4,12},{5,13},{6,14},{7,15},{8,0},{9,1},... | collective-permute-start | bytes 958472 | tf_op jit(solution)/shard_map/ppermute | solution.py:44
  44.9 8.4 %collective-permute-start.6 = (bf16[832,512]{1,0:T(8,128)(2,1)S(1)}, bf16[832,512]{1,0:T(8,128)(2,1)S(1)}, u32[]{:S(2)}, u32[]{:S(2)}) collective-permute-start(bf16[832,512]{1,0:T(8,128)(2,1)S(1)} %join.7), channel_id=1, source_target_pairs={{0,1},{1,0},{2,3},{3,2},{4,5},{5,4},{6,7},{7,6},{8,9},{9,8},{10,11... | collective-permute-start | bytes 2555912 | tf_op jit(solution)/shard_map/ppermute | solution.py:36
  45.0 25.0 %collective-permute-start.11 = (bf16[416,768]{1,0:T(8,128)(2,1)S(1)}, bf16[416,768]{1,0:T(8,128)(2,1)S(1)}, u32[]{:S(2)}, u32[]{:S(2)}) collective-permute-start(bf16[416,768]{1,0:T(8,128)(2,1)S(1)} %join.8), channel_id=1, source_target_pairs={{0,2},{1,3},{2,0},{3,1},{4,6},{5,7},{6,4},{7,5},{8,10},{9,11},{10,... | collective-permute-start | bytes 1916936 | tf_op jit(solution)/shard_map/ppermute | solution.py:36
  45.6 17.3 %collective-permute-start.10 = (bf16[208,768]{1,0:T(8,128)(2,1)S(1)}, bf16[208,768]{1,0:T(8,128)(2,1)S(1)}, u32[]{:S(2)}, u32[]{:S(2)}) collective-permute-start(bf16[208,768]{1,0:T(8,128)(2,1)S(1)} %unfold.1.refs_1_.refs_2_.refs_0_), channel_id=1, source_target_pairs={{0,8},{1,9},{2,10},{3,11},{4,12},{5,13},{6,14},{7,15},{8,0},{9,1},... | collective-permute-start | bytes 958472 | tf_op jit(solution)/shard_map/ppermute | solution.py:44
  46.3 23.6 %collective-permute-start.9 = (bf16[208,768]{1,0:T(8,128)(2,1)S(1)}, bf16[208,768]{1,0:T(8,128)(2,1)S(1)}, u32[]{:S(2)}, u32[]{:S(2)}) collective-permute-start(bf16[208,768]{1,0:T(8,128)(2,1)S(1)} %unfold.1.refs_1_.refs_2_.refs_0_), channel_id=1, source_target_pairs={{0,4},{1,5},{2,6},{3,7},{4,8},{5,9},{6,10},{7,11},{8,12},{9,13},{1... | collective-permute-start | bytes 958472 | tf_op jit(solution)/shard_map/ppermute | solution.py:44
  57.4 16.0 %collective-permute-start.7 = (bf16[144,1024]{1,0:T(8,128)(2,1)S(1)}, bf16[144,1024]{1,0:T(8,128)(2,1)S(1)}, u32[]{:S(2)}, u32[]{:S(2)}) collective-permute-start(bf16[144,1024]{1,0:T(8,128)(2,1)S(1)} %slice.16), channel_id=1, source_target_pairs={{0,16},{16,0},{1,17},{17,1},{2,18},{18,2},{3,19},{19,3},{4,20},{20... | collective-permute-start | bytes 884744 | tf_op jit(solution)/shard_map/ppermute | solution.py:36
  73.4 0.7 copy-start.6
  74.2 3.1 %collective-permute-start.13 = (bf16[832,768]{1,0:T(8,128)(2,1)S(1)}, bf16[832,768]{1,0:T(8,128)(2,1)S(1)}, u32[]{:S(2)}, u32[]{:S(2)}) collective-permute-start(bf16[832,768]{1,0:T(8,128)(2,1)S(1)} %join.9), channel_id=1, source_target_pairs={{0,1},{1,0},{2,3},{3,2},{4,5},{5,4},{6,7},{7,6},{8,9},{9,8},{10,11... | collective-permute-start | bytes 3833864 | tf_op jit(solution)/shard_map/ppermute | solution.py:36
  74.6 16.8 %collective-permute-start.16 = (bf16[416,768]{1,0:T(8,128)(2,1)S(1)}, bf16[416,768]{1,0:T(8,128)(2,1)S(1)}, u32[]{:S(2)}, u32[]{:S(2)}) collective-permute-start(bf16[416,768]{1,0:T(8,128)(2,1)S(1)} %join.10), channel_id=1, source_target_pairs={{0,2},{1,3},{2,0},{3,1},{4,6},{5,7},{6,4},{7,5},{8,10},{9,11},{10,... | collective-permute-start | bytes 1916936 | tf_op jit(solution)/shard_map/ppermute | solution.py:36
  76.2 13.9 %collective-permute-start.8 = (bf16[240,1024]{1,0:T(8,128)(2,1)S(1)}, bf16[240,1024]{1,0:T(8,128)(2,1)S(1)}, u32[]{:S(2)}, u32[]{:S(2)}) collective-permute-start(bf16[240,1024]{1,0:T(8,128)(2,1)S(1)} %pad_maximum_fusion), channel_id=1, source_target_pairs={{0,16},{16,0},{1,17},{17,1},{2,18},{18,2},{3,19},{19,3},{4,20},{20... | collective-permute-start | bytes 1474568 | tf_op jit(solution)/shard_map/ppermute | solution.py:36
  91.7 12.8 %collective-permute-start.17 = (bf16[832,768]{1,0:T(8,128)(2,1)S(1)}, bf16[832,768]{1,0:T(8,128)(2,1)S(1)}, u32[]{:S(2)}, u32[]{:S(2)}) collective-permute-start(bf16[832,768]{1,0:T(8,128)(2,1)S(1)} %join.11), channel_id=1, source_target_pairs={{0,1},{1,0},{2,3},{3,2},{4,5},{5,4},{6,7},{7,6},{8,9},{9,8},{10,11... | collective-permute-start | bytes 3833864 | tf_op jit(solution)/shard_map/ppermute | solution.py:36
  91.8 12.0 %collective-permute-start.14 = (bf16[192,1024]{1,0:T(8,128)(2,1)S(1)}, bf16[192,1024]{1,0:T(8,128)(2,1)S(1)}, u32[]{:S(2)}, u32[]{:S(2)}) collective-permute-start(bf16[192,1024]{1,0:T(8,128)(2,1)S(1)} %attend.10), channel_id=1, source_target_pairs={{0,16},{16,0},{1,17},{17,1},{2,18},{18,2},{3,19},{19,3},{4,20},{20... | collective-permute-start | bytes 1179656 | tf_op jit(solution)/shard_map/ppermute | solution.py:36
  92.4 19.8 %collective-permute-start.15 = (bf16[192,1024]{1,0:T(8,128)(2,1)S(1)}, bf16[192,1024]{1,0:T(8,128)(2,1)S(1)}, u32[]{:S(2)}, u32[]{:S(2)}) collective-permute-start(bf16[192,1024]{1,0:T(8,128)(2,1)S(1)} %attend.11), channel_id=1, source_target_pairs={{0,16},{16,0},{1,17},{17,1},{2,18},{18,2},{3,19},{19,3},{4,20},{20... | collective-permute-start | bytes 1179656 | tf_op jit(solution)/shard_map/ppermute | solution.py:36
  94.0 26.9 %collective-permute-start.18 = (bf16[192,1024]{1,0:T(8,128)(2,1)}, bf16[192,1024]{1,0:T(8,128)(2,1)}, u32[]{:S(2)}, u32[]{:S(2)}) collective-permute-start(bf16[192,1024]{1,0:T(8,128)(2,1)} %attend.12), channel_id=1, source_target_pairs={{0,16},{16,0},{1,17},{17,1},{2,18},{18,2},{3,19},{19,3},{4,20},{20... | collective-permute-start | bytes 1179656 | tf_op jit(solution)/shard_map/ppermute | solution.py:36
  103.8 0.7 copy-start.4
  116.5 4.4 %copy-start.5 = (bf16[192,1024]{1,0:T(8,128)(2,1)S(1)}, bf16[192,1024]{1,0:T(8,128)(2,1)}, u32[]{:S(2)}) copy-start(bf16[192,1024]{1,0:T(8,128)(2,1)} %copy-done.4) | copy-start | bytes 1179652
  116.5 4.4 %copy-start.7 = (bf16[144,1024]{1,0:T(8,128)(2,1)S(1)}, bf16[144,1024]{1,0:T(8,128)(2,1)}, u32[]{:S(2)}) copy-start(bf16[144,1024]{1,0:T(8,128)(2,1)} %copy-done.6) | copy-start | bytes 884740

commit v3 on v2

--- a/solution.py
+++ b/solution.py
@@ -104,27 +104,6 @@
         out[tokens : tokens + 1, n * PAIR : n * PAIR + tokens] = row
 
 
-def pack_blocks_kernel(tokens, chunks, keys, values, seg, *outs):
-    for out, chunk in zip(outs, chunks):
-        fill_block(out, tokens, chunk, keys, values, seg)
-
-
-def pack_blocks(keys, values, segments, chunks):
-    tokens = keys.shape[0]
-    shapes = [(tokens + SEG_ROWS, size * PAIR) for _, size in chunks]
-    one = lambda i: (0, 0)
-    return pl.pallas_call(
-        functools.partial(pack_blocks_kernel, tokens, chunks),
-        grid=(1,),
-        in_specs=[pl.BlockSpec(keys.shape, one)] * 2 + [pl.BlockSpec((1, tokens), one)],
-        out_specs=[pl.BlockSpec(shape, one) for shape in shapes],
-        out_shape=[jax.ShapeDtypeStruct(shape, jnp.bfloat16) for shape in shapes],
-        cost_estimate=LIGHT,
-        compiler_params=pltpu.CompilerParams(vmem_limit_bytes=56 * 2**20),
-        name="pack_blocks",
-    )(keys, values, segments)
-
-
 def fold_places(rows, size):
     per_row = WIDTH // PAIR
     tiles = [(n, r) for n in range(size) for r in range(rows // SEG_ROWS)]
@@ -134,49 +113,85 @@
     ]
 
 
-def pack_wide_kernel(parts, chunk, queries, stream, *refs):
-    keys, values, seg, out, block, sems = refs if chunk else (None,) * 3 + refs[:1] + (None,) + refs[1:]
+def pack_first_kernel(chunks, passed, query_head, queries, keys_in, values_in, seg_in, *refs):
+    *blocks, out, block, keys, values, seg, sems = refs
+    tokens = queries.shape[0]
+    copies = [
+        pltpu.make_async_copy(source, target, sems.at[n])
+        for n, (source, target) in enumerate(
+            (
+                (keys_in, keys),
+                (values_in, values),
+                (seg_in, seg),
+                (queries.at[:, pl.ds(query_head * WIDTH, WIDTH)], out.at[pl.ds(0, tokens)]),
+            )
+        )
+    ]
+    for copy in copies:
+        copy.start()
+    for copy in copies[:3]:
+        copy.wait()
+    for target, chunk in zip(blocks, chunks):
+        fill_block(target, tokens, chunk, keys, values, seg)
+    fill_block(block, tokens, passed, keys, values, seg)
+    for row, column, to_row, to_column in fold_places(block.shape[0], passed[1]):
+        out[tokens + to_row : tokens + to_row + SEG_ROWS, to_column : to_column + PAIR] = block[
+            row : row + SEG_ROWS, column : column + PAIR
+        ]
+    copies[3].wait()
+
+
+def pack_first(queries, keys, values, segments, chunks, passed):
+    tokens = queries.shape[0]
+    block = lambda chunk: (tokens + SEG_ROWS, chunk[1] * PAIR)
+    folded = max(place[2] for place in fold_places(tokens + SEG_ROWS, passed[1])) + SEG_ROWS
+    shapes = [block(chunk) for chunk in chunks] + [(tokens + folded, WIDTH)]
+    vmem = pl.BlockSpec(memory_space=pltpu.VMEM)
+    return pl.pallas_call(
+        functools.partial(pack_first_kernel, chunks, passed, passed[0]),
+        in_specs=[pl.BlockSpec(memory_space=pltpu.HBM)] * 4,
+        out_specs=[vmem] * len(shapes),
+        out_shape=[jax.ShapeDtypeStruct(shape, jnp.bfloat16) for shape in shapes],
+        scratch_shapes=[
+            pltpu.VMEM(block(passed), jnp.bfloat16),
+            pltpu.VMEM(keys.shape, jnp.bfloat16),
+            pltpu.VMEM(values.shape, jnp.bfloat16),
+            pltpu.VMEM(segments.shape, segments.dtype),
+            pltpu.SemaphoreType.DMA((4,)),
+        ],
+        cost_estimate=LIGHT,
+        compiler_params=pltpu.CompilerParams(vmem_limit_bytes=56 * 2**20),
+        name="pack_first",
+    )(queries, keys, values, segments)
+
+
+def pack_wide_kernel(parts, queries, stream, out, sems):
     tokens = queries.shape[0]
     copies = [
         pltpu.make_async_copy(
-            source.at[:, pl.ds(head * WIDTH, WIDTH)],
+            (queries, stream)[m].at[:, pl.ds(head * WIDTH, WIDTH)],
             out.at[pl.ds(n * tokens, tokens)],
             sems.at[n],
         )
-        for n, (source, head) in enumerate(((queries, stream)[m], head) for m, head in parts)
+        for n, (m, head) in enumerate(parts)
     ]
     for copy in copies:
         copy.start()
-    if chunk:
-        fill_block(block, tokens, chunk, keys, values, seg)
-        base = len(parts) * tokens
-        for row, column, to_row, to_column in fold_places(block.shape[0], chunk[1]):
-            out[base + to_row : base + to_row + SEG_ROWS, to_column : to_column + PAIR] = block[
-                row : row + SEG_ROWS, column : column + PAIR
-            ]
     for copy in copies:
         copy.wait()
 
 
-def pack_wide(queries, stream, parts, chunk=None, others=()):
-    tokens = queries.shape[0]
-    rows = len(parts) * tokens
-    vmem = pl.BlockSpec(memory_space=pltpu.VMEM)
-    scratch = [pltpu.SemaphoreType.DMA((len(parts),))]
-    if chunk:
-        block = (tokens + SEG_ROWS, chunk[1] * PAIR)
-        rows += max(place[2] for place in fold_places(*block[:1], chunk[1])) + SEG_ROWS
-        scratch = [pltpu.VMEM(block, jnp.bfloat16)] + scratch
-    return pl.pallas_call(
-        functools.partial(pack_wide_kernel, parts, chunk),
-        in_specs=[pl.BlockSpec(memory_space=pltpu.HBM)] * 2 + [vmem] * len(others),
-        out_specs=vmem,
-        out_shape=jax.ShapeDtypeStruct((rows, WIDTH), jnp.bfloat16),
-        scratch_shapes=scratch,
+def pack_wide(queries, stream, parts):
+    return pl.pallas_call(
+        functools.partial(pack_wide_kernel, parts),
+        in_specs=[pl.BlockSpec(memory_space=pltpu.HBM)] * 2,
+        out_specs=pl.BlockSpec(memory_space=pltpu.VMEM),
+        out_shape=jax.ShapeDtypeStruct((len(parts) * queries.shape[0], WIDTH), jnp.bfloat16),
+        scratch_shapes=[pltpu.SemaphoreType.DMA((len(parts),))],
         cost_estimate=LIGHT,
         compiler_params=pltpu.CompilerParams(vmem_limit_bytes=56 * 2**20),
         name="pack_wide",
-    )(queries, stream, *others)
+    )(queries, stream)
 
 
 def unfold_kernel(base, size, wide, out):
@@ -364,14 +379,13 @@
         return attend(at, queries, stream, head * WIDTH, 0, 0, LIGHT)
 
     def passed(full, n, q, q_row, s, s_row):
-        return attend([(part, n) for part in full], q, s, 0, q_row, s_row, HEAVY)
+        return attend([(part, n) for part in full], q, s, 0, q_row, s_row, LIGHT)
 
     chunk_a, chunk_b, chunk_f = (0, 2), (2, 3), (5, 3)
-    cut = 3 * tokens // 4
+    cut, half = 3 * tokens // 4, tokens // 2
     whole = lambda chunk: (0, chunk[1])
-    block_a, block_b = pack_blocks(keys, values, segments, (chunk_a, chunk_b))
-    keys = gate(keys, block_a)
-    wide_a = relay(pack_wide(queries, stream, ((0, 5),), chunk_f, (keys, values, segments)))
+    block_a, block_b, wide_a = pack_first(queries, keys, values, segments, (chunk_a, chunk_b), chunk_f)
+    wide_a = relay(wide_a)
     behind_a = gather_behind(block_a)
     wide_b = pack_wide(gate(queries, block_a), stream, ((1, 5), (0, 6), (1, 6), (0, 7), (1, 7)))
     wide_b, behind_a = gate((wide_b, behind_a), wide_a, wide_b)
@@ -392,28 +406,31 @@
     y_f = over_y(block_f, behind_f, whole(chunk_f))
     full_b = (block_b, behind_b[0], y_b, core_b)
     piece_2 = own(full_b + (2,), 2)
-    recv_2 = relay(piece_2)
+    recv_2 = relay(piece_2[:half])
     piece_3 = own(gate(full_b, piece_2) + (2,), 3)
-    recv_3 = relay(piece_3)
+    recv_3 = relay(jnp.concatenate([piece_2[half:], piece_3]))
     piece_4 = own(gate(full_b, piece_3) + (2,), 4)
     recv_4 = relay(piece_4)
-    core_f = over_core(gate(block_f, piece_4, recv_1), behind_f, y_f, whole(chunk_f))
+    core_f = over_core(gate(block_f, piece_4, recv_1, recv_2), behind_f, y_f, whole(chunk_f))
     full_f = (block_f, behind_f[0], y_f, core_f)
-    piece_5 = passed(gate(full_f, recv_2), 0, wide_a, 0, wide_b, 0)
-    piece_6 = passed(gate(full_f, piece_5, recv_3), 1, wide_b, tokens, wide_b, 2 * tokens)
+    piece_5 = passed(full_f, 0, wide_a, 0, wide_b, 0)
+    piece_6 = passed(gate(full_f, piece_5), 1, wide_b, tokens, wide_b, 2 * tokens)
     piece_7 = passed(gate(full_f, piece_6), 2, wide_b, 3 * tokens, wide_b, 4 * tokens)
+    recv_3 = gate(recv_3, piece_6)
     pieces = [
         (recv_0, (0, 0)),
         (recv_1[: tokens - cut], (cut, 0)),
         (recv_1[tokens - cut :], (0, WIDTH)),
         (recv_2, (0, 2 * WIDTH)),
-        (recv_3, (0, 3 * WIDTH)),
+        (recv_3[: tokens - half], (half, 2 * WIDTH)),
+        (recv_3[tokens - half :], (0, 3 * WIDTH)),
         (piece_5, (0, 5 * WIDTH)),
         (piece_6, (0, 6 * WIDTH)),
-        (piece_7, (0, 7 * WIDTH)),
-    ]
-    pieces.append((recv_4, (0, 4 * WIDTH)))
-    return assemble(None, pieces, queries.shape, LIGHT)[None]
+    ]
+    out = assemble(None, pieces, queries.shape, LIGHT)
+    out = lax.dynamic_update_slice(out, piece_7, (0, 7 * WIDTH))
+    recv_4 = gate(recv_4, out)
+    return lax.dynamic_update_slice(out, recv_4, (0, 4 * WIDTH))[None]
 
 
 def solution(mesh):

time: 126 us -> 117 us (0.929)
  Pallas kernels: 45.2 us -> 40.6 us
  waiting for transfers between devices: 50.2 us -> 46.5 us
    ppermute x13, waiting for transfers between devices: 20.8 us -> 17.1 us  [exchange(): lax.ppermute(value, axis, [(i, i ^ bit) for i in range(lax.axis_size(axis...]
    pallas_call x3 -> x2, Pallas kernels: 7.96 us -> 5.32 us  [the longest x1 2.94 us: pack_wide(): pl.pallas_call(functools.partial(pack_wide_kernel, parts), in_specs=[pl.B...]
    dynamic_update_slice x0 -> x2, local copies, waits for them, and re-layouts: none -> 1.55 us  [the longest x1 0.78 us: local(): out = lax.dynamic_update_slice(out, piece_7, (0, 7 * WIDTH))]
    unnamed x16 -> x8, local copies, waits for them, and re-layouts: 1.49 us -> 0.02 us
  transfers between devices with their start and end apart: 19 -> 19, of which waited for: 9 -> 10; matrix products, arithmetic and copies ran while one was open for 0% -> 1% of each run, Pallas kernels for 30% -> 33%
where the time goes in v3:
time: 117 us; the launch traced here: 116 us
  waiting for transfers between devices  46.5 us (40%)
  Pallas kernels  40.6 us (35%)
  starting transfers between devices  26.5 us (23%)
  local copies, waits for them, and re-layouts  1.7 us (1%)
    pallas_call x8, Pallas kernels, attend(): pl.pallas_call(functools.partial(attend_kernel, tokens, column, query_row...  33.2 us
    ppermute x6, waiting for transfers between devices, from_groups_behind(): return lax.ppermute(value, 'ctx', pairs)  29.4 us
    ppermute x13, waiting for transfers between devices, exchange(): lax.ppermute(value, axis, [(i, i ^ bit) for i in range(lax.axis_size(axis...  17.1 us
    ppermute x6, starting transfers between devices, from_groups_behind(): return lax.ppermute(value, 'ctx', pairs)  16.3 us
    ppermute x13, starting transfers between devices, exchange(): lax.ppermute(value, axis, [(i, i ^ bit) for i in range(lax.axis_size(axis...  10.2 us
    pallas_call x1, Pallas kernels, pack_wide(): pl.pallas_call(functools.partial(pack_wide_kernel, parts), in_specs=[pl.B...  2.94 us
    pallas_call x1, Pallas kernels, pack_first(): pl.pallas_call(functools.partial(pack_first_kernel, chunks, passed, passe...  2.38 us
  transfers between devices with their start and end apart: 19, of which 10 were waited for; matrix products, arithmetic and copies ran while one was open for 1% of the time, Pallas kernels for 33%

profile of v3, /device:TPU:18, one launch (start us, length us, event | category | flops | bytes accessed | tf_op | source)
XLA Modules:
  0.0 115.7 jit_solution(10970289299528489633)
XLA Ops:
  0.0 2.4 %pack_first.1 = (bf16[208,512]{1,0:T(8,128)(2,1)}, bf16[208,768]{1,0:T(8,128)(2,1)}, bf16[352,1024]{1,0:T(8,128)(2,1)}) custom-call(bf16[192,8192]{1,0:T(8,128)(2,1)} %bitcast.7, bf16[192,1024]{1,0:T(8,128)(2,1)} %bitcast.21, bf16[192,1024]{1,0:T(8,128)(2,1)} %bitcast.22, s32[1,192]{1,0:T(1,128)} %seg_in.1), custom_call_target="tpu_custom_call" | custom-call | flops 1 | bytes 1 | tf_op jit(solution)/shard_map/pack_first/pallas_call | solution.py:150
  3.0 3.5 %collective-permute-start = (bf16[208,512]{1,0:T(8,128)(2,1)}, bf16[208,512]{1,0:T(8,128)(2,1)S(1)}, u32[]{:S(2)}, u32[]{:S(2)}) collective-permute-start(bf16[208,512]{1,0:T(8,128)(2,1)} %get-tuple-element.49.refs_1_.refs_2_.refs_0_), channel_id=1, source_target_pairs={{0,4},{1,5},{2,6},{3,7},{4,8},{5,9},{6,10},{7,11},{8,12},{9,13},{1... | collective-permute-start | bytes 638984 | tf_op jit(solution)/shard_map/ppermute | solution.py:44
  6.9 2.9 %pack_wide.1 = bf16[960,1024]{1,0:T(8,128)(2,1)} custom-call(bf16[192,8192]{1,0:T(8,128)(2,1)} %bitcast.8, bf16[192,8192]{1,0:T(8,128)(2,1)} %bitcast.14), custom_call_target="tpu_custom_call" | custom-call | flops 1 | bytes 1 | tf_op jit(solution)/shard_map/pack_wide/pallas_call | solution.py:185
  9.8 8.0 %collective-permute-done.refs_0_.refs_1_ = bf16[208,512]{1,0:T(8,128)(2,1)S(1)} collective-permute-done((bf16[208,512]{1,0:T(8,128)(2,1)}, bf16[208,512]{1,0:T(8,128)(2,1)S(1)}, u32[]{:S(2)}, u32[]{:S(2)}) %collective-permute-start) | collective-permute-done | bytes 213024 | tf_op jit(solution)/shard_map/ppermute | solution.py:44
  17.8 2.7 %collective-permute-done.2.wide.refs_8_ = bf16[352,1024]{1,0:T(8,128)(2,1)S(1)} collective-permute-done((bf16[352,1024]{1,0:T(8,128)(2,1)}, bf16[352,1024]{1,0:T(8,128)(2,1)S(1)}, u32[]{:S(2)}, u32[]{:S(2)}) %collective-permute-start.2) | collective-permute-done | bytes 720928 | tf_op jit(solution)/shard_map/ppermute | solution.py:36
  21.1 1.6 %collective-permute-start.3 = (bf16[416,512]{1,0:T(8,128)(2,1)S(1)}, bf16[416,512]{1,0:T(8,128)(2,1)S(1)}, u32[]{:S(2)}, u32[]{:S(2)}) collective-permute-start(bf16[416,512]{1,0:T(8,128)(2,1)S(1)} %join.6), channel_id=1, source_target_pairs={{0,2},{1,3},{2,0},{3,1},{4,6},{5,7},{6,4},{7,5},{8,10},{9,11},{10,... | collective-permute-start | bytes 1277960 | tf_op jit(solution)/shard_map/ppermute | solution.py:36
  22.7 4.7 %collective-permute-start.4 = (bf16[208,768]{1,0:T(8,128)(2,1)S(1)}, bf16[208,768]{1,0:T(8,128)(2,1)S(1)}, u32[]{:S(2)}, u32[]{:S(2)}) collective-permute-start(bf16[208,768]{1,0:T(8,128)(2,1)S(1)} %copy-done.2), channel_id=1, source_target_pairs={{0,4},{1,5},{2,6},{3,7},{4,8},{5,9},{6,10},{7,11},{8,12},{9,13},{1... | collective-permute-start | bytes 958472 | tf_op jit(solution)/shard_map/ppermute | solution.py:44
  27.5 14.4 %collective-permute-done.4.refs_0_.refs_1_ = bf16[208,768]{1,0:T(8,128)(2,1)S(1)} collective-permute-done((bf16[208,768]{1,0:T(8,128)(2,1)S(1)}, bf16[208,768]{1,0:T(8,128)(2,1)S(1)}, u32[]{:S(2)}, u32[]{:S(2)}) %collective-permute-start.4) | collective-permute-done | bytes 319520 | tf_op jit(solution)/shard_map/ppermute | solution.py:44
  42.7 0.9 collective-permute-start.10
  43.6 6.8 %collective-permute-start.9 = (bf16[208,768]{1,0:T(8,128)(2,1)S(1)}, bf16[208,768]{1,0:T(8,128)(2,1)S(1)}, u32[]{:S(2)}, u32[]{:S(2)}) collective-permute-start(bf16[208,768]{1,0:T(8,128)(2,1)S(1)} %unfold.1.refs_1_.refs_2_.refs_0_), channel_id=1, source_target_pairs={{0,4},{1,5},{2,6},{3,7},{4,8},{5,9},{6,10},{7,11},{8,12},{9,13},{1... | collective-permute-start | bytes 958472 | tf_op jit(solution)/shard_map/ppermute | solution.py:44
  50.4 4.0 %attend.8 = bf16[192,1024]{1,0:T(8,128)(2,1)S(1)} custom-call(bf16[208,512]{1,0:T(8,128)(2,1)S(1)} %copy-done.3, bf16[208,512]{1,0:T(8,128)(2,1)S(1)} %collective-permute-done.refs_0_.refs_1_, bf16[416,512]{1,0:T(8,128)(2,1)S(1)} %collective-permute-done.3.refs_1_.refs_2_.refs_3_, bf16[416,512]{1,0:T(8,128)(2,1)S(1)} %collective-permute-done.3.refs_1_.refs_2_.refs_3_, ...), custom_call_target="tpu_custom_call" | custom-call | flops 1 | bytes 1 | tf_op jit(solution)/shard_map/attend/pallas_call | solution.py:315
  54.5 1.6 %collective-permute-start.7 = (bf16[144,1024]{1,0:T(8,128)(2,1)S(1)}, bf16[144,1024]{1,0:T(8,128)(2,1)S(1)}, u32[]{:S(2)}, u32[]{:S(2)}) collective-permute-start(bf16[144,1024]{1,0:T(8,128)(2,1)S(1)} %slice.32), channel_id=1, source_target_pairs={{0,16},{16,0},{1,17},{17,1},{2,18},{18,2},{3,19},{19,3},{4,20},{20... | collective-permute-start | bytes 884744 | tf_op jit(solution)/shard_map/ppermute | solution.py:36
  56.0 4.0 %attend.9 = bf16[192,1024]{1,0:T(8,128)(2,1)S(1)} custom-call(bf16[208,512]{1,0:T(8,128)(2,1)S(1)} %copy-done.3, bf16[208,512]{1,0:T(8,128)(2,1)S(1)} %collective-permute-done.refs_0_.refs_1_, bf16[416,512]{1,0:T(8,128)(2,1)S(1)} %collective-permute-done.3.refs_1_.refs_2_.refs_3_, bf16[416,512]{1,0:T(8,128)(2,1)S(1)} %collective-permute-done.3.refs_1_.refs_2_.refs_3_, ...), custom_call_target="tpu_custom_call" | custom-call | flops 1 | bytes 1 | tf_op jit(solution)/shard_map/attend/pallas_call | solution.py:315
  60.0 7.0 %collective-permute-done.9.refs_0_.refs_1_ = bf16[208,768]{1,0:T(8,128)(2,1)S(1)} collective-permute-done((bf16[208,768]{1,0:T(8,128)(2,1)S(1)}, bf16[208,768]{1,0:T(8,128)(2,1)S(1)}, u32[]{:S(2)}, u32[]{:S(2)}) %collective-permute-start.9) | collective-permute-done | bytes 319520 | tf_op jit(solution)/shard_map/ppermute | solution.py:44
  67.1 3.7 %collective-permute-done.7.refs_0_ = bf16[144,1024]{1,0:T(8,128)(2,1)S(1)} collective-permute-done((bf16[144,1024]{1,0:T(8,128)(2,1)S(1)}, bf16[144,1024]{1,0:T(8,128)(2,1)S(1)}, u32[]{:S(2)}, u32[]{:S(2)}) %collective-permute-start.7) | collective-permute-done | bytes 294944 | tf_op jit(solution)/shard_map/ppermute | solution.py:36
  71.0 1.6 %collective-permute-start.16 = (bf16[416,768]{1,0:T(8,128)(2,1)S(1)}, bf16[416,768]{1,0:T(8,128)(2,1)S(1)}, u32[]{:S(2)}, u32[]{:S(2)}) collective-permute-start(bf16[416,768]{1,0:T(8,128)(2,1)S(1)} %join.10), channel_id=1, source_target_pairs={{0,2},{1,3},{2,0},{3,1},{4,6},{5,7},{6,4},{7,5},{8,10},{9,11},{10,... | collective-permute-start | bytes 1916936 | tf_op jit(solution)/shard_map/ppermute | solution.py:36
  73.2 0.7 collective-permute-done.13.refs_4_.refs_5_.refs_6_.refs_7_
  73.9 4.2 %attend.10 = bf16[192,1024]{1,0:T(8,128)(2,1)S(1)} custom-call(bf16[208,768]{1,0:T(8,128)(2,1)S(1)} %copy-done.2, bf16[208,768]{1,0:T(8,128)(2,1)S(1)} %collective-permute-done.4.refs_0_.refs_1_, bf16[416,768]{1,0:T(8,128)(2,1)S(1)} %collective-permute-done.11.refs_1_.refs_2_.refs_3_, bf16[416,768]{1,0:T(8,128)(2,1)S(1)} %collective-permute-done.11.refs_1_.refs_2_.refs_3_, ...), custom_call_target="tpu_custom_call" | custom-call | flops 1 | bytes 1 | tf_op jit(solution)/shard_map/attend/pallas_call | solution.py:315
  78.1 0.9 collective-permute-start.14
  79.0 4.0 %attend.11 = bf16[192,1024]{1,0:T(8,128)(2,1)S(1)} custom-call(bf16[208,768]{1,0:T(8,128)(2,1)S(1)} %copy-done.2, bf16[208,768]{1,0:T(8,128)(2,1)S(1)} %collective-permute-done.4.refs_0_.refs_1_, bf16[416,768]{1,0:T(8,128)(2,1)S(1)} %collective-permute-done.11.refs_1_.refs_2_.refs_3_, bf16[416,768]{1,0:T(8,128)(2,1)S(1)} %collective-permute-done.11.refs_1_.refs_2_.refs_3_, ...), custom_call_target="tpu_custom_call" | custom-call | flops 1 | bytes 1 | tf_op jit(solution)/shard_map/attend/pallas_call | solution.py:315
  83.0 4.0 %attend.12 = bf16[192,1024]{1,0:T(8,128)(2,1)S(1)} custom-call(bf16[208,768]{1,0:T(8,128)(2,1)S(1)} %copy-done.2, bf16[208,768]{1,0:T(8,128)(2,1)S(1)} %collective-permute-done.4.refs_0_.refs_1_, bf16[416,768]{1,0:T(8,128)(2,1)S(1)} %collective-permute-done.11.refs_1_.refs_2_.refs_3_, bf16[416,768]{1,0:T(8,128)(2,1)S(1)} %collective-permute-done.11.refs_1_.refs_2_.refs_3_, ...), custom_call_target="tpu_custom_call" | custom-call | flops 1 | bytes 1 | tf_op jit(solution)/shard_map/attend/pallas_call | solution.py:315
  87.0 3.2 %collective-permute-done.14.refs_3_ = bf16[96,1024]{1,0:T(8,128)(2,1)S(1)} collective-permute-done((bf16[96,1024]{1,0:T(8,128)(2,1)S(1)}, bf16[96,1024]{1,0:T(8,128)(2,1)S(1)}, u32[]{:S(2)}, u32[]{:S(2)}) %collective-permute-start.14) | collective-permute-done | bytes 196640 | tf_op jit(solution)/shard_map/ppermute | solution.py:36
  91.3 1.5 %collective-permute-start.18 = (bf16[192,1024]{1,0:T(8,128)(2,1)S(1)}, bf16[192,1024]{1,0:T(8,128)(2,1)S(1)}, u32[]{:S(2)}, u32[]{:S(2)}) collective-permute-start(bf16[192,1024]{1,0:T(8,128)(2,1)S(1)} %attend.12), channel_id=1, source_target_pairs={{0,16},{16,0},{1,17},{17,1},{2,18},{18,2},{3,19},{19,3},{4,20},{20... | collective-permute-start | bytes 1179656 | tf_op jit(solution)/shard_map/ppermute | solution.py:36
  92.8 0.8 collective-permute-done.17.refs_4_.refs_5_.refs_6_.refs_7_
  93.6 4.3 %attend.13.refs_6_ = bf16[192,1024]{1,0:T(8,128)(2,1)S(1)} custom-call(bf16[208,768]{1,0:T(8,128)(2,1)S(1)} %unfold.1.refs_1_.refs_2_.refs_0_, bf16[208,768]{1,0:T(8,128)(2,1)S(1)} %collective-permute-done.9.refs_0_.refs_1_, bf16[416,768]{1,0:T(8,128)(2,1)S(1)} %collective-permute-done.16.refs_1_.refs_2_.refs_3_, ...), custom_call_target="tpu_custom_call" | custom-call | flops 1 | bytes 1 | tf_op jit(solution)/shard_map/attend/pallas_call | solution.py:315
  97.9 4.3 %attend.14.refs_7_ = bf16[192,1024]{1,0:T(8,128)(2,1)S(1)} custom-call(bf16[208,768]{1,0:T(8,128)(2,1)S(1)} %unfold.1.refs_1_.refs_2_.refs_0_, bf16[208,768]{1,0:T(8,128)(2,1)S(1)} %collective-permute-done.9.refs_0_.refs_1_, bf16[416,768]{1,0:T(8,128)(2,1)S(1)} %collective-permute-done.16.refs_1_.refs_2_.refs_3_, ...), custom_call_target="tpu_custom_call" | custom-call | flops 1 | bytes 1 | tf_op jit(solution)/shard_map/attend/pallas_call | solution.py:315
  102.3 4.6 %collective-permute-done.15 = bf16[288,1024]{1,0:T(8,128)(2,1)S(1)} collective-permute-done((bf16[288,1024]{1,0:T(8,128)(2,1)S(1)}, bf16[288,1024]{1,0:T(8,128)(2,1)S(1)}, u32[]{:S(2)}, u32[]{:S(2)}) %collective-permute-start.15) | collective-permute-done | bytes 589856 | tf_op jit(solution)/shard_map/ppermute | solution.py:36
  106.9 4.3 %attend.15 = bf16[192,1024]{1,0:T(8,128)(2,1)S(1)} custom-call(bf16[208,768]{1,0:T(8,128)(2,1)S(1)} %unfold.1.refs_1_.refs_2_.refs_0_, bf16[208,768]{1,0:T(8,128)(2,1)S(1)} %collective-permute-done.9.refs_0_.refs_1_, bf16[416,768]{1,0:T(8,128)(2,1)S(1)} %collective-permute-done.16.refs_1_.refs_2_.refs_3_, ...), custom_call_target="tpu_custom_call" | custom-call | flops 1 | bytes 1 | tf_op jit(solution)/shard_map/attend/pallas_call | solution.py:315
  111.3 1.5 %assemble.1 = bf16[192,8192]{1,0:T(8,128)(2,1)} custom-call(bf16[144,1024]{1,0:T(8,128)(2,1)S(1)} %collective-permute-done.7.refs_0_, bf16[48,1024]{1,0:T(8,128)(2,1)S(1)} %slice.34.refs_1_, bf16[192,1024]{1,0:T(8,128)(2,1)S(1)} %slice.35.refs_2_, bf16[96,1024]{1,0:T(8,128)(2,1)S(1)} %collective-permute-done.14.refs_3_, bf16[96,1024]{1,0:T(8,128)(2,1)S(1)} %slice.30.refs_4_, ...), custom_call_target="tpu_custom_call" | custom-call | flops 1 | bytes 1 | tf_op jit(solution)/shard_map/assemble/pallas_call | solution.py:357
  112.7 0.8 constant_dynamic-update-slice_fusion
  113.5 1.4 %collective-permute-done.18 = bf16[192,1024]{1,0:T(8,128)(2,1)S(1)} collective-permute-done((bf16[192,1024]{1,0:T(8,128)(2,1)S(1)}, bf16[192,1024]{1,0:T(8,128)(2,1)S(1)}, u32[]{:S(2)}, u32[]{:S(2)}) %collective-permute-start.18) | collective-permute-done | bytes 393248 | tf_op jit(solution)/shard_map/ppermute | solution.py:36
  114.9 0.8 bitcast_dynamic-update-slice_fusion
  (43 shorter events, 4.5 us)
Async XLA Ops:
  2.4 18.2 %collective-permute-start.2 = (bf16[352,1024]{1,0:T(8,128)(2,1)}, bf16[352,1024]{1,0:T(8,128)(2,1)S(1)}, u32[]{:S(2)}, u32[]{:S(2)}) collective-permute-start(bf16[352,1024]{1,0:T(8,128)(2,1)} %get-tuple-element.43), channel_id=1, source_target_pairs={{0,16},{16,0},{1,17},{17,1},{2,18},{18,2},{3,19},{19,3},{4,20},{20... | collective-permute-start | bytes 2162696 | tf_op jit(solution)/shard_map/ppermute | solution.py:36
  3.0 14.8 %collective-permute-start = (bf16[208,512]{1,0:T(8,128)(2,1)}, bf16[208,512]{1,0:T(8,128)(2,1)S(1)}, u32[]{:S(2)}, u32[]{:S(2)}) collective-permute-start(bf16[208,512]{1,0:T(8,128)(2,1)} %get-tuple-element.49.refs_1_.refs_2_.refs_0_), channel_id=1, source_target_pairs={{0,4},{1,5},{2,6},{3,7},{4,8},{5,9},{6,10},{7,11},{8,12},{9,13},{1... | collective-permute-start | bytes 638984 | tf_op jit(solution)/shard_map/ppermute | solution.py:44
  6.5 11.4 %collective-permute-start.1 = (bf16[208,512]{1,0:T(8,128)(2,1)}, bf16[208,512]{1,0:T(8,128)(2,1)S(1)}, u32[]{:S(2)}, u32[]{:S(2)}) collective-permute-start(bf16[208,512]{1,0:T(8,128)(2,1)} %get-tuple-element.49.refs_1_.refs_2_.refs_0_), channel_id=1, source_target_pairs={{0,8},{1,9},{2,10},{3,11},{4,12},{5,13},{6,14},{7,15},{8,0},{9,1},... | collective-permute-start | bytes 638984 | tf_op jit(solution)/shard_map/ppermute | solution.py:44
  6.9 14.2 %copy-start.3 = (bf16[208,512]{1,0:T(8,128)(2,1)S(1)}, bf16[208,512]{1,0:T(8,128)(2,1)}, u32[]{:S(2)}) copy-start(bf16[208,512]{1,0:T(8,128)(2,1)} %get-tuple-element.49.refs_1_.refs_2_.refs_0_) | copy-start | bytes 638980
  6.9 15.8 %copy-start.2 = (bf16[208,768]{1,0:T(8,128)(2,1)S(1)}, bf16[208,768]{1,0:T(8,128)(2,1)}, u32[]{:S(2)}) copy-start(bf16[208,768]{1,0:T(8,128)(2,1)} %get-tuple-element.62.refs_1_.refs_2_.refs_0_) | copy-start | bytes 958468
  6.9 43.5 %copy-start.1 = (bf16[1,192,8192]{2,1,0:T(8,128)(2,1)S(1)}, bf16[1,192,8192]{2,1,0:T(8,128)(2,1)}, u32[]{:S(2)}) copy-start(bf16[1,192,8192]{2,1,0:T(8,128)(2,1)} %param.5) | copy-start | bytes 9437188
  9.8 40.6 %copy-start = (bf16[1,192,8192]{2,1,0:T(8,128)(2,1)S(1)}, bf16[1,192,8192]{2,1,0:T(8,128)(2,1)}, u32[]{:S(2)}) copy-start(bf16[1,192,8192]{2,1,0:T(8,128)(2,1)} %param.6) | copy-start | bytes 9437188
  20.5 50.2 %collective-permute-start.12 = (bf16[960,1024]{1,0:T(8,128)(2,1)}, bf16[960,1024]{1,0:T(8,128)(2,1)S(1)}, u32[]{:S(2)}, u32[]{:S(2)}) collective-permute-start(bf16[960,1024]{1,0:T(8,128)(2,1)} %pack_wide.1), channel_id=1, source_target_pairs={{0,16},{16,0},{1,17},{17,1},{2,18},{18,2},{3,19},{19,3},{4,20},{20... | collective-permute-start | bytes 5898248 | tf_op jit(solution)/shard_map/ppermute | solution.py:36
  21.1 20.8 %collective-permute-start.3 = (bf16[416,512]{1,0:T(8,128)(2,1)S(1)}, bf16[416,512]{1,0:T(8,128)(2,1)S(1)}, u32[]{:S(2)}, u32[]{:S(2)}) collective-permute-start(bf16[416,512]{1,0:T(8,128)(2,1)S(1)} %join.6), channel_id=1, source_target_pairs={{0,2},{1,3},{2,0},{3,1},{4,6},{5,7},{6,4},{7,5},{8,10},{9,11},{10,... | collective-permute-start | bytes 1277960 | tf_op jit(solution)/shard_map/ppermute | solution.py:36
  22.7 19.2 %collective-permute-start.4 = (bf16[208,768]{1,0:T(8,128)(2,1)S(1)}, bf16[208,768]{1,0:T(8,128)(2,1)S(1)}, u32[]{:S(2)}, u32[]{:S(2)}) collective-permute-start(bf16[208,768]{1,0:T(8,128)(2,1)S(1)} %copy-done.2), channel_id=1, source_target_pairs={{0,4},{1,5},{2,6},{3,7},{4,8},{5,9},{6,10},{7,11},{8,12},{9,13},{1... | collective-permute-start | bytes 958472 | tf_op jit(solution)/shard_map/ppermute | solution.py:44
  27.4 14.5 %collective-permute-start.5 = (bf16[208,768]{1,0:T(8,128)(2,1)S(1)}, bf16[208,768]{1,0:T(8,128)(2,1)S(1)}, u32[]{:S(2)}, u32[]{:S(2)}) collective-permute-start(bf16[208,768]{1,0:T(8,128)(2,1)S(1)} %copy-done.2), channel_id=1, source_target_pairs={{0,8},{1,9},{2,10},{3,11},{4,12},{5,13},{6,14},{7,15},{8,0},{9,1},... | collective-permute-start | bytes 958472 | tf_op jit(solution)/shard_map/ppermute | solution.py:44
  42.0 8.4 %collective-permute-start.6 = (bf16[832,512]{1,0:T(8,128)(2,1)S(1)}, bf16[832,512]{1,0:T(8,128)(2,1)S(1)}, u32[]{:S(2)}, u32[]{:S(2)}) collective-permute-start(bf16[832,512]{1,0:T(8,128)(2,1)S(1)} %join.7), channel_id=1, source_target_pairs={{0,1},{1,0},{2,3},{3,2},{4,5},{5,4},{6,7},{7,6},{8,9},{9,8},{10,11... | collective-permute-start | bytes 2555912 | tf_op jit(solution)/shard_map/ppermute | solution.py:36
  42.1 25.0 %collective-permute-start.11 = (bf16[416,768]{1,0:T(8,128)(2,1)S(1)}, bf16[416,768]{1,0:T(8,128)(2,1)S(1)}, u32[]{:S(2)}, u32[]{:S(2)}) collective-permute-start(bf16[416,768]{1,0:T(8,128)(2,1)S(1)} %join.8), channel_id=1, source_target_pairs={{0,2},{1,3},{2,0},{3,1},{4,6},{5,7},{6,4},{7,5},{8,10},{9,11},{10,... | collective-permute-start | bytes 1916936 | tf_op jit(solution)/shard_map/ppermute | solution.py:36
  42.7 17.3 %collective-permute-start.10 = (bf16[208,768]{1,0:T(8,128)(2,1)S(1)}, bf16[208,768]{1,0:T(8,128)(2,1)S(1)}, u32[]{:S(2)}, u32[]{:S(2)}) collective-permute-start(bf16[208,768]{1,0:T(8,128)(2,1)S(1)} %unfold.1.refs_1_.refs_2_.refs_0_), channel_id=1, source_target_pairs={{0,8},{1,9},{2,10},{3,11},{4,12},{5,13},{6,14},{7,15},{8,0},{9,1},... | collective-permute-start | bytes 958472 | tf_op jit(solution)/shard_map/ppermute | solution.py:44
  43.6 23.4 %collective-permute-start.9 = (bf16[208,768]{1,0:T(8,128)(2,1)S(1)}, bf16[208,768]{1,0:T(8,128)(2,1)S(1)}, u32[]{:S(2)}, u32[]{:S(2)}) collective-permute-start(bf16[208,768]{1,0:T(8,128)(2,1)S(1)} %unfold.1.refs_1_.refs_2_.refs_0_), channel_id=1, source_target_pairs={{0,4},{1,5},{2,6},{3,7},{4,8},{5,9},{6,10},{7,11},{8,12},{9,13},{1... | collective-permute-start | bytes 958472 | tf_op jit(solution)/shard_map/ppermute | solution.py:44
  54.5 16.3 %collective-permute-start.7 = (bf16[144,1024]{1,0:T(8,128)(2,1)S(1)}, bf16[144,1024]{1,0:T(8,128)(2,1)S(1)}, u32[]{:S(2)}, u32[]{:S(2)}) collective-permute-start(bf16[144,1024]{1,0:T(8,128)(2,1)S(1)} %slice.32), channel_id=1, source_target_pairs={{0,16},{16,0},{1,17},{17,1},{2,18},{18,2},{3,19},{19,3},{4,20},{20... | collective-permute-start | bytes 884744 | tf_op jit(solution)/shard_map/ppermute | solution.py:36
  70.9 3.1 %collective-permute-start.13 = (bf16[832,768]{1,0:T(8,128)(2,1)S(1)}, bf16[832,768]{1,0:T(8,128)(2,1)S(1)}, u32[]{:S(2)}, u32[]{:S(2)}) collective-permute-start(bf16[832,768]{1,0:T(8,128)(2,1)S(1)} %join.9), channel_id=1, source_target_pairs={{0,1},{1,0},{2,3},{3,2},{4,5},{5,4},{6,7},{7,6},{8,9},{9,8},{10,11... | collective-permute-start | bytes 3833864 | tf_op jit(solution)/shard_map/ppermute | solution.py:36
  71.0 19.2 %collective-permute-start.16 = (bf16[416,768]{1,0:T(8,128)(2,1)S(1)}, bf16[416,768]{1,0:T(8,128)(2,1)S(1)}, u32[]{:S(2)}, u32[]{:S(2)}) collective-permute-start(bf16[416,768]{1,0:T(8,128)(2,1)S(1)} %join.10), channel_id=1, source_target_pairs={{0,2},{1,3},{2,0},{3,1},{4,6},{5,7},{6,4},{7,5},{8,10},{9,11},{10,... | collective-permute-start | bytes 1916936 | tf_op jit(solution)/shard_map/ppermute | solution.py:36
  72.6 14.4 %collective-permute-start.8 = (bf16[240,1024]{1,0:T(8,128)(2,1)S(1)}, bf16[240,1024]{1,0:T(8,128)(2,1)S(1)}, u32[]{:S(2)}, u32[]{:S(2)}) collective-permute-start(bf16[240,1024]{1,0:T(8,128)(2,1)S(1)} %pad_maximum_fusion.1), channel_id=1, source_target_pairs={{0,16},{16,0},{1,17},{17,1},{2,18},{18,2},{3,19},{19,3},{4,20},{20... | collective-permute-start | bytes 1474568 | tf_op jit(solution)/shard_map/ppermute | solution.py:36
  78.1 12.1 %collective-permute-start.14 = (bf16[96,1024]{1,0:T(8,128)(2,1)S(1)}, bf16[96,1024]{1,0:T(8,128)(2,1)S(1)}, u32[]{:S(2)}, u32[]{:S(2)}) collective-permute-start(bf16[96,1024]{1,0:T(8,128)(2,1)S(1)} %get-tuple-element.78), channel_id=1, source_target_pairs={{0,16},{16,0},{1,17},{17,1},{2,18},{18,2},{3,19},{19,3},{4,20},{20... | collective-permute-start | bytes 589832 | tf_op jit(solution)/shard_map/ppermute | solution.py:36
  90.6 3.1 %collective-permute-start.17 = (bf16[832,768]{1,0:T(8,128)(2,1)S(1)}, bf16[832,768]{1,0:T(8,128)(2,1)S(1)}, u32[]{:S(2)}, u32[]{:S(2)}) collective-permute-start(bf16[832,768]{1,0:T(8,128)(2,1)S(1)} %join.11), channel_id=1, source_target_pairs={{0,1},{1,0},{2,3},{3,2},{4,5},{5,4},{6,7},{7,6},{8,9},{9,8},{10,11... | collective-permute-start | bytes 3833864 | tf_op jit(solution)/shard_map/ppermute | solution.py:36
  90.7 16.2 %collective-permute-start.15 = (bf16[288,1024]{1,0:T(8,128)(2,1)S(1)}, bf16[288,1024]{1,0:T(8,128)(2,1)S(1)}, u32[]{:S(2)}, u32[]{:S(2)}) collective-permute-start(bf16[288,1024]{1,0:T(8,128)(2,1)S(1)} %pad_maximum_fusion), channel_id=1, source_target_pairs={{0,16},{16,0},{1,17},{17,1},{2,18},{18,2},{3,19},{19,3},{4,20},{20... | collective-permute-start | bytes 1769480 | tf_op jit(solution)/shard_map/ppermute | solution.py:36
  91.3 23.6 %collective-permute-start.18 = (bf16[192,1024]{1,0:T(8,128)(2,1)S(1)}, bf16[192,1024]{1,0:T(8,128)(2,1)S(1)}, u32[]{:S(2)}, u32[]{:S(2)}) collective-permute-start(bf16[192,1024]{1,0:T(8,128)(2,1)S(1)} %attend.12), channel_id=1, source_target_pairs={{0,16},{16,0},{1,17},{17,1},{2,18},{18,2},{3,19},{19,3},{4,20},{20... | collective-permute-start | bytes 1179656 | tf_op jit(solution)/shard_map/ppermute | solution.py:36

commit v4 on v3

--- a/solution.py
+++ b/solution.py
@@ -113,7 +113,7 @@
     ]
 
 
-def pack_first_kernel(chunks, passed, query_head, queries, keys_in, values_in, seg_in, *refs):
+def pack_first_kernel(chunks, passed, queries, stream, keys_in, values_in, seg_in, *refs):
     *blocks, out, block, keys, values, seg, sems = refs
     tokens = queries.shape[0]
     copies = [
@@ -123,7 +123,8 @@
                 (keys_in, keys),
                 (values_in, values),
                 (seg_in, seg),
-                (queries.at[:, pl.ds(query_head * WIDTH, WIDTH)], out.at[pl.ds(0, tokens)]),
+                (queries.at[:, pl.ds(passed[0] * WIDTH, WIDTH)], out.at[pl.ds(0, tokens)]),
+                (stream.at[:, pl.ds(passed[0] * WIDTH, WIDTH)], out.at[pl.ds(tokens, tokens)]),
             )
         )
     ]
@@ -135,21 +136,23 @@
         fill_block(target, tokens, chunk, keys, values, seg)
     fill_block(block, tokens, passed, keys, values, seg)
     for row, column, to_row, to_column in fold_places(block.shape[0], passed[1]):
-        out[tokens + to_row : tokens + to_row + SEG_ROWS, to_column : to_column + PAIR] = block[
+        to_row += 2 * tokens
+        out[to_row : to_row + SEG_ROWS, to_column : to_column + PAIR] = block[
             row : row + SEG_ROWS, column : column + PAIR
         ]
-    copies[3].wait()
-
-
-def pack_first(queries, keys, values, segments, chunks, passed):
+    for copy in copies[3:]:
+        copy.wait()
+
+
+def pack_first(queries, stream, keys, values, segments, chunks, passed):
     tokens = queries.shape[0]
     block = lambda chunk: (tokens + SEG_ROWS, chunk[1] * PAIR)
     folded = max(place[2] for place in fold_places(tokens + SEG_ROWS, passed[1])) + SEG_ROWS
-    shapes = [block(chunk) for chunk in chunks] + [(tokens + folded, WIDTH)]
+    shapes = [block(chunk) for chunk in chunks] + [(2 * tokens + folded, WIDTH)]
     vmem = pl.BlockSpec(memory_space=pltpu.VMEM)
     return pl.pallas_call(
-        functools.partial(pack_first_kernel, chunks, passed, passed[0]),
-        in_specs=[pl.BlockSpec(memory_space=pltpu.HBM)] * 4,
+        functools.partial(pack_first_kernel, chunks, passed),
+        in_specs=[pl.BlockSpec(memory_space=pltpu.HBM)] * 5,
         out_specs=[vmem] * len(shapes),
         out_shape=[jax.ShapeDtypeStruct(shape, jnp.bfloat16) for shape in shapes],
         scratch_shapes=[
@@ -157,12 +160,12 @@
             pltpu.VMEM(keys.shape, jnp.bfloat16),
             pltpu.VMEM(values.shape, jnp.bfloat16),
             pltpu.VMEM(segments.shape, segments.dtype),
-            pltpu.SemaphoreType.DMA((4,)),
+            pltpu.SemaphoreType.DMA((5,)),
         ],
         cost_estimate=LIGHT,
         compiler_params=pltpu.CompilerParams(vmem_limit_bytes=56 * 2**20),
         name="pack_first",
-    )(queries, keys, values, segments)
+    )(queries, stream, keys, values, segments)
 
 
 def pack_wide_kernel(parts, queries, stream, out, sems):
@@ -373,64 +376,68 @@
     segments = segments.reshape(1, -1)
     tokens = queries.shape[0]
     relay = lambda value: exchange(value, "section", 1)
-    def own(full, head):
-        block, one, mates, core, first = full
-        at = [(part, head - first) for part in (block, one, mates, core)]
+    def own(full, n, core, at, head):
+        at = [(part, n) for part in full] + [(core, at)]
         return attend(at, queries, stream, head * WIDTH, 0, 0, LIGHT)
 
-    def passed(full, n, q, q_row, s, s_row):
-        return attend([(part, n) for part in full], q, s, 0, q_row, s_row, LIGHT)
-
-    chunk_a, chunk_b, chunk_f = (0, 2), (2, 3), (5, 3)
-    cut, half = 3 * tokens // 4, tokens // 2
+    def passed(full, n, core, at, wide, row):
+        at = [(part, n) for part in full] + [(core, at)]
+        return attend(at, wide, wide, 0, row, row + tokens, LIGHT)
+
+    chunk_a, chunk_b, chunk_f = (0, 3), (3, 2), (5, 3)
+    cut = 3 * tokens // 4
     whole = lambda chunk: (0, chunk[1])
-    block_a, block_b, wide_a = pack_first(queries, keys, values, segments, (chunk_a, chunk_b), chunk_f)
+    block_a, block_b, wide_a = pack_first(
+        queries, stream, keys, values, segments, (chunk_a, chunk_b), chunk_f
+    )
     wide_a = relay(wide_a)
     behind_a = gather_behind(block_a)
-    wide_b = pack_wide(gate(queries, block_a), stream, ((1, 5), (0, 6), (1, 6), (0, 7), (1, 7)))
+    wide_b = pack_wide(gate(queries, block_a), stream, ((0, 6), (1, 6), (0, 7), (1, 7)))
     wide_b, behind_a = gate((wide_b, behind_a), wide_a, wide_b)
     wide_b = relay(wide_b)
-    block_f = unfold(wide_a, tokens, tokens, chunk_f)
+    block_f = unfold(wide_a, 2 * tokens, tokens, chunk_f)
     behind_b = gather_behind(gate(block_b, behind_a))
     y_a = over_y(block_a, behind_a, whole(chunk_a))
     behind_f = gather_behind(gate(block_f, behind_b, y_a))
     y_b = over_y(gate(block_b, y_a), behind_b, whole(chunk_b))
-    core_a = over_core(gate(block_a, behind_b), behind_a, y_a, whole(chunk_a))
-    full_a = (block_a, behind_a[0], y_a, core_a)
-    piece_0 = own(full_a + (0,), 0)
+    block_a = gate(block_a, behind_b)
+    core_a = over_core(block_a, behind_a, y_a, (0, 2))
+    core_2 = over_core(block_a, behind_a, y_a, (2, 1))
+    full_a = (block_a, behind_a[0], y_a)
+    piece_0 = own(full_a, 0, core_a, 0, 0)
     recv_0 = relay(piece_0[:cut])
-    piece_1 = own(gate(full_a, piece_0) + (0,), 1)
-    recv_1 = relay(jnp.concatenate([piece_0[cut:], piece_1]))
-    block_b, block_f = gate((block_b, block_f), behind_f, y_b, recv_0, piece_1, wide_b)
-    core_b = over_core(block_b, behind_b, y_b, whole(chunk_b))
+    piece_1 = own(gate(full_a, piece_0), 1, core_a, 1, 1)
+    piece_2 = own(gate(full_a, piece_1), 2, core_2, 0, 2)
+    recv_1 = relay(jnp.concatenate([piece_0[cut:], piece_1, piece_2[:cut]]))
+    block_b, block_f = gate((block_b, block_f), behind_f, y_b, recv_0, piece_2, wide_b)
+    core_b = [over_core(block_b, behind_b, y_b, (n, 1)) for n in range(chunk_b[1])]
     y_f = over_y(block_f, behind_f, whole(chunk_f))
-    full_b = (block_b, behind_b[0], y_b, core_b)
-    piece_2 = own(full_b + (2,), 2)
-    recv_2 = relay(piece_2[:half])
-    piece_3 = own(gate(full_b, piece_2) + (2,), 3)
-    recv_3 = relay(jnp.concatenate([piece_2[half:], piece_3]))
-    piece_4 = own(gate(full_b, piece_3) + (2,), 4)
-    recv_4 = relay(piece_4)
-    core_f = over_core(gate(block_f, piece_4, recv_1, recv_2), behind_f, y_f, whole(chunk_f))
-    full_f = (block_f, behind_f[0], y_f, core_f)
-    piece_5 = passed(full_f, 0, wide_a, 0, wide_b, 0)
-    piece_6 = passed(gate(full_f, piece_5), 1, wide_b, tokens, wide_b, 2 * tokens)
-    piece_7 = passed(gate(full_f, piece_6), 2, wide_b, 3 * tokens, wide_b, 4 * tokens)
-    recv_3 = gate(recv_3, piece_6)
+    full_b = (block_b, behind_b[0], y_b)
+    piece_3 = own(full_b, 0, core_b[0], 0, 3)
+    piece_4 = own(gate(full_b, piece_3), 1, core_b[1], 0, 4)
+    recv_2 = relay(jnp.concatenate([piece_2[cut:], piece_3, piece_4]))
+    block_f = gate(block_f, piece_4, recv_1)
+    core_f = over_core(block_f, behind_f, y_f, (0, 2))
+    core_7 = over_core(block_f, behind_f, y_f, (2, 1))
+    full_f = (block_f, behind_f[0], y_f)
+    piece_5 = passed(full_f, 0, core_f, 0, wide_a, 0)
+    piece_6 = passed(gate(full_f, piece_5), 1, core_f, 1, wide_b, 0)
+    piece_7 = passed(gate(full_f, piece_6), 2, core_7, 0, wide_b, 2 * tokens)
+    rest = tokens - cut
     pieces = [
         (recv_0, (0, 0)),
-        (recv_1[: tokens - cut], (cut, 0)),
-        (recv_1[tokens - cut :], (0, WIDTH)),
-        (recv_2, (0, 2 * WIDTH)),
-        (recv_3[: tokens - half], (half, 2 * WIDTH)),
-        (recv_3[tokens - half :], (0, 3 * WIDTH)),
+        (recv_1[:rest], (cut, 0)),
+        (recv_1[rest : rest + tokens], (0, WIDTH)),
+        (recv_1[rest + tokens :], (0, 2 * WIDTH)),
         (piece_5, (0, 5 * WIDTH)),
         (piece_6, (0, 6 * WIDTH)),
+        (piece_7, (0, 7 * WIDTH)),
     ]
     out = assemble(None, pieces, queries.shape, LIGHT)
-    out = lax.dynamic_update_slice(out, piece_7, (0, 7 * WIDTH))
-    recv_4 = gate(recv_4, out)
-    return lax.dynamic_update_slice(out, recv_4, (0, 4 * WIDTH))[None]
+    recv_2 = gate(recv_2, out)
+    out = lax.dynamic_update_slice(out, recv_2[:rest], (cut, 2 * WIDTH))
+    last = jnp.concatenate([recv_2[rest : rest + tokens], recv_2[rest + tokens :]], axis=1)
+    return lax.dynamic_update_slice(out, last, (0, 3 * WIDTH))[None]
 
 
 def solution(mesh):

time: 117 us -> 111 us (0.949)
  starting transfers between devices: 26.5 us -> 22.3 us
  waiting for transfers between devices: 46.5 us -> 45 us
    ppermute x6, waiting for transfers between devices: 29.4 us -> 23.4 us  [from_groups_behind(): return lax.ppermute(value, 'ctx', pairs)]
    ppermute x13 -> x14, waiting for transfers between devices: 17.1 us -> 21.6 us  [exchange(): lax.ppermute(value, axis, [(i, i ^ bit) for i in range(lax.axis_size(axis...]
    ppermute x6, starting transfers between devices: 16.3 us -> 13.8 us  [from_groups_behind(): return lax.ppermute(value, 'ctx', pairs)]
    ppermute x13 -> x14, starting transfers between devices: 10.2 us -> 8.49 us  [exchange(): lax.ppermute(value, axis, [(i, i ^ bit) for i in range(lax.axis_size(axis...]
  transfers between devices with their start and end apart: 19 -> 20, of which waited for: 10 -> 9; matrix products, arithmetic and copies ran while one was open for 1% -> 0% of each run, Pallas kernels for 33% -> 34%
where the time goes in v4:
time: 111 us; the launch traced here: 110 us
  waiting for transfers between devices  45 us (41%)
  Pallas kernels  40.3 us (36%)
  starting transfers between devices  22.3 us (20%)
    pallas_call x8, Pallas kernels, attend(): pl.pallas_call(functools.partial(attend_kernel, tokens, column, query_row...  32.9 us
    ppermute x6, waiting for transfers between devices, from_groups_behind(): return lax.ppermute(value, 'ctx', pairs)  23.4 us
    ppermute x14, waiting for transfers between devices, exchange(): lax.ppermute(value, axis, [(i, i ^ bit) for i in range(lax.axis_size(axis...  21.6 us
    ppermute x6, starting transfers between devices, from_groups_behind(): return lax.ppermute(value, 'ctx', pairs)  13.8 us
    ppermute x14, starting transfers between devices, exchange(): lax.ppermute(value, axis, [(i, i ^ bit) for i in range(lax.axis_size(axis...  8.49 us
    pallas_call x1, Pallas kernels, pack_first(): pl.pallas_call(functools.partial(pack_first_kernel, chunks, passed), in_s...  2.62 us
    pallas_call x1, Pallas kernels, pack_wide(): pl.pallas_call(functools.partial(pack_wide_kernel, parts), in_specs=[pl.B...  2.53 us
  transfers between devices with their start and end apart: 20, of which 9 were waited for; matrix products, arithmetic and copies ran while one was open for 0% of the time, Pallas kernels for 34%

profile of v4, /device:TPU:18, one launch (start us, length us, event | category | flops | bytes accessed | tf_op | source)
XLA Modules:
  0.0 109.8 jit_solution(8914246068632312569)
XLA Ops:
  0.0 2.6 %pack_first.1 = (bf16[208,768]{1,0:T(8,128)(2,1)}, bf16[208,512]{1,0:T(8,128)(2,1)}, bf16[544,1024]{1,0:T(8,128)(2,1)}) custom-call(bf16[192,8192]{1,0:T(8,128)(2,1)} %bitcast.11, bf16[192,8192]{1,0:T(8,128)(2,1)} %bitcast.18, bf16[192,1024]{1,0:T(8,128)(2,1)} %bitcast.26, bf16[192,1024]{1,0:T(8,128)(2,1)} %bitcast.27, s32[1,192]{1,0:T(1,128)} %seg_in.1), custom_call_target="tpu_custom_call" | custom-call | flops 1 | bytes 1 | tf_op jit(solution)/shard_map/pack_first/pallas_call | solution.py:153
  2.6 0.6 collective-permute-start.2
  3.2 3.6 %collective-permute-start = (bf16[208,768]{1,0:T(8,128)(2,1)}, bf16[208,768]{1,0:T(8,128)(2,1)S(1)}, u32[]{:S(2)}, u32[]{:S(2)}) collective-permute-start(bf16[208,768]{1,0:T(8,128)(2,1)} %get-tuple-element.46.refs_1_.refs_2_.refs_0_), channel_id=1, source_target_pairs={{0,4},{1,5},{2,6},{3,7},{4,8},{5,9},{6,10},{7,11},{8,12},{9,13},{1... | collective-permute-start | bytes 958472 | tf_op jit(solution)/shard_map/ppermute | solution.py:44
  7.3 2.5 %pack_wide.1 = bf16[768,1024]{1,0:T(8,128)(2,1)} custom-call(bf16[192,8192]{1,0:T(8,128)(2,1)} %bitcast.12, bf16[192,8192]{1,0:T(8,128)(2,1)} %bitcast.19), custom_call_target="tpu_custom_call" | custom-call | flops 1 | bytes 1 | tf_op jit(solution)/shard_map/pack_wide/pallas_call | solution.py:188
  9.8 13.0 %collective-permute-done.refs_0_.refs_1_ = bf16[208,768]{1,0:T(8,128)(2,1)S(1)} collective-permute-done((bf16[208,768]{1,0:T(8,128)(2,1)}, bf16[208,768]{1,0:T(8,128)(2,1)S(1)}, u32[]{:S(2)}, u32[]{:S(2)}) %collective-permute-start) | collective-permute-done | bytes 319520 | tf_op jit(solution)/shard_map/ppermute | solution.py:44
  22.8 6.4 %collective-permute-done.2.wide.refs_8_.refs_9_ = bf16[544,1024]{1,0:T(8,128)(2,1)S(1)} collective-permute-done((bf16[544,1024]{1,0:T(8,128)(2,1)}, bf16[544,1024]{1,0:T(8,128)(2,1)S(1)}, u32[]{:S(2)}, u32[]{:S(2)}) %collective-permute-start.2) | collective-permute-done | bytes 1114144 | tf_op jit(solution)/shard_map/ppermute | solution.py:36
  29.3 1.6 %collective-permute-start.5 = (bf16[416,768]{1,0:T(8,128)(2,1)S(1)}, bf16[416,768]{1,0:T(8,128)(2,1)S(1)}, u32[]{:S(2)}, u32[]{:S(2)}) collective-permute-start(bf16[416,768]{1,0:T(8,128)(2,1)S(1)} %join.9), channel_id=1, source_target_pairs={{0,2},{1,3},{2,0},{3,1},{4,6},{5,7},{6,4},{7,5},{8,10},{9,11},{10,... | collective-permute-start | bytes 1916936 | tf_op jit(solution)/shard_map/ppermute | solution.py:36
  31.4 3.5 %collective-permute-start.3 = (bf16[208,512]{1,0:T(8,128)(2,1)S(1)}, bf16[208,512]{1,0:T(8,128)(2,1)S(1)}, u32[]{:S(2)}, u32[]{:S(2)}) collective-permute-start(bf16[208,512]{1,0:T(8,128)(2,1)S(1)} %copy-done.3), channel_id=1, source_target_pairs={{0,4},{1,5},{2,6},{3,7},{4,8},{5,9},{6,10},{7,11},{8,12},{9,13},{1... | collective-permute-start | bytes 638984 | tf_op jit(solution)/shard_map/ppermute | solution.py:44
  35.3 10.4 %collective-permute-done.3.refs_0_.refs_1_ = bf16[208,512]{1,0:T(8,128)(2,1)S(1)} collective-permute-done((bf16[208,512]{1,0:T(8,128)(2,1)S(1)}, bf16[208,512]{1,0:T(8,128)(2,1)S(1)}, u32[]{:S(2)}, u32[]{:S(2)}) %collective-permute-start.3) | collective-permute-done | bytes 213024 | tf_op jit(solution)/shard_map/ppermute | solution.py:44
  46.5 5.9 %collective-permute-start.10 = (bf16[208,768]{1,0:T(8,128)(2,1)S(1)}, bf16[208,768]{1,0:T(8,128)(2,1)S(1)}, u32[]{:S(2)}, u32[]{:S(2)}) collective-permute-start(bf16[208,768]{1,0:T(8,128)(2,1)S(1)} %unfold.1.refs_1_.refs_2_.refs_0_), channel_id=1, source_target_pairs={{0,4},{1,5},{2,6},{3,7},{4,8},{5,9},{6,10},{7,11},{8,12},{9,13},{1... | collective-permute-start | bytes 958472 | tf_op jit(solution)/shard_map/ppermute | solution.py:44
  52.4 0.6 collective-permute-start.12
  53.0 4.0 %attend.8 = bf16[192,1024]{1,0:T(8,128)(2,1)S(1)} custom-call(bf16[208,768]{1,0:T(8,128)(2,1)S(1)} %copy-done.2, bf16[208,768]{1,0:T(8,128)(2,1)S(1)} %collective-permute-done.refs_0_.refs_1_, bf16[416,768]{1,0:T(8,128)(2,1)S(1)} %collective-permute-done.5.refs_1_.refs_2_.refs_3_, bf16[416,768]{1,0:T(8,128)(2,1)S(1)} %collective-permute-done.5.refs_1_.refs_2_.refs_3_, ...), custom_call_target="tpu_custom_call" | custom-call | flops 1 | bytes 1 | tf_op jit(solution)/shard_map/attend/pallas_call | solution.py:318
  57.1 1.6 %collective-permute-start.7 = (bf16[144,1024]{1,0:T(8,128)(2,1)S(1)}, bf16[144,1024]{1,0:T(8,128)(2,1)S(1)}, u32[]{:S(2)}, u32[]{:S(2)}) collective-permute-start(bf16[144,1024]{1,0:T(8,128)(2,1)S(1)} %slice.40), channel_id=1, source_target_pairs={{0,16},{16,0},{1,17},{17,1},{2,18},{18,2},{3,19},{19,3},{4,20},{20... | collective-permute-start | bytes 884744 | tf_op jit(solution)/shard_map/ppermute | solution.py:36
  58.6 4.0 %attend.9 = bf16[192,1024]{1,0:T(8,128)(2,1)S(1)} custom-call(bf16[208,768]{1,0:T(8,128)(2,1)S(1)} %copy-done.2, bf16[208,768]{1,0:T(8,128)(2,1)S(1)} %collective-permute-done.refs_0_.refs_1_, bf16[416,768]{1,0:T(8,128)(2,1)S(1)} %collective-permute-done.5.refs_1_.refs_2_.refs_3_, bf16[416,768]{1,0:T(8,128)(2,1)S(1)} %collective-permute-done.5.refs_1_.refs_2_.refs_3_, ...), custom_call_target="tpu_custom_call" | custom-call | flops 1 | bytes 1 | tf_op jit(solution)/shard_map/attend/pallas_call | solution.py:318
  62.6 4.0 %attend.10 = bf16[192,1024]{1,0:T(8,128)(2,1)S(1)} custom-call(bf16[208,768]{1,0:T(8,128)(2,1)S(1)} %copy-done.2, bf16[208,768]{1,0:T(8,128)(2,1)S(1)} %collective-permute-done.refs_0_.refs_1_, bf16[416,768]{1,0:T(8,128)(2,1)S(1)} %collective-permute-done.5.refs_1_.refs_2_.refs_3_, bf16[416,768]{1,0:T(8,128)(2,1)S(1)} %collective-permute-done.5.refs_1_.refs_2_.refs_3_, ...), custom_call_target="tpu_custom_call" | custom-call | flops 1 | bytes 1 | tf_op jit(solution)/shard_map/attend/pallas_call | solution.py:318
  66.8 0.6 collective-permute-start.9
  67.4 1.0 collective-permute-done.13.refs_8_.refs_9_
  68.4 6.3 %collective-permute-done.7.refs_0_ = bf16[144,1024]{1,0:T(8,128)(2,1)S(1)} collective-permute-done((bf16[144,1024]{1,0:T(8,128)(2,1)S(1)}, bf16[144,1024]{1,0:T(8,128)(2,1)S(1)}, u32[]{:S(2)}, u32[]{:S(2)}) %collective-permute-start.7) | collective-permute-done | bytes 294944 | tf_op jit(solution)/shard_map/ppermute | solution.py:36
  74.9 0.6 collective-permute-start.16
  76.2 1.2 %collective-permute-done.14.refs_4_.refs_5_.refs_6_.refs_7_ = bf16[832,256]{1,0:T(8,128)(2,1)S(1)} collective-permute-done((bf16[832,256]{1,0:T(8,128)(2,1)S(1)}, bf16[832,256]{1,0:T(8,128)(2,1)S(1)}, u32[]{:S(2)}, u32[]{:S(2)}) %collective-permute-start.14) | collective-permute-done | bytes 426016 | tf_op jit(solution)/shard_map/ppermute | solution.py:36
  77.4 4.0 %attend.11 = bf16[192,1024]{1,0:T(8,128)(2,1)S(1)} custom-call(bf16[208,512]{1,0:T(8,128)(2,1)S(1)} %copy-done.3, bf16[208,512]{1,0:T(8,128)(2,1)S(1)} %collective-permute-done.3.refs_0_.refs_1_, bf16[416,512]{1,0:T(8,128)(2,1)S(1)} %collective-permute-done.12.refs_1_.refs_2_.refs_3_, bf16[416,512]{1,0:T(8,128)(2,1)S(1)} %collective-permute-done.12.refs_1_.refs_2_.refs_3_, ...), custom_call_target="tpu_custom_call" | custom-call | flops 1 | bytes 1 | tf_op jit(solution)/shard_map/attend/pallas_call | solution.py:318
  81.4 4.0 %attend.12 = bf16[192,1024]{1,0:T(8,128)(2,1)S(1)} custom-call(bf16[208,512]{1,0:T(8,128)(2,1)S(1)} %copy-done.3, bf16[208,512]{1,0:T(8,128)(2,1)S(1)} %collective-permute-done.3.refs_0_.refs_1_, bf16[416,512]{1,0:T(8,128)(2,1)S(1)} %collective-permute-done.12.refs_1_.refs_2_.refs_3_, bf16[416,512]{1,0:T(8,128)(2,1)S(1)} %collective-permute-done.12.refs_1_.refs_2_.refs_3_, ...), custom_call_target="tpu_custom_call" | custom-call | flops 1 | bytes 1 | tf_op jit(solution)/shard_map/attend/pallas_call | solution.py:318
  85.5 0.6 collective-permute-start.19
  86.1 4.1 %collective-permute-done.9 = bf16[384,1024]{1,0:T(8,128)(2,1)S(1)} collective-permute-done((bf16[384,1024]{1,0:T(8,128)(2,1)S(1)}, bf16[384,1024]{1,0:T(8,128)(2,1)S(1)}, u32[]{:S(2)}, u32[]{:S(2)}) %collective-permute-start.9) | collective-permute-done | bytes 786464 | tf_op jit(solution)/shard_map/ppermute | solution.py:36
  91.2 1.5 %collective-permute-done.17.refs_4_.refs_5_.refs_6_.refs_7_ = bf16[832,512]{1,0:T(8,128)(2,1)S(1)} collective-permute-done((bf16[832,512]{1,0:T(8,128)(2,1)S(1)}, bf16[832,512]{1,0:T(8,128)(2,1)S(1)}, u32[]{:S(2)}, u32[]{:S(2)}) %collective-permute-start.17) | collective-permute-done | bytes 852000 | tf_op jit(solution)/shard_map/ppermute | solution.py:36
  92.6 4.3 %attend.13.refs_4_ = bf16[192,1024]{1,0:T(8,128)(2,1)S(1)} custom-call(bf16[208,768]{1,0:T(8,128)(2,1)S(1)} %unfold.1.refs_1_.refs_2_.refs_0_, bf16[208,768]{1,0:T(8,128)(2,1)S(1)} %collective-permute-done.10.refs_0_.refs_1_, bf16[416,768]{1,0:T(8,128)(2,1)S(1)} %collective-permute-done.16.refs_1_.refs_2_.refs_3_, ...), custom_call_target="tpu_custom_call" | custom-call | flops 1 | bytes 1 | tf_op jit(solution)/shard_map/attend/pallas_call | solution.py:318
  97.0 4.3 %attend.14.refs_5_ = bf16[192,1024]{1,0:T(8,128)(2,1)S(1)} custom-call(bf16[208,768]{1,0:T(8,128)(2,1)S(1)} %unfold.1.refs_1_.refs_2_.refs_0_, bf16[208,768]{1,0:T(8,128)(2,1)S(1)} %collective-permute-done.10.refs_0_.refs_1_, bf16[416,768]{1,0:T(8,128)(2,1)S(1)} %collective-permute-done.16.refs_1_.refs_2_.refs_3_, ...), custom_call_target="tpu_custom_call" | custom-call | flops 1 | bytes 1 | tf_op jit(solution)/shard_map/attend/pallas_call | solution.py:318
  101.3 4.3 %attend.15.refs_6_ = bf16[192,1024]{1,0:T(8,128)(2,1)S(1)} custom-call(bf16[208,768]{1,0:T(8,128)(2,1)S(1)} %unfold.1.refs_1_.refs_2_.refs_0_, bf16[208,768]{1,0:T(8,128)(2,1)S(1)} %collective-permute-done.10.refs_0_.refs_1_, bf16[416,768]{1,0:T(8,128)(2,1)S(1)} %collective-permute-done.16.refs_1_.refs_2_.refs_3_, ...), custom_call_target="tpu_custom_call" | custom-call | flops 1 | bytes 1 | tf_op jit(solution)/shard_map/attend/pallas_call | solution.py:318
  105.6 1.4 %assemble.1 = bf16[192,8192]{1,0:T(8,128)(2,1)} custom-call(bf16[144,1024]{1,0:T(8,128)(2,1)S(1)} %collective-permute-done.7.refs_0_, bf16[48,1024]{1,0:T(8,128)(2,1)S(1)} %slice.43.refs_1_, bf16[192,1024]{1,0:T(8,128)(2,1)S(1)} %slice.44.refs_2_, bf16[144,1024]{1,0:T(8,128)(2,1)S(1)} %slice.45.refs_3_, bf16[192,1024]{1,0:T(8,128)(2,1)S(1)} %attend.13.refs_4_, ...), custom_call_target="tpu_custom_call" | custom-call | flops 1 | bytes 1 | tf_op jit(solution)/shard_map/assemble/pallas_call | solution.py:360
  107.1 1.1 %collective-permute-done.19 = bf16[432,1024]{1,0:T(8,128)(2,1)S(1)} collective-permute-done((bf16[432,1024]{1,0:T(8,128)(2,1)S(1)}, bf16[432,1024]{1,0:T(8,128)(2,1)S(1)}, u32[]{:S(2)}, u32[]{:S(2)}) %collective-permute-start.19) | collective-permute-done | bytes 884768 | tf_op jit(solution)/shard_map/ppermute | solution.py:36
  108.2 0.7 bitcast_dynamic-update-slice_fusion
  108.9 0.9 fusion
  (52 shorter events, 4.4 us)
Async XLA Ops:
  2.6 26.6 %collective-permute-start.2 = (bf16[544,1024]{1,0:T(8,128)(2,1)}, bf16[544,1024]{1,0:T(8,128)(2,1)S(1)}, u32[]{:S(2)}, u32[]{:S(2)}) collective-permute-start(bf16[544,1024]{1,0:T(8,128)(2,1)} %get-tuple-element.38), channel_id=1, source_target_pairs={{0,16},{16,0},{1,17},{17,1},{2,18},{18,2},{3,19},{19,3},{4,20},{20... | collective-permute-start | bytes 3342344 | tf_op jit(solution)/shard_map/ppermute | solution.py:36
  3.2 26.0 %copy-start.2 = (bf16[208,768]{1,0:T(8,128)(2,1)S(1)}, bf16[208,768]{1,0:T(8,128)(2,1)}, u32[]{:S(2)}) copy-start(bf16[208,768]{1,0:T(8,128)(2,1)} %get-tuple-element.46.refs_1_.refs_2_.refs_0_) | copy-start | bytes 958468
  3.2 28.2 %copy-start.3 = (bf16[208,512]{1,0:T(8,128)(2,1)S(1)}, bf16[208,512]{1,0:T(8,128)(2,1)}, u32[]{:S(2)}) copy-start(bf16[208,512]{1,0:T(8,128)(2,1)} %get-tuple-element.54.refs_1_.refs_2_.refs_0_) | copy-start | bytes 638980
  3.2 19.5 %collective-permute-start = (bf16[208,768]{1,0:T(8,128)(2,1)}, bf16[208,768]{1,0:T(8,128)(2,1)S(1)}, u32[]{:S(2)}, u32[]{:S(2)}) collective-permute-start(bf16[208,768]{1,0:T(8,128)(2,1)} %get-tuple-element.46.refs_1_.refs_2_.refs_0_), channel_id=1, source_target_pairs={{0,4},{1,5},{2,6},{3,7},{4,8},{5,9},{6,10},{7,11},{8,12},{9,13},{1... | collective-permute-start | bytes 958472 | tf_op jit(solution)/shard_map/ppermute | solution.py:44
  6.8 15.9 %collective-permute-start.1 = (bf16[208,768]{1,0:T(8,128)(2,1)}, bf16[208,768]{1,0:T(8,128)(2,1)S(1)}, u32[]{:S(2)}, u32[]{:S(2)}) collective-permute-start(bf16[208,768]{1,0:T(8,128)(2,1)} %get-tuple-element.46.refs_1_.refs_2_.refs_0_), channel_id=1, source_target_pairs={{0,8},{1,9},{2,10},{3,11},{4,12},{5,13},{6,14},{7,15},{8,0},{9,1},... | collective-permute-start | bytes 958472 | tf_op jit(solution)/shard_map/ppermute | solution.py:44
  29.3 16.4 %collective-permute-start.5 = (bf16[416,768]{1,0:T(8,128)(2,1)S(1)}, bf16[416,768]{1,0:T(8,128)(2,1)S(1)}, u32[]{:S(2)}, u32[]{:S(2)}) collective-permute-start(bf16[416,768]{1,0:T(8,128)(2,1)S(1)} %join.9), channel_id=1, source_target_pairs={{0,2},{1,3},{2,0},{3,1},{4,6},{5,7},{6,4},{7,5},{8,10},{9,11},{10,... | collective-permute-start | bytes 1916936 | tf_op jit(solution)/shard_map/ppermute | solution.py:36
  30.9 37.5 %collective-permute-start.13 = (bf16[768,1024]{1,0:T(8,128)(2,1)}, bf16[768,1024]{1,0:T(8,128)(2,1)S(1)}, u32[]{:S(2)}, u32[]{:S(2)}) collective-permute-start(bf16[768,1024]{1,0:T(8,128)(2,1)} %pack_wide.1), channel_id=1, source_target_pairs={{0,16},{16,0},{1,17},{17,1},{2,18},{18,2},{3,19},{19,3},{4,20},{20... | collective-permute-start | bytes 4718600 | tf_op jit(solution)/shard_map/ppermute | solution.py:36
  31.4 14.3 %collective-permute-start.3 = (bf16[208,512]{1,0:T(8,128)(2,1)S(1)}, bf16[208,512]{1,0:T(8,128)(2,1)S(1)}, u32[]{:S(2)}, u32[]{:S(2)}) collective-permute-start(bf16[208,512]{1,0:T(8,128)(2,1)S(1)} %copy-done.3), channel_id=1, source_target_pairs={{0,4},{1,5},{2,6},{3,7},{4,8},{5,9},{6,10},{7,11},{8,12},{9,13},{1... | collective-permute-start | bytes 638984 | tf_op jit(solution)/shard_map/ppermute | solution.py:44
  34.9 10.8 %collective-permute-start.4 = (bf16[208,512]{1,0:T(8,128)(2,1)S(1)}, bf16[208,512]{1,0:T(8,128)(2,1)S(1)}, u32[]{:S(2)}, u32[]{:S(2)}) collective-permute-start(bf16[208,512]{1,0:T(8,128)(2,1)S(1)} %copy-done.3), channel_id=1, source_target_pairs={{0,8},{1,9},{2,10},{3,11},{4,12},{5,13},{6,14},{7,15},{8,0},{9,1},... | collective-permute-start | bytes 638984 | tf_op jit(solution)/shard_map/ppermute | solution.py:44
  45.7 7.3 %copy-start.1 = (bf16[1,192,8192]{2,1,0:T(8,128)(2,1)S(1)}, bf16[1,192,8192]{2,1,0:T(8,128)(2,1)}, u32[]{:S(2)}) copy-start(bf16[1,192,8192]{2,1,0:T(8,128)(2,1)} %param.5) | copy-start | bytes 9437188
  45.8 7.3 %copy-start = (bf16[1,192,8192]{2,1,0:T(8,128)(2,1)S(1)}, bf16[1,192,8192]{2,1,0:T(8,128)(2,1)}, u32[]{:S(2)}) copy-start(bf16[1,192,8192]{2,1,0:T(8,128)(2,1)} %param.6) | copy-start | bytes 9437188
  45.8 7.2 %collective-permute-start.6 = (bf16[832,512]{1,0:T(8,128)(2,1)S(1)}, bf16[832,512]{1,0:T(8,128)(2,1)S(1)}, u32[]{:S(2)}, u32[]{:S(2)}) collective-permute-start(bf16[832,512]{1,0:T(8,128)(2,1)S(1)} %join.10), channel_id=1, source_target_pairs={{0,1},{1,0},{2,3},{3,2},{4,5},{5,4},{6,7},{7,6},{8,9},{9,8},{10,11... | collective-permute-start | bytes 2555912 | tf_op jit(solution)/shard_map/ppermute | solution.py:36
  45.9 11.2 %collective-permute-start.8 = (bf16[832,256]{1,0:T(8,128)(2,1)S(1)}, bf16[832,256]{1,0:T(8,128)(2,1)S(1)}, u32[]{:S(2)}, u32[]{:S(2)}) collective-permute-start(bf16[832,256]{1,0:T(8,128)(2,1)S(1)} %join.11), channel_id=1, source_target_pairs={{0,1},{1,0},{2,3},{3,2},{4,5},{5,4},{6,7},{7,6},{8,9},{9,8},{10,11... | collective-permute-start | bytes 1277960 | tf_op jit(solution)/shard_map/ppermute | solution.py:36
  46.5 20.3 %collective-permute-start.10 = (bf16[208,768]{1,0:T(8,128)(2,1)S(1)}, bf16[208,768]{1,0:T(8,128)(2,1)S(1)}, u32[]{:S(2)}, u32[]{:S(2)}) collective-permute-start(bf16[208,768]{1,0:T(8,128)(2,1)S(1)} %unfold.1.refs_1_.refs_2_.refs_0_), channel_id=1, source_target_pairs={{0,4},{1,5},{2,6},{3,7},{4,8},{5,9},{6,10},{7,11},{8,12},{9,13},{1... | collective-permute-start | bytes 958472 | tf_op jit(solution)/shard_map/ppermute | solution.py:44
  52.4 14.9 %collective-permute-start.12 = (bf16[416,512]{1,0:T(8,128)(2,1)S(1)}, bf16[416,512]{1,0:T(8,128)(2,1)S(1)}, u32[]{:S(2)}, u32[]{:S(2)}) collective-permute-start(bf16[416,512]{1,0:T(8,128)(2,1)S(1)} %join.12), channel_id=1, source_target_pairs={{0,2},{1,3},{2,0},{3,1},{4,6},{5,7},{6,4},{7,5},{8,10},{9,11},{10,... | collective-permute-start | bytes 1277960 | tf_op jit(solution)/shard_map/ppermute | solution.py:36
  53.0 14.3 %collective-permute-start.11 = (bf16[208,768]{1,0:T(8,128)(2,1)S(1)}, bf16[208,768]{1,0:T(8,128)(2,1)S(1)}, u32[]{:S(2)}, u32[]{:S(2)}) collective-permute-start(bf16[208,768]{1,0:T(8,128)(2,1)S(1)} %unfold.1.refs_1_.refs_2_.refs_0_), channel_id=1, source_target_pairs={{0,8},{1,9},{2,10},{3,11},{4,12},{5,13},{6,14},{7,15},{8,0},{9,1},... | collective-permute-start | bytes 958472 | tf_op jit(solution)/shard_map/ppermute | solution.py:44
  57.1 17.6 %collective-permute-start.7 = (bf16[144,1024]{1,0:T(8,128)(2,1)S(1)}, bf16[144,1024]{1,0:T(8,128)(2,1)S(1)}, u32[]{:S(2)}, u32[]{:S(2)}) collective-permute-start(bf16[144,1024]{1,0:T(8,128)(2,1)S(1)} %slice.40), channel_id=1, source_target_pairs={{0,16},{16,0},{1,17},{17,1},{2,18},{18,2},{3,19},{19,3},{4,20},{20... | collective-permute-start | bytes 884744 | tf_op jit(solution)/shard_map/ppermute | solution.py:36
  66.6 9.6 %copy-start.4 = (bf16[192,1024]{1,0:T(8,128)(2,1)}, bf16[192,1024]{1,0:T(8,128)(2,1)S(1)}, u32[]{:S(2)}) copy-start(bf16[192,1024]{1,0:T(8,128)(2,1)S(1)} %attend.10) | copy-start | bytes 1179652
  66.8 23.4 %collective-permute-start.9 = (bf16[384,1024]{1,0:T(8,128)(2,1)S(1)}, bf16[384,1024]{1,0:T(8,128)(2,1)S(1)}, u32[]{:S(2)}, u32[]{:S(2)}) collective-permute-start(bf16[384,1024]{1,0:T(8,128)(2,1)S(1)} %pad_maximum_fusion.1), channel_id=1, source_target_pairs={{0,16},{16,0},{1,17},{17,1},{2,18},{18,2},{3,19},{19,3},{4,20},{20... | collective-permute-start | bytes 2359304 | tf_op jit(solution)/shard_map/ppermute | solution.py:36
  74.9 15.2 %collective-permute-start.16 = (bf16[416,768]{1,0:T(8,128)(2,1)S(1)}, bf16[416,768]{1,0:T(8,128)(2,1)S(1)}, u32[]{:S(2)}, u32[]{:S(2)}) collective-permute-start(bf16[416,768]{1,0:T(8,128)(2,1)S(1)} %join.15), channel_id=1, source_target_pairs={{0,2},{1,3},{2,0},{3,1},{4,6},{5,7},{6,4},{7,5},{8,10},{9,11},{10,... | collective-permute-start | bytes 1916936 | tf_op jit(solution)/shard_map/ppermute | solution.py:36
  75.6 1.8 %collective-permute-start.14 = (bf16[832,256]{1,0:T(8,128)(2,1)S(1)}, bf16[832,256]{1,0:T(8,128)(2,1)S(1)}, u32[]{:S(2)}, u32[]{:S(2)}) collective-permute-start(bf16[832,256]{1,0:T(8,128)(2,1)S(1)} %join.13), channel_id=1, source_target_pairs={{0,1},{1,0},{2,3},{3,2},{4,5},{5,4},{6,7},{7,6},{8,9},{9,8},{10,11... | collective-permute-start | bytes 1277960 | tf_op jit(solution)/shard_map/ppermute | solution.py:36
  75.7 5.7 %collective-permute-start.15 = (bf16[832,256]{1,0:T(8,128)(2,1)S(1)}, bf16[832,256]{1,0:T(8,128)(2,1)S(1)}, u32[]{:S(2)}, u32[]{:S(2)}) collective-permute-start(bf16[832,256]{1,0:T(8,128)(2,1)S(1)} %join.14), channel_id=1, source_target_pairs={{0,1},{1,0},{2,3},{3,2},{4,5},{5,4},{6,7},{7,6},{8,9},{9,8},{10,11... | collective-permute-start | bytes 1277960 | tf_op jit(solution)/shard_map/ppermute | solution.py:36
  81.4 4.0 %slice-start = ((bf16[192,1024]{1,0:T(8,128)(2,1)}), bf16[48,1024]{1,0:T(8,128)(2,1)S(1)}, s32[]{:S(2)}) async-start(bf16[192,1024]{1,0:T(8,128)(2,1)} %copy-done.4), calls=%async_computation | async-start | bytes 196608 | tf_op jit(solution)/shard_map/slice | solution.py:418
  85.5 22.7 %collective-permute-start.19 = (bf16[432,1024]{1,0:T(8,128)(2,1)S(1)}, bf16[432,1024]{1,0:T(8,128)(2,1)S(1)}, u32[]{:S(2)}, u32[]{:S(2)}) collective-permute-start(bf16[432,1024]{1,0:T(8,128)(2,1)S(1)} %pad_maximum_fusion), channel_id=1, source_target_pairs={{0,16},{16,0},{1,17},{17,1},{2,18},{18,2},{3,19},{19,3},{4,20},{20... | collective-permute-start | bytes 2654216 | tf_op jit(solution)/shard_map/ppermute | solution.py:36
  90.2 2.4 %collective-permute-start.17 = (bf16[832,512]{1,0:T(8,128)(2,1)S(1)}, bf16[832,512]{1,0:T(8,128)(2,1)S(1)}, u32[]{:S(2)}, u32[]{:S(2)}) collective-permute-start(bf16[832,512]{1,0:T(8,128)(2,1)S(1)} %join.16), channel_id=1, source_target_pairs={{0,1},{1,0},{2,3},{3,2},{4,5},{5,4},{6,7},{7,6},{8,9},{9,8},{10,11... | collective-permute-start | bytes 2555912 | tf_op jit(solution)/shard_map/ppermute | solution.py:36
  90.5 10.8 %collective-permute-start.18 = (bf16[832,256]{1,0:T(8,128)(2,1)S(1)}, bf16[832,256]{1,0:T(8,128)(2,1)S(1)}, u32[]{:S(2)}, u32[]{:S(2)}) collective-permute-start(bf16[832,256]{1,0:T(8,128)(2,1)S(1)} %join.17), channel_id=1, source_target_pairs={{0,1},{1,0},{2,3},{3,2},{4,5},{5,4},{6,7},{7,6},{8,9},{9,8},{10,11... | collective-permute-start | bytes 1277960 | tf_op jit(solution)/shard_map/ppermute | solution.py:36

commit v5 on v4

--- a/solution.py
+++ b/solution.py
@@ -113,7 +113,7 @@
     ]
 
 
-def pack_first_kernel(chunks, passed, queries, stream, keys_in, values_in, seg_in, *refs):
+def pack_first_kernel(chunks, passed, query_head, queries, keys_in, values_in, seg_in, *refs):
     *blocks, out, block, keys, values, seg, sems = refs
     tokens = queries.shape[0]
     copies = [
@@ -123,8 +123,7 @@
                 (keys_in, keys),
                 (values_in, values),
                 (seg_in, seg),
-                (queries.at[:, pl.ds(passed[0] * WIDTH, WIDTH)], out.at[pl.ds(0, tokens)]),
-                (stream.at[:, pl.ds(passed[0] * WIDTH, WIDTH)], out.at[pl.ds(tokens, tokens)]),
+                (queries.at[:, pl.ds(query_head * WIDTH, WIDTH)], out.at[pl.ds(0, tokens)]),
             )
         )
     ]
@@ -136,23 +135,21 @@
         fill_block(target, tokens, chunk, keys, values, seg)
     fill_block(block, tokens, passed, keys, values, seg)
     for row, column, to_row, to_column in fold_places(block.shape[0], passed[1]):
-        to_row += 2 * tokens
-        out[to_row : to_row + SEG_ROWS, to_column : to_column + PAIR] = block[
+        out[tokens + to_row : tokens + to_row + SEG_ROWS, to_column : to_column + PAIR] = block[
             row : row + SEG_ROWS, column : column + PAIR
         ]
-    for copy in copies[3:]:
-        copy.wait()
-
-
-def pack_first(queries, stream, keys, values, segments, chunks, passed):
+    copies[3].wait()
+
+
+def pack_first(queries, keys, values, segments, chunks, passed):
     tokens = queries.shape[0]
     block = lambda chunk: (tokens + SEG_ROWS, chunk[1] * PAIR)
     folded = max(place[2] for place in fold_places(tokens + SEG_ROWS, passed[1])) + SEG_ROWS
-    shapes = [block(chunk) for chunk in chunks] + [(2 * tokens + folded, WIDTH)]
+    shapes = [block(chunk) for chunk in chunks] + [(tokens + folded, WIDTH)]
     vmem = pl.BlockSpec(memory_space=pltpu.VMEM)
     return pl.pallas_call(
-        functools.partial(pack_first_kernel, chunks, passed),
-        in_specs=[pl.BlockSpec(memory_space=pltpu.HBM)] * 5,
+        functools.partial(pack_first_kernel, chunks, passed, passed[0]),
+        in_specs=[pl.BlockSpec(memory_space=pltpu.HBM)] * 4,
         out_specs=[vmem] * len(shapes),
         out_shape=[jax.ShapeDtypeStruct(shape, jnp.bfloat16) for shape in shapes],
         scratch_shapes=[
@@ -160,12 +157,12 @@
             pltpu.VMEM(keys.shape, jnp.bfloat16),
             pltpu.VMEM(values.shape, jnp.bfloat16),
             pltpu.VMEM(segments.shape, segments.dtype),
-            pltpu.SemaphoreType.DMA((5,)),
+            pltpu.SemaphoreType.DMA((4,)),
         ],
         cost_estimate=LIGHT,
         compiler_params=pltpu.CompilerParams(vmem_limit_bytes=56 * 2**20),
         name="pack_first",
-    )(queries, stream, keys, values, segments)
+    )(queries, keys, values, segments)
 
 
 def pack_wide_kernel(parts, queries, stream, out, sems):
@@ -380,22 +377,19 @@
         at = [(part, n) for part in full] + [(core, at)]
         return attend(at, queries, stream, head * WIDTH, 0, 0, LIGHT)
 
-    def passed(full, n, core, at, wide, row):
+    def passed(full, n, core, at, q, q_row, s_row):
         at = [(part, n) for part in full] + [(core, at)]
-        return attend(at, wide, wide, 0, row, row + tokens, LIGHT)
+        return attend(at, q, wide_b, 0, q_row, s_row, LIGHT)
 
     chunk_a, chunk_b, chunk_f = (0, 3), (3, 2), (5, 3)
     cut = 3 * tokens // 4
     whole = lambda chunk: (0, chunk[1])
-    block_a, block_b, wide_a = pack_first(
-        queries, stream, keys, values, segments, (chunk_a, chunk_b), chunk_f
-    )
+    block_a, block_b, wide_a = pack_first(queries, keys, values, segments, (chunk_a, chunk_b), chunk_f)
     wide_a = relay(wide_a)
     behind_a = gather_behind(block_a)
-    wide_b = pack_wide(gate(queries, block_a), stream, ((0, 6), (1, 6), (0, 7), (1, 7)))
-    wide_b, behind_a = gate((wide_b, behind_a), wide_a, wide_b)
-    wide_b = relay(wide_b)
-    block_f = unfold(wide_a, 2 * tokens, tokens, chunk_f)
+    wide_b = pack_wide(gate(queries, block_a), stream, ((1, 5), (0, 6), (1, 6), (0, 7), (1, 7)))
+    wide_b, behind_a = relay(wide_b), gate(behind_a, wide_a)
+    block_f = unfold(wide_a, tokens, tokens, chunk_f)
     behind_b = gather_behind(gate(block_b, behind_a))
     y_a = over_y(block_a, behind_a, whole(chunk_a))
     behind_f = gather_behind(gate(block_f, behind_b, y_a))
@@ -418,26 +412,29 @@
     recv_2 = relay(jnp.concatenate([piece_2[cut:], piece_3, piece_4]))
     block_f = gate(block_f, piece_4, recv_1)
     core_f = over_core(block_f, behind_f, y_f, (0, 2))
-    core_7 = over_core(block_f, behind_f, y_f, (2, 1))
-    full_f = (block_f, behind_f[0], y_f)
-    piece_5 = passed(full_f, 0, core_f, 0, wide_a, 0)
-    piece_6 = passed(gate(full_f, piece_5), 1, core_f, 1, wide_b, 0)
-    piece_7 = passed(gate(full_f, piece_6), 2, core_7, 0, wide_b, 2 * tokens)
     rest = tokens - cut
-    pieces = [
+    early = [
         (recv_0, (0, 0)),
         (recv_1[:rest], (cut, 0)),
         (recv_1[rest : rest + tokens], (0, WIDTH)),
         (recv_1[rest + tokens :], (0, 2 * WIDTH)),
+    ]
+    out = assemble(None, early, queries.shape, LIGHT)
+    core_7 = over_core(gate(block_f, out), behind_f, y_f, (2, 1))
+    full_f = (block_f, behind_f[0], y_f)
+    piece_5 = passed(full_f, 0, core_f, 0, wide_a, 0, 0)
+    piece_6 = passed(gate(full_f, piece_5), 1, core_f, 1, wide_b, tokens, 2 * tokens)
+    piece_7 = passed(gate(full_f, piece_6), 2, core_7, 0, wide_b, 3 * tokens, 4 * tokens)
+    recv_2 = gate(recv_2, piece_7)
+    late = [
         (piece_5, (0, 5 * WIDTH)),
         (piece_6, (0, 6 * WIDTH)),
         (piece_7, (0, 7 * WIDTH)),
-    ]
-    out = assemble(None, pieces, queries.shape, LIGHT)
-    recv_2 = gate(recv_2, out)
-    out = lax.dynamic_update_slice(out, recv_2[:rest], (cut, 2 * WIDTH))
-    last = jnp.concatenate([recv_2[rest : rest + tokens], recv_2[rest + tokens :]], axis=1)
-    return lax.dynamic_update_slice(out, last, (0, 3 * WIDTH))[None]
+        (recv_2[:rest], (cut, 2 * WIDTH)),
+        (recv_2[rest : rest + tokens], (0, 3 * WIDTH)),
+        (recv_2[rest + tokens :], (0, 4 * WIDTH)),
+    ]
+    return assemble(out, late, queries.shape, LIGHT)[None]
 
 
 def solution(mesh):

time: 111 us -> 108 us (0.973)
  waiting for transfers between devices: 45 us -> 42.8 us
    ppermute x14, waiting for transfers between devices: 21.6 us -> 14.2 us  [exchange(): lax.ppermute(value, axis, [(i, i ^ bit) for i in range(lax.axis_size(axis...]
    ppermute x6, waiting for transfers between devices: 23.4 us -> 28.6 us  [from_groups_behind(): return lax.ppermute(value, 'ctx', pairs)]
    ppermute x6, starting transfers between devices: 13.8 us -> 9.85 us  [from_groups_behind(): return lax.ppermute(value, 'ctx', pairs)]
    ppermute x14, starting transfers between devices: 8.49 us -> 11.5 us  [exchange(): lax.ppermute(value, axis, [(i, i ^ bit) for i in range(lax.axis_size(axis...]
    pallas_call x1 -> x2, Pallas kernels: 1.43 us -> 2.36 us  [assemble(): pl.pallas_call(functools.partial(assemble_kernel, places), in_specs=[pl.B...]
  transfers between devices with their start and end apart: 20 -> 20, of which waited for: 9 -> 11; matrix products, arithmetic and copies ran while one was open for 0% -> 0% of each run, Pallas kernels for 34% -> 35%
where the time goes in v5:
time: 108 us; the launch traced here: 106 us
  waiting for transfers between devices  42.8 us (40%)
  Pallas kernels  41.3 us (38%)
  starting transfers between devices  21.4 us (20%)
    pallas_call x8, Pallas kernels, attend(): pl.pallas_call(functools.partial(attend_kernel, tokens, column, query_row...  32.9 us
    ppermute x6, waiting for transfers between devices, from_groups_behind(): return lax.ppermute(value, 'ctx', pairs)  28.6 us
    ppermute x14, waiting for transfers between devices, exchange(): lax.ppermute(value, axis, [(i, i ^ bit) for i in range(lax.axis_size(axis...  14.2 us
    ppermute x14, starting transfers between devices, exchange(): lax.ppermute(value, axis, [(i, i ^ bit) for i in range(lax.axis_size(axis...  11.5 us
    ppermute x6, starting transfers between devices, from_groups_behind(): return lax.ppermute(value, 'ctx', pairs)  9.85 us
    pallas_call x1, Pallas kernels, pack_wide(): pl.pallas_call(functools.partial(pack_wide_kernel, parts), in_specs=[pl.B...  2.85 us
    pallas_call x1, Pallas kernels, pack_first(): pl.pallas_call(functools.partial(pack_first_kernel, chunks, passed, passe...  2.39 us
    pallas_call x2, Pallas kernels, assemble(): pl.pallas_call(functools.partial(assemble_kernel, places), in_specs=[pl.B...  2.36 us
  transfers between devices with their start and end apart: 20, of which 11 were waited for; matrix products, arithmetic and copies ran while one was open for 0% of the time, Pallas kernels for 35%

profile of v5, /device:TPU:18, one launch (start us, length us, event | category | flops | bytes accessed | tf_op | source)
XLA Modules:
  0.0 106.4 jit_solution(17864574790651838558)
XLA Ops:
  0.0 2.4 %pack_first.1 = (bf16[208,768]{1,0:T(8,128)(2,1)}, bf16[208,512]{1,0:T(8,128)(2,1)}, bf16[352,1024]{1,0:T(8,128)(2,1)}) custom-call(bf16[192,8192]{1,0:T(8,128)(2,1)} %bitcast.5, bf16[192,1024]{1,0:T(8,128)(2,1)} %bitcast.18, bf16[192,1024]{1,0:T(8,128)(2,1)} %bitcast.19, s32[1,192]{1,0:T(1,128)} %seg_in.1), custom_call_target="tpu_custom_call" | custom-call | flops 1 | bytes 1 | tf_op jit(solution)/shard_map/pack_first/pallas_call | solution.py:150
  2.4 0.6 collective-permute-start.2
  3.0 3.8 %collective-permute-start = (bf16[208,768]{1,0:T(8,128)(2,1)}, bf16[208,768]{1,0:T(8,128)(2,1)S(1)}, u32[]{:S(2)}, u32[]{:S(2)}) collective-permute-start(bf16[208,768]{1,0:T(8,128)(2,1)} %get-tuple-element.45.refs_1_.refs_2_.refs_0_), channel_id=1, source_target_pairs={{0,4},{1,5},{2,6},{3,7},{4,8},{5,9},{6,10},{7,11},{8,12},{9,13},{1... | collective-permute-start | bytes 958472 | tf_op jit(solution)/shard_map/ppermute | solution.py:44
  6.8 2.8 %pack_wide.1 = bf16[960,1024]{1,0:T(8,128)(2,1)} custom-call(bf16[192,8192]{1,0:T(8,128)(2,1)} %bitcast.6, bf16[192,8192]{1,0:T(8,128)(2,1)} %bitcast.12), custom_call_target="tpu_custom_call" | custom-call | flops 1 | bytes 1 | tf_op jit(solution)/shard_map/pack_wide/pallas_call | solution.py:185
  9.7 1.6 %collective-permute-start.13 = (bf16[960,1024]{1,0:T(8,128)(2,1)}, bf16[960,1024]{1,0:T(8,128)(2,1)S(1)}, u32[]{:S(2)}, u32[]{:S(2)}) collective-permute-start(bf16[960,1024]{1,0:T(8,128)(2,1)} %pack_wide.1), channel_id=1, source_target_pairs={{0,16},{16,0},{1,17},{17,1},{2,18},{18,2},{3,19},{19,3},{4,20},{20... | collective-permute-start | bytes 5898248 | tf_op jit(solution)/shard_map/ppermute | solution.py:36
  11.2 5.7 %collective-permute-done.1.refs_2_.refs_3_ = bf16[208,768]{1,0:T(8,128)(2,1)S(1)} collective-permute-done((bf16[208,768]{1,0:T(8,128)(2,1)}, bf16[208,768]{1,0:T(8,128)(2,1)S(1)}, u32[]{:S(2)}, u32[]{:S(2)}) %collective-permute-start.1) | collective-permute-done | bytes 319520 | tf_op jit(solution)/shard_map/ppermute | solution.py:44
  17.0 9.9 %collective-permute-done.refs_0_.refs_1_ = bf16[208,768]{1,0:T(8,128)(2,1)S(1)} collective-permute-done((bf16[208,768]{1,0:T(8,128)(2,1)}, bf16[208,768]{1,0:T(8,128)(2,1)S(1)}, u32[]{:S(2)}, u32[]{:S(2)}) %collective-permute-start) | collective-permute-done | bytes 319520 | tf_op jit(solution)/shard_map/ppermute | solution.py:44
  26.9 1.6 %collective-permute-start.5 = (bf16[416,768]{1,0:T(8,128)(2,1)S(1)}, bf16[416,768]{1,0:T(8,128)(2,1)S(1)}, u32[]{:S(2)}, u32[]{:S(2)}) collective-permute-start(bf16[416,768]{1,0:T(8,128)(2,1)S(1)} %join.9), channel_id=1, source_target_pairs={{0,2},{1,3},{2,0},{3,1},{4,6},{5,7},{6,4},{7,5},{8,10},{9,11},{10,... | collective-permute-start | bytes 1916936 | tf_op jit(solution)/shard_map/ppermute | solution.py:36
  28.5 3.0 %collective-permute-start.3 = (bf16[208,512]{1,0:T(8,128)(2,1)S(1)}, bf16[208,512]{1,0:T(8,128)(2,1)S(1)}, u32[]{:S(2)}, u32[]{:S(2)}) collective-permute-start(bf16[208,512]{1,0:T(8,128)(2,1)S(1)} %copy-done.3), channel_id=1, source_target_pairs={{0,4},{1,5},{2,6},{3,7},{4,8},{5,9},{6,10},{7,11},{8,12},{9,13},{1... | collective-permute-start | bytes 638984 | tf_op jit(solution)/shard_map/ppermute | solution.py:44
  31.5 6.2 %collective-permute-done.4.refs_2_.refs_3_ = bf16[208,512]{1,0:T(8,128)(2,1)S(1)} collective-permute-done((bf16[208,512]{1,0:T(8,128)(2,1)S(1)}, bf16[208,512]{1,0:T(8,128)(2,1)S(1)}, u32[]{:S(2)}, u32[]{:S(2)}) %collective-permute-start.4) | collective-permute-done | bytes 213024 | tf_op jit(solution)/shard_map/ppermute | solution.py:44
  37.7 4.7 %collective-permute-done.3.refs_0_.refs_1_ = bf16[208,512]{1,0:T(8,128)(2,1)S(1)} collective-permute-done((bf16[208,512]{1,0:T(8,128)(2,1)S(1)}, bf16[208,512]{1,0:T(8,128)(2,1)S(1)}, u32[]{:S(2)}, u32[]{:S(2)}) %collective-permute-start.3) | collective-permute-done | bytes 213024 | tf_op jit(solution)/shard_map/ppermute | solution.py:44
  42.4 0.8 collective-permute-done.5.refs_1_.refs_2_.refs_3_
  44.2 1.6 %collective-permute-start.12 = (bf16[416,512]{1,0:T(8,128)(2,1)S(1)}, bf16[416,512]{1,0:T(8,128)(2,1)S(1)}, u32[]{:S(2)}, u32[]{:S(2)}) collective-permute-start(bf16[416,512]{1,0:T(8,128)(2,1)S(1)} %join.12), channel_id=1, source_target_pairs={{0,2},{1,3},{2,0},{3,1},{4,6},{5,7},{6,4},{7,5},{8,10},{9,11},{10,... | collective-permute-start | bytes 1277960 | tf_op jit(solution)/shard_map/ppermute | solution.py:36
  45.8 3.0 %collective-permute-start.10 = (bf16[208,768]{1,0:T(8,128)(2,1)S(1)}, bf16[208,768]{1,0:T(8,128)(2,1)S(1)}, u32[]{:S(2)}, u32[]{:S(2)}) collective-permute-start(bf16[208,768]{1,0:T(8,128)(2,1)S(1)} %unfold.1.refs_1_.refs_2_.refs_0_), channel_id=1, source_target_pairs={{0,4},{1,5},{2,6},{3,7},{4,8},{5,9},{6,10},{7,11},{8,12},{9,13},{1... | collective-permute-start | bytes 958472 | tf_op jit(solution)/shard_map/ppermute | solution.py:44
  48.8 4.0 %attend.8 = bf16[192,1024]{1,0:T(8,128)(2,1)S(1)} custom-call(bf16[208,768]{1,0:T(8,128)(2,1)S(1)} %copy-done.2, bf16[208,768]{1,0:T(8,128)(2,1)S(1)} %collective-permute-done.refs_0_.refs_1_, bf16[416,768]{1,0:T(8,128)(2,1)S(1)} %collective-permute-done.5.refs_1_.refs_2_.refs_3_, bf16[416,768]{1,0:T(8,128)(2,1)S(1)} %collective-permute-done.5.refs_1_.refs_2_.refs_3_, ...), custom_call_target="tpu_custom_call" | custom-call | flops 1 | bytes 1 | tf_op jit(solution)/shard_map/attend/pallas_call | solution.py:315
  52.8 1.6 %collective-permute-start.7 = (bf16[144,1024]{1,0:T(8,128)(2,1)S(1)}, bf16[144,1024]{1,0:T(8,128)(2,1)S(1)}, u32[]{:S(2)}, u32[]{:S(2)}) collective-permute-start(bf16[144,1024]{1,0:T(8,128)(2,1)S(1)} %slice.40), channel_id=1, source_target_pairs={{0,16},{16,0},{1,17},{17,1},{2,18},{18,2},{3,19},{19,3},{4,20},{20... | collective-permute-start | bytes 884744 | tf_op jit(solution)/shard_map/ppermute | solution.py:36
  54.4 4.0 %attend.9 = bf16[192,1024]{1,0:T(8,128)(2,1)S(1)} custom-call(bf16[208,768]{1,0:T(8,128)(2,1)S(1)} %copy-done.2, bf16[208,768]{1,0:T(8,128)(2,1)S(1)} %collective-permute-done.refs_0_.refs_1_, bf16[416,768]{1,0:T(8,128)(2,1)S(1)} %collective-permute-done.5.refs_1_.refs_2_.refs_3_, bf16[416,768]{1,0:T(8,128)(2,1)S(1)} %collective-permute-done.5.refs_1_.refs_2_.refs_3_, ...), custom_call_target="tpu_custom_call" | custom-call | flops 1 | bytes 1 | tf_op jit(solution)/shard_map/attend/pallas_call | solution.py:315
  58.4 4.0 %attend.10 = bf16[192,1024]{1,0:T(8,128)(2,1)S(1)} custom-call(bf16[208,768]{1,0:T(8,128)(2,1)S(1)} %copy-done.2, bf16[208,768]{1,0:T(8,128)(2,1)S(1)} %collective-permute-done.refs_0_.refs_1_, bf16[416,768]{1,0:T(8,128)(2,1)S(1)} %collective-permute-done.5.refs_1_.refs_2_.refs_3_, bf16[416,768]{1,0:T(8,128)(2,1)S(1)} %collective-permute-done.5.refs_1_.refs_2_.refs_3_, ...), custom_call_target="tpu_custom_call" | custom-call | flops 1 | bytes 1 | tf_op jit(solution)/shard_map/attend/pallas_call | solution.py:315
  62.5 0.6 collective-permute-start.9
  63.1 2.1 %collective-permute-done.10.refs_0_.refs_1_ = bf16[208,768]{1,0:T(8,128)(2,1)S(1)} collective-permute-done((bf16[208,768]{1,0:T(8,128)(2,1)S(1)}, bf16[208,768]{1,0:T(8,128)(2,1)S(1)}, u32[]{:S(2)}, u32[]{:S(2)}) %collective-permute-start.10) | collective-permute-done | bytes 319520 | tf_op jit(solution)/shard_map/ppermute | solution.py:44
  65.2 4.9 %collective-permute-done.7.refs_0_ = bf16[144,1024]{1,0:T(8,128)(2,1)S(1)} collective-permute-done((bf16[144,1024]{1,0:T(8,128)(2,1)S(1)}, bf16[144,1024]{1,0:T(8,128)(2,1)S(1)}, u32[]{:S(2)}, u32[]{:S(2)}) %collective-permute-start.7) | collective-permute-done | bytes 294944 | tf_op jit(solution)/shard_map/ppermute | solution.py:36
  70.4 1.6 %collective-permute-start.16 = (bf16[416,768]{1,0:T(8,128)(2,1)S(1)}, bf16[416,768]{1,0:T(8,128)(2,1)S(1)}, u32[]{:S(2)}, u32[]{:S(2)}) collective-permute-start(bf16[416,768]{1,0:T(8,128)(2,1)S(1)} %join.15), channel_id=1, source_target_pairs={{0,2},{1,3},{2,0},{3,1},{4,6},{5,7},{6,4},{7,5},{8,10},{9,11},{10,... | collective-permute-start | bytes 1916936 | tf_op jit(solution)/shard_map/ppermute | solution.py:36
  72.7 1.2 %collective-permute-done.14.refs_4_.refs_5_.refs_6_.refs_7_ = bf16[832,256]{1,0:T(8,128)(2,1)S(1)} collective-permute-done((bf16[832,256]{1,0:T(8,128)(2,1)S(1)}, bf16[832,256]{1,0:T(8,128)(2,1)S(1)}, u32[]{:S(2)}, u32[]{:S(2)}) %collective-permute-start.14) | collective-permute-done | bytes 426016 | tf_op jit(solution)/shard_map/ppermute | solution.py:36
  73.8 4.0 %attend.11 = bf16[192,1024]{1,0:T(8,128)(2,1)S(1)} custom-call(bf16[208,512]{1,0:T(8,128)(2,1)S(1)} %copy-done.3, bf16[208,512]{1,0:T(8,128)(2,1)S(1)} %collective-permute-done.3.refs_0_.refs_1_, bf16[416,512]{1,0:T(8,128)(2,1)S(1)} %collective-permute-done.12.refs_1_.refs_2_.refs_3_, bf16[416,512]{1,0:T(8,128)(2,1)S(1)} %collective-permute-done.12.refs_1_.refs_2_.refs_3_, ...), custom_call_target="tpu_custom_call" | custom-call | flops 1 | bytes 1 | tf_op jit(solution)/shard_map/attend/pallas_call | solution.py:315
  77.8 4.0 %attend.12 = bf16[192,1024]{1,0:T(8,128)(2,1)S(1)} custom-call(bf16[208,512]{1,0:T(8,128)(2,1)S(1)} %copy-done.3, bf16[208,512]{1,0:T(8,128)(2,1)S(1)} %collective-permute-done.3.refs_0_.refs_1_, bf16[416,512]{1,0:T(8,128)(2,1)S(1)} %collective-permute-done.12.refs_1_.refs_2_.refs_3_, bf16[416,512]{1,0:T(8,128)(2,1)S(1)} %collective-permute-done.12.refs_1_.refs_2_.refs_3_, ...), custom_call_target="tpu_custom_call" | custom-call | flops 1 | bytes 1 | tf_op jit(solution)/shard_map/attend/pallas_call | solution.py:315
  82.5 4.4 %collective-permute-done.9 = bf16[384,1024]{1,0:T(8,128)(2,1)S(1)} collective-permute-done((bf16[384,1024]{1,0:T(8,128)(2,1)S(1)}, bf16[384,1024]{1,0:T(8,128)(2,1)S(1)}, u32[]{:S(2)}, u32[]{:S(2)}) %collective-permute-start.9) | collective-permute-done | bytes 786464 | tf_op jit(solution)/shard_map/ppermute | solution.py:36
  87.2 1.0 assemble.2.refs_0_
  89.5 4.3 %attend.13.refs_1_ = bf16[192,1024]{1,0:T(8,128)(2,1)S(1)} custom-call(bf16[208,768]{1,0:T(8,128)(2,1)S(1)} %unfold.1.refs_1_.refs_2_.refs_0_, bf16[208,768]{1,0:T(8,128)(2,1)S(1)} %collective-permute-done.10.refs_0_.refs_1_, bf16[416,768]{1,0:T(8,128)(2,1)S(1)} %collective-permute-done.16.refs_1_.refs_2_.refs_3_, ...), custom_call_target="tpu_custom_call" | custom-call | flops 1 | bytes 1 | tf_op jit(solution)/shard_map/attend/pallas_call | solution.py:315
  93.8 4.3 %attend.14.refs_2_ = bf16[192,1024]{1,0:T(8,128)(2,1)S(1)} custom-call(bf16[208,768]{1,0:T(8,128)(2,1)S(1)} %unfold.1.refs_1_.refs_2_.refs_0_, bf16[208,768]{1,0:T(8,128)(2,1)S(1)} %collective-permute-done.10.refs_0_.refs_1_, bf16[416,768]{1,0:T(8,128)(2,1)S(1)} %collective-permute-done.16.refs_1_.refs_2_.refs_3_, ...), custom_call_target="tpu_custom_call" | custom-call | flops 1 | bytes 1 | tf_op jit(solution)/shard_map/attend/pallas_call | solution.py:315
  98.1 4.3 %attend.15.refs_3_ = bf16[192,1024]{1,0:T(8,128)(2,1)S(1)} custom-call(bf16[208,768]{1,0:T(8,128)(2,1)S(1)} %unfold.1.refs_1_.refs_2_.refs_0_, bf16[208,768]{1,0:T(8,128)(2,1)S(1)} %collective-permute-done.10.refs_0_.refs_1_, bf16[416,768]{1,0:T(8,128)(2,1)S(1)} %collective-permute-done.16.refs_1_.refs_2_.refs_3_, ...), custom_call_target="tpu_custom_call" | custom-call | flops 1 | bytes 1 | tf_op jit(solution)/shard_map/attend/pallas_call | solution.py:315
  102.4 2.4 %collective-permute-done.19 = bf16[432,1024]{1,0:T(8,128)(2,1)S(1)} collective-permute-done((bf16[432,1024]{1,0:T(8,128)(2,1)S(1)}, bf16[432,1024]{1,0:T(8,128)(2,1)S(1)}, u32[]{:S(2)}, u32[]{:S(2)}) %collective-permute-start.19) | collective-permute-done | bytes 884768 | tf_op jit(solution)/shard_map/ppermute | solution.py:36
  104.9 1.4 %assemble.3 = bf16[192,8192]{1,0:T(8,128)(2,1)} custom-call(bf16[192,8192]{1,0:T(8,128)(2,1)} %assemble.2.refs_0_, bf16[192,1024]{1,0:T(8,128)(2,1)S(1)} %attend.13.refs_1_, bf16[192,1024]{1,0:T(8,128)(2,1)S(1)} %attend.14.refs_2_, bf16[192,1024]{1,0:T(8,128)(2,1)S(1)} %attend.15.refs_3_, ...), custom_call_target="tpu_custom_call", output_to_operand_aliasing={{}: (0, {})} | custom-call | flops 1 | bytes 1 | tf_op jit(solution)/shard_map/assemble/pallas_call | solution.py:357
  (52 shorter events, 4.2 us)
Async XLA Ops:
  2.4 24.4 %collective-permute-start.2 = (bf16[352,1024]{1,0:T(8,128)(2,1)}, bf16[352,1024]{1,0:T(8,128)(2,1)S(1)}, u32[]{:S(2)}, u32[]{:S(2)}) collective-permute-start(bf16[352,1024]{1,0:T(8,128)(2,1)} %get-tuple-element.37), channel_id=1, source_target_pairs={{0,16},{16,0},{1,17},{17,1},{2,18},{18,2},{3,19},{19,3},{4,20},{20... | collective-permute-start | bytes 2162696 | tf_op jit(solution)/shard_map/ppermute | solution.py:36
  3.0 14.0 %collective-permute-start.1 = (bf16[208,768]{1,0:T(8,128)(2,1)}, bf16[208,768]{1,0:T(8,128)(2,1)S(1)}, u32[]{:S(2)}, u32[]{:S(2)}) collective-permute-start(bf16[208,768]{1,0:T(8,128)(2,1)} %get-tuple-element.45.refs_1_.refs_2_.refs_0_), channel_id=1, source_target_pairs={{0,8},{1,9},{2,10},{3,11},{4,12},{5,13},{6,14},{7,15},{8,0},{9,1},... | collective-permute-start | bytes 958472 | tf_op jit(solution)/shard_map/ppermute | solution.py:44
  3.0 23.8 %collective-permute-start = (bf16[208,768]{1,0:T(8,128)(2,1)}, bf16[208,768]{1,0:T(8,128)(2,1)S(1)}, u32[]{:S(2)}, u32[]{:S(2)}) collective-permute-start(bf16[208,768]{1,0:T(8,128)(2,1)} %get-tuple-element.45.refs_1_.refs_2_.refs_0_), channel_id=1, source_target_pairs={{0,4},{1,5},{2,6},{3,7},{4,8},{5,9},{6,10},{7,11},{8,12},{9,13},{1... | collective-permute-start | bytes 958472 | tf_op jit(solution)/shard_map/ppermute | solution.py:44
  6.8 20.0 %copy-start.2 = (bf16[208,768]{1,0:T(8,128)(2,1)S(1)}, bf16[208,768]{1,0:T(8,128)(2,1)}, u32[]{:S(2)}) copy-start(bf16[208,768]{1,0:T(8,128)(2,1)} %get-tuple-element.45.refs_1_.refs_2_.refs_0_) | copy-start | bytes 958468
  6.8 21.7 %copy-start.3 = (bf16[208,512]{1,0:T(8,128)(2,1)S(1)}, bf16[208,512]{1,0:T(8,128)(2,1)}, u32[]{:S(2)}) copy-start(bf16[208,512]{1,0:T(8,128)(2,1)} %get-tuple-element.53.refs_1_.refs_2_.refs_0_) | copy-start | bytes 638980
  9.7 55.5 %collective-permute-start.13 = (bf16[960,1024]{1,0:T(8,128)(2,1)}, bf16[960,1024]{1,0:T(8,128)(2,1)S(1)}, u32[]{:S(2)}, u32[]{:S(2)}) collective-permute-start(bf16[960,1024]{1,0:T(8,128)(2,1)} %pack_wide.1), channel_id=1, source_target_pairs={{0,16},{16,0},{1,17},{17,1},{2,18},{18,2},{3,19},{19,3},{4,20},{20... | collective-permute-start | bytes 5898248 | tf_op jit(solution)/shard_map/ppermute | solution.py:36
  26.9 16.4 %collective-permute-start.5 = (bf16[416,768]{1,0:T(8,128)(2,1)S(1)}, bf16[416,768]{1,0:T(8,128)(2,1)S(1)}, u32[]{:S(2)}, u32[]{:S(2)}) collective-permute-start(bf16[416,768]{1,0:T(8,128)(2,1)S(1)} %join.9), channel_id=1, source_target_pairs={{0,2},{1,3},{2,0},{3,1},{4,6},{5,7},{6,4},{7,5},{8,10},{9,11},{10,... | collective-permute-start | bytes 1916936 | tf_op jit(solution)/shard_map/ppermute | solution.py:36
  28.5 9.3 %collective-permute-start.4 = (bf16[208,512]{1,0:T(8,128)(2,1)S(1)}, bf16[208,512]{1,0:T(8,128)(2,1)S(1)}, u32[]{:S(2)}, u32[]{:S(2)}) collective-permute-start(bf16[208,512]{1,0:T(8,128)(2,1)S(1)} %copy-done.3), channel_id=1, source_target_pairs={{0,8},{1,9},{2,10},{3,11},{4,12},{5,13},{6,14},{7,15},{8,0},{9,1},... | collective-permute-start | bytes 638984 | tf_op jit(solution)/shard_map/ppermute | solution.py:44
  28.5 13.9 %collective-permute-start.3 = (bf16[208,512]{1,0:T(8,128)(2,1)S(1)}, bf16[208,512]{1,0:T(8,128)(2,1)S(1)}, u32[]{:S(2)}, u32[]{:S(2)}) collective-permute-start(bf16[208,512]{1,0:T(8,128)(2,1)S(1)} %copy-done.3), channel_id=1, source_target_pairs={{0,4},{1,5},{2,6},{3,7},{4,8},{5,9},{6,10},{7,11},{8,12},{9,13},{1... | collective-permute-start | bytes 638984 | tf_op jit(solution)/shard_map/ppermute | solution.py:44
  43.3 5.5 %copy-start.1 = (bf16[1,192,8192]{2,1,0:T(8,128)(2,1)S(1)}, bf16[1,192,8192]{2,1,0:T(8,128)(2,1)}, u32[]{:S(2)}) copy-start(bf16[1,192,8192]{2,1,0:T(8,128)(2,1)} %param.5) | copy-start | bytes 9437188
  43.3 5.4 %copy-start = (bf16[1,192,8192]{2,1,0:T(8,128)(2,1)S(1)}, bf16[1,192,8192]{2,1,0:T(8,128)(2,1)}, u32[]{:S(2)}) copy-start(bf16[1,192,8192]{2,1,0:T(8,128)(2,1)} %param.6) | copy-start | bytes 9437188
  43.3 2.4 %collective-permute-start.6 = (bf16[832,512]{1,0:T(8,128)(2,1)S(1)}, bf16[832,512]{1,0:T(8,128)(2,1)S(1)}, u32[]{:S(2)}, u32[]{:S(2)}) collective-permute-start(bf16[832,512]{1,0:T(8,128)(2,1)S(1)} %join.10), channel_id=1, source_target_pairs={{0,1},{1,0},{2,3},{3,2},{4,5},{5,4},{6,7},{7,6},{8,9},{9,8},{10,11... | collective-permute-start | bytes 2555912 | tf_op jit(solution)/shard_map/ppermute | solution.py:36
  43.5 9.4 %collective-permute-start.8 = (bf16[832,256]{1,0:T(8,128)(2,1)S(1)}, bf16[832,256]{1,0:T(8,128)(2,1)S(1)}, u32[]{:S(2)}, u32[]{:S(2)}) collective-permute-start(bf16[832,256]{1,0:T(8,128)(2,1)S(1)} %join.11), channel_id=1, source_target_pairs={{0,1},{1,0},{2,3},{3,2},{4,5},{5,4},{6,7},{7,6},{8,9},{9,8},{10,11... | collective-permute-start | bytes 1277960 | tf_op jit(solution)/shard_map/ppermute | solution.py:36
  44.0 18.5 %collective-permute-start.11 = (bf16[208,768]{1,0:T(8,128)(2,1)S(1)}, bf16[208,768]{1,0:T(8,128)(2,1)S(1)}, u32[]{:S(2)}, u32[]{:S(2)}) collective-permute-start(bf16[208,768]{1,0:T(8,128)(2,1)S(1)} %unfold.1.refs_1_.refs_2_.refs_0_), channel_id=1, source_target_pairs={{0,8},{1,9},{2,10},{3,11},{4,12},{5,13},{6,14},{7,15},{8,0},{9,1},... | collective-permute-start | bytes 958472 | tf_op jit(solution)/shard_map/ppermute | solution.py:44
  44.2 21.1 %collective-permute-start.12 = (bf16[416,512]{1,0:T(8,128)(2,1)S(1)}, bf16[416,512]{1,0:T(8,128)(2,1)S(1)}, u32[]{:S(2)}, u32[]{:S(2)}) collective-permute-start(bf16[416,512]{1,0:T(8,128)(2,1)S(1)} %join.12), channel_id=1, source_target_pairs={{0,2},{1,3},{2,0},{3,1},{4,6},{5,7},{6,4},{7,5},{8,10},{9,11},{10,... | collective-permute-start | bytes 1277960 | tf_op jit(solution)/shard_map/ppermute | solution.py:36
  45.8 19.4 %collective-permute-start.10 = (bf16[208,768]{1,0:T(8,128)(2,1)S(1)}, bf16[208,768]{1,0:T(8,128)(2,1)S(1)}, u32[]{:S(2)}, u32[]{:S(2)}) collective-permute-start(bf16[208,768]{1,0:T(8,128)(2,1)S(1)} %unfold.1.refs_1_.refs_2_.refs_0_), channel_id=1, source_target_pairs={{0,4},{1,5},{2,6},{3,7},{4,8},{5,9},{6,10},{7,11},{8,12},{9,13},{1... | collective-permute-start | bytes 958472 | tf_op jit(solution)/shard_map/ppermute | solution.py:44
  52.8 17.3 %collective-permute-start.7 = (bf16[144,1024]{1,0:T(8,128)(2,1)S(1)}, bf16[144,1024]{1,0:T(8,128)(2,1)S(1)}, u32[]{:S(2)}, u32[]{:S(2)}) collective-permute-start(bf16[144,1024]{1,0:T(8,128)(2,1)S(1)} %slice.40), channel_id=1, source_target_pairs={{0,16},{16,0},{1,17},{17,1},{2,18},{18,2},{3,19},{19,3},{4,20},{20... | collective-permute-start | bytes 884744 | tf_op jit(solution)/shard_map/ppermute | solution.py:36
  62.4 10.3 %copy-start.4 = (bf16[192,1024]{1,0:T(8,128)(2,1)}, bf16[192,1024]{1,0:T(8,128)(2,1)S(1)}, u32[]{:S(2)}) copy-start(bf16[192,1024]{1,0:T(8,128)(2,1)S(1)} %attend.10) | copy-start | bytes 1179652
  62.5 24.4 %collective-permute-start.9 = (bf16[384,1024]{1,0:T(8,128)(2,1)S(1)}, bf16[384,1024]{1,0:T(8,128)(2,1)S(1)}, u32[]{:S(2)}, u32[]{:S(2)}) collective-permute-start(bf16[384,1024]{1,0:T(8,128)(2,1)S(1)} %pad_maximum_fusion.1), channel_id=1, source_target_pairs={{0,16},{16,0},{1,17},{17,1},{2,18},{18,2},{3,19},{19,3},{4,20},{20... | collective-permute-start | bytes 2359304 | tf_op jit(solution)/shard_map/ppermute | solution.py:36
  70.4 16.6 %collective-permute-start.16 = (bf16[416,768]{1,0:T(8,128)(2,1)S(1)}, bf16[416,768]{1,0:T(8,128)(2,1)S(1)}, u32[]{:S(2)}, u32[]{:S(2)}) collective-permute-start(bf16[416,768]{1,0:T(8,128)(2,1)S(1)} %join.15), channel_id=1, source_target_pairs={{0,2},{1,3},{2,0},{3,1},{4,6},{5,7},{6,4},{7,5},{8,10},{9,11},{10,... | collective-permute-start | bytes 1916936 | tf_op jit(solution)/shard_map/ppermute | solution.py:36
  72.0 1.8 %collective-permute-start.14 = (bf16[832,256]{1,0:T(8,128)(2,1)S(1)}, bf16[832,256]{1,0:T(8,128)(2,1)S(1)}, u32[]{:S(2)}, u32[]{:S(2)}) collective-permute-start(bf16[832,256]{1,0:T(8,128)(2,1)S(1)} %join.13), channel_id=1, source_target_pairs={{0,1},{1,0},{2,3},{3,2},{4,5},{5,4},{6,7},{7,6},{8,9},{9,8},{10,11... | collective-permute-start | bytes 1277960 | tf_op jit(solution)/shard_map/ppermute | solution.py:36
  72.1 5.7 %collective-permute-start.15 = (bf16[832,256]{1,0:T(8,128)(2,1)S(1)}, bf16[832,256]{1,0:T(8,128)(2,1)S(1)}, u32[]{:S(2)}, u32[]{:S(2)}) collective-permute-start(bf16[832,256]{1,0:T(8,128)(2,1)S(1)} %join.14), channel_id=1, source_target_pairs={{0,1},{1,0},{2,3},{3,2},{4,5},{5,4},{6,7},{7,6},{8,9},{9,8},{10,11... | collective-permute-start | bytes 1277960 | tf_op jit(solution)/shard_map/ppermute | solution.py:36
  77.8 4.0 %slice-start = ((bf16[192,1024]{1,0:T(8,128)(2,1)}), bf16[48,1024]{1,0:T(8,128)(2,1)S(1)}, s32[]{:S(2)}) async-start(bf16[192,1024]{1,0:T(8,128)(2,1)} %copy-done.4), calls=%async_computation | async-start | bytes 196608 | tf_op jit(solution)/shard_map/slice | solution.py:412
  81.9 22.9 %collective-permute-start.19 = (bf16[432,1024]{1,0:T(8,128)(2,1)S(1)}, bf16[432,1024]{1,0:T(8,128)(2,1)S(1)}, u32[]{:S(2)}, u32[]{:S(2)}) collective-permute-start(bf16[432,1024]{1,0:T(8,128)(2,1)S(1)} %pad_maximum_fusion), channel_id=1, source_target_pairs={{0,16},{16,0},{1,17},{17,1},{2,18},{18,2},{3,19},{19,3},{4,20},{20... | collective-permute-start | bytes 2654216 | tf_op jit(solution)/shard_map/ppermute | solution.py:36
  87.0 2.4 %collective-permute-start.17 = (bf16[832,512]{1,0:T(8,128)(2,1)S(1)}, bf16[832,512]{1,0:T(8,128)(2,1)S(1)}, u32[]{:S(2)}, u32[]{:S(2)}) collective-permute-start(bf16[832,512]{1,0:T(8,128)(2,1)S(1)} %join.16), channel_id=1, source_target_pairs={{0,1},{1,0},{2,3},{3,2},{4,5},{5,4},{6,7},{7,6},{8,9},{9,8},{10,11... | collective-permute-start | bytes 2555912 | tf_op jit(solution)/shard_map/ppermute | solution.py:36
  88.5 9.7 %collective-permute-start.18 = (bf16[832,256]{1,0:T(8,128)(2,1)S(1)}, bf16[832,256]{1,0:T(8,128)(2,1)S(1)}, u32[]{:S(2)}, u32[]{:S(2)}) collective-permute-start(bf16[832,256]{1,0:T(8,128)(2,1)S(1)} %join.17), channel_id=1, source_target_pairs={{0,1},{1,0},{2,3},{3,2},{4,5},{5,4},{6,7},{7,6},{8,9},{9,8},{10,11... | collective-permute-start | bytes 1277960 | tf_op jit(solution)/shard_map/ppermute | solution.py:36

commit v6 on v5

--- a/solution.py
+++ b/solution.py
@@ -113,9 +113,9 @@
     ]
 
 
-def pack_first_kernel(chunks, passed, query_head, queries, keys_in, values_in, seg_in, *refs):
+def pack_first_kernel(chunks, passed, keys_in, values_in, seg_in, *refs):
     *blocks, out, block, keys, values, seg, sems = refs
-    tokens = queries.shape[0]
+    tokens = keys_in.shape[0]
     copies = [
         pltpu.make_async_copy(source, target, sems.at[n])
         for n, (source, target) in enumerate(
@@ -123,33 +123,31 @@
                 (keys_in, keys),
                 (values_in, values),
                 (seg_in, seg),
-                (queries.at[:, pl.ds(query_head * WIDTH, WIDTH)], out.at[pl.ds(0, tokens)]),
             )
         )
     ]
     for copy in copies:
         copy.start()
-    for copy in copies[:3]:
+    for copy in copies:
         copy.wait()
     for target, chunk in zip(blocks, chunks):
         fill_block(target, tokens, chunk, keys, values, seg)
     fill_block(block, tokens, passed, keys, values, seg)
     for row, column, to_row, to_column in fold_places(block.shape[0], passed[1]):
-        out[tokens + to_row : tokens + to_row + SEG_ROWS, to_column : to_column + PAIR] = block[
+        out[to_row : to_row + SEG_ROWS, to_column : to_column + PAIR] = block[
             row : row + SEG_ROWS, column : column + PAIR
         ]
-    copies[3].wait()
-
-
-def pack_first(queries, keys, values, segments, chunks, passed):
-    tokens = queries.shape[0]
+
+
+def pack_first(keys, values, segments, chunks, passed):
+    tokens = keys.shape[0]
     block = lambda chunk: (tokens + SEG_ROWS, chunk[1] * PAIR)
     folded = max(place[2] for place in fold_places(tokens + SEG_ROWS, passed[1])) + SEG_ROWS
-    shapes = [block(chunk) for chunk in chunks] + [(tokens + folded, WIDTH)]
+    shapes = [block(chunk) for chunk in chunks] + [(folded, WIDTH)]
     vmem = pl.BlockSpec(memory_space=pltpu.VMEM)
     return pl.pallas_call(
-        functools.partial(pack_first_kernel, chunks, passed, passed[0]),
-        in_specs=[pl.BlockSpec(memory_space=pltpu.HBM)] * 4,
+        functools.partial(pack_first_kernel, chunks, passed),
+        in_specs=[pl.BlockSpec(memory_space=pltpu.HBM)] * 3,
         out_specs=[vmem] * len(shapes),
         out_shape=[jax.ShapeDtypeStruct(shape, jnp.bfloat16) for shape in shapes],
         scratch_shapes=[
@@ -157,12 +155,12 @@
             pltpu.VMEM(keys.shape, jnp.bfloat16),
             pltpu.VMEM(values.shape, jnp.bfloat16),
             pltpu.VMEM(segments.shape, segments.dtype),
-            pltpu.SemaphoreType.DMA((4,)),
+            pltpu.SemaphoreType.DMA((3,)),
         ],
         cost_estimate=LIGHT,
         compiler_params=pltpu.CompilerParams(vmem_limit_bytes=56 * 2**20),
         name="pack_first",
-    )(queries, keys, values, segments)
+    )(keys, values, segments)
 
 
 def pack_wide_kernel(parts, queries, stream, out, sems):
@@ -384,12 +382,15 @@
     chunk_a, chunk_b, chunk_f = (0, 3), (3, 2), (5, 3)
     cut = 3 * tokens // 4
     whole = lambda chunk: (0, chunk[1])
-    block_a, block_b, wide_a = pack_first(queries, keys, values, segments, (chunk_a, chunk_b), chunk_f)
+    query_5 = queries[:, 5 * WIDTH : 6 * WIDTH]
+    keys = gate(keys, query_5)
+    query_5 = relay(query_5)
+    block_a, block_b, wide_a = pack_first(keys, values, segments, (chunk_a, chunk_b), chunk_f)
     wide_a = relay(wide_a)
     behind_a = gather_behind(block_a)
     wide_b = pack_wide(gate(queries, block_a), stream, ((1, 5), (0, 6), (1, 6), (0, 7), (1, 7)))
-    wide_b, behind_a = relay(wide_b), gate(behind_a, wide_a)
-    block_f = unfold(wide_a, tokens, tokens, chunk_f)
+    wide_b, behind_a = relay(wide_b), gate(behind_a, wide_a, query_5)
+    block_f = unfold(wide_a, 0, tokens, chunk_f)
     behind_b = gather_behind(gate(block_b, behind_a))
     y_a = over_y(block_a, behind_a, whole(chunk_a))
     behind_f = gather_behind(gate(block_f, behind_b, y_a))
@@ -422,7 +423,7 @@
     out = assemble(None, early, queries.shape, LIGHT)
     core_7 = over_core(gate(block_f, out), behind_f, y_f, (2, 1))
     full_f = (block_f, behind_f[0], y_f)
-    piece_5 = passed(full_f, 0, core_f, 0, wide_a, 0, 0)
+    piece_5 = passed(full_f, 0, core_f, 0, query_5, 0, 0)
     piece_6 = passed(gate(full_f, piece_5), 1, core_f, 1, wide_b, tokens, 2 * tokens)
     piece_7 = passed(gate(full_f, piece_6), 2, core_7, 0, wide_b, 3 * tokens, 4 * tokens)
     recv_2 = gate(recv_2, piece_7)

time: 108 us -> 106 us (0.981)
  waiting for transfers between devices: 42.8 us -> 39.9 us
    ppermute x14 -> x15, waiting for transfers between devices: 14.2 us -> 10.6 us  [exchange(): lax.ppermute(value, axis, [(i, i ^ bit) for i in range(lax.axis_size(axis...]
    ppermute x14 -> x15, starting transfers between devices: 11.5 us -> 12.1 us  [exchange(): lax.ppermute(value, axis, [(i, i ^ bit) for i in range(lax.axis_size(axis...]
  transfers between devices with their start and end apart: 20 -> 21, of which waited for: 11 -> 11; matrix products, arithmetic and copies ran while one was open for 0% -> 0% of each run, Pallas kernels for 35% -> 38%
where the time goes in v6:
time: 106 us; the launch traced here: 105 us
  Pallas kernels  41 us (39%)
  waiting for transfers between devices  39.9 us (38%)
  starting transfers between devices  22 us (21%)
  local copies, waits for them, and re-layouts  1.22 us (1%)
    pallas_call x8, Pallas kernels, attend(): pl.pallas_call(functools.partial(attend_kernel, tokens, column, query_row...  32.9 us
    ppermute x6, waiting for transfers between devices, from_groups_behind(): return lax.ppermute(value, 'ctx', pairs)  29.3 us
    ppermute x15, starting transfers between devices, exchange(): lax.ppermute(value, axis, [(i, i ^ bit) for i in range(lax.axis_size(axis...  12.1 us
    ppermute x15, waiting for transfers between devices, exchange(): lax.ppermute(value, axis, [(i, i ^ bit) for i in range(lax.axis_size(axis...  10.6 us
    ppermute x6, starting transfers between devices, from_groups_behind(): return lax.ppermute(value, 'ctx', pairs)  9.85 us
    pallas_call x1, Pallas kernels, pack_wide(): pl.pallas_call(functools.partial(pack_wide_kernel, parts), in_specs=[pl.B...  2.85 us
    pallas_call x2, Pallas kernels, assemble(): pl.pallas_call(functools.partial(assemble_kernel, places), in_specs=[pl.B...  2.36 us
  transfers between devices with their start and end apart: 21, of which 11 were waited for; matrix products, arithmetic and copies ran while one was open for 0% of the time, Pallas kernels for 38%

profile of v6, /device:TPU:18, one launch (start us, length us, event | category | flops | bytes accessed | tf_op | source)
XLA Modules:
  0.0 104.8 jit_solution(13531727574841662682)
XLA Ops:
  0.0 1.0 slice.44
  1.6 2.1 %pack_first.1 = (bf16[208,768]{1,0:T(8,128)(2,1)}, bf16[208,512]{1,0:T(8,128)(2,1)}, bf16[160,1024]{1,0:T(8,128)(2,1)}) custom-call(bf16[192,1024]{1,0:T(8,128)(2,1)} %bitcast.18, bf16[192,1024]{1,0:T(8,128)(2,1)} %bitcast.19, s32[1,192]{1,0:T(1,128)} %seg_in.1), custom_call_target="tpu_custom_call" | custom-call | flops 1 | bytes 1 | tf_op jit(solution)/shard_map/pack_first/pallas_call | solution.py:148
  3.7 1.6 %collective-permute-start.2 = (bf16[160,1024]{1,0:T(8,128)(2,1)}, bf16[160,1024]{1,0:T(8,128)(2,1)S(1)}, u32[]{:S(2)}, u32[]{:S(2)}) collective-permute-start(bf16[160,1024]{1,0:T(8,128)(2,1)} %get-tuple-element.39), channel_id=1, source_target_pairs={{0,16},{16,0},{1,17},{17,1},{2,18},{18,2},{3,19},{19,3},{4,20},{20... | collective-permute-start | bytes 983048 | tf_op jit(solution)/shard_map/ppermute | solution.py:36
  5.6 3.5 %collective-permute-start = (bf16[208,768]{1,0:T(8,128)(2,1)}, bf16[208,768]{1,0:T(8,128)(2,1)S(1)}, u32[]{:S(2)}, u32[]{:S(2)}) collective-permute-start(bf16[208,768]{1,0:T(8,128)(2,1)} %get-tuple-element.47.refs_1_.refs_2_.refs_0_), channel_id=1, source_target_pairs={{0,4},{1,5},{2,6},{3,7},{4,8},{5,9},{6,10},{7,11},{8,12},{9,13},{1... | collective-permute-start | bytes 958472 | tf_op jit(solution)/shard_map/ppermute | solution.py:44
  9.1 2.8 %pack_wide.1 = bf16[960,1024]{1,0:T(8,128)(2,1)} custom-call(bf16[192,8192]{1,0:T(8,128)(2,1)} %bitcast.6, bf16[192,8192]{1,0:T(8,128)(2,1)} %bitcast.12), custom_call_target="tpu_custom_call" | custom-call | flops 1 | bytes 1 | tf_op jit(solution)/shard_map/pack_wide/pallas_call | solution.py:183
  12.6 6.4 %collective-permute-done.1.refs_2_.refs_3_ = bf16[208,768]{1,0:T(8,128)(2,1)S(1)} collective-permute-done((bf16[208,768]{1,0:T(8,128)(2,1)}, bf16[208,768]{1,0:T(8,128)(2,1)S(1)}, u32[]{:S(2)}, u32[]{:S(2)}) %collective-permute-start.1) | collective-permute-done | bytes 319520 | tf_op jit(solution)/shard_map/ppermute | solution.py:44
  19.0 9.8 %collective-permute-done.refs_0_.refs_1_ = bf16[208,768]{1,0:T(8,128)(2,1)S(1)} collective-permute-done((bf16[208,768]{1,0:T(8,128)(2,1)}, bf16[208,768]{1,0:T(8,128)(2,1)S(1)}, u32[]{:S(2)}, u32[]{:S(2)}) %collective-permute-start) | collective-permute-done | bytes 319520 | tf_op jit(solution)/shard_map/ppermute | solution.py:44
  28.9 1.6 %collective-permute-start.6 = (bf16[416,768]{1,0:T(8,128)(2,1)S(1)}, bf16[416,768]{1,0:T(8,128)(2,1)S(1)}, u32[]{:S(2)}, u32[]{:S(2)}) collective-permute-start(bf16[416,768]{1,0:T(8,128)(2,1)S(1)} %join.9), channel_id=1, source_target_pairs={{0,2},{1,3},{2,0},{3,1},{4,6},{5,7},{6,4},{7,5},{8,10},{9,11},{10,... | collective-permute-start | bytes 1916936 | tf_op jit(solution)/shard_map/ppermute | solution.py:36
  30.5 3.0 %collective-permute-start.4 = (bf16[208,512]{1,0:T(8,128)(2,1)S(1)}, bf16[208,512]{1,0:T(8,128)(2,1)S(1)}, u32[]{:S(2)}, u32[]{:S(2)}) collective-permute-start(bf16[208,512]{1,0:T(8,128)(2,1)S(1)} %copy-done.3), channel_id=1, source_target_pairs={{0,4},{1,5},{2,6},{3,7},{4,8},{5,9},{6,10},{7,11},{8,12},{9,13},{1... | collective-permute-start | bytes 638984 | tf_op jit(solution)/shard_map/ppermute | solution.py:44
  33.5 6.2 %collective-permute-done.5.refs_2_.refs_3_ = bf16[208,512]{1,0:T(8,128)(2,1)S(1)} collective-permute-done((bf16[208,512]{1,0:T(8,128)(2,1)S(1)}, bf16[208,512]{1,0:T(8,128)(2,1)S(1)}, u32[]{:S(2)}, u32[]{:S(2)}) %collective-permute-start.5) | collective-permute-done | bytes 213024 | tf_op jit(solution)/shard_map/ppermute | solution.py:44
  39.8 4.7 %collective-permute-done.4.refs_0_.refs_1_ = bf16[208,512]{1,0:T(8,128)(2,1)S(1)} collective-permute-done((bf16[208,512]{1,0:T(8,128)(2,1)S(1)}, bf16[208,512]{1,0:T(8,128)(2,1)S(1)}, u32[]{:S(2)}, u32[]{:S(2)}) %collective-permute-start.4) | collective-permute-done | bytes 213024 | tf_op jit(solution)/shard_map/ppermute | solution.py:44
  44.5 0.8 collective-permute-done.6.refs_1_.refs_2_.refs_3_
  46.2 1.6 %collective-permute-start.13 = (bf16[416,512]{1,0:T(8,128)(2,1)S(1)}, bf16[416,512]{1,0:T(8,128)(2,1)S(1)}, u32[]{:S(2)}, u32[]{:S(2)}) collective-permute-start(bf16[416,512]{1,0:T(8,128)(2,1)S(1)} %join.12), channel_id=1, source_target_pairs={{0,2},{1,3},{2,0},{3,1},{4,6},{5,7},{6,4},{7,5},{8,10},{9,11},{10,... | collective-permute-start | bytes 1277960 | tf_op jit(solution)/shard_map/ppermute | solution.py:36
  47.8 3.0 %collective-permute-start.11 = (bf16[208,768]{1,0:T(8,128)(2,1)S(1)}, bf16[208,768]{1,0:T(8,128)(2,1)S(1)}, u32[]{:S(2)}, u32[]{:S(2)}) collective-permute-start(bf16[208,768]{1,0:T(8,128)(2,1)S(1)} %unfold.1.refs_1_.refs_2_.refs_0_), channel_id=1, source_target_pairs={{0,4},{1,5},{2,6},{3,7},{4,8},{5,9},{6,10},{7,11},{8,12},{9,13},{1... | collective-permute-start | bytes 958472 | tf_op jit(solution)/shard_map/ppermute | solution.py:44
  50.8 4.0 %attend.8 = bf16[192,1024]{1,0:T(8,128)(2,1)S(1)} custom-call(bf16[208,768]{1,0:T(8,128)(2,1)S(1)} %copy-done.2, bf16[208,768]{1,0:T(8,128)(2,1)S(1)} %collective-permute-done.refs_0_.refs_1_, bf16[416,768]{1,0:T(8,128)(2,1)S(1)} %collective-permute-done.6.refs_1_.refs_2_.refs_3_, bf16[416,768]{1,0:T(8,128)(2,1)S(1)} %collective-permute-done.6.refs_1_.refs_2_.refs_3_, ...), custom_call_target="tpu_custom_call" | custom-call | flops 1 | bytes 1 | tf_op jit(solution)/shard_map/attend/pallas_call | solution.py:313
  54.9 0.6 collective-permute-start.8
  55.5 4.0 %attend.9 = bf16[192,1024]{1,0:T(8,128)(2,1)S(1)} custom-call(bf16[208,768]{1,0:T(8,128)(2,1)S(1)} %copy-done.2, bf16[208,768]{1,0:T(8,128)(2,1)S(1)} %collective-permute-done.refs_0_.refs_1_, bf16[416,768]{1,0:T(8,128)(2,1)S(1)} %collective-permute-done.6.refs_1_.refs_2_.refs_3_, bf16[416,768]{1,0:T(8,128)(2,1)S(1)} %collective-permute-done.6.refs_1_.refs_2_.refs_3_, ...), custom_call_target="tpu_custom_call" | custom-call | flops 1 | bytes 1 | tf_op jit(solution)/shard_map/attend/pallas_call | solution.py:313
  59.5 4.0 %attend.10 = bf16[192,1024]{1,0:T(8,128)(2,1)S(1)} custom-call(bf16[208,768]{1,0:T(8,128)(2,1)S(1)} %copy-done.2, bf16[208,768]{1,0:T(8,128)(2,1)S(1)} %collective-permute-done.refs_0_.refs_1_, bf16[416,768]{1,0:T(8,128)(2,1)S(1)} %collective-permute-done.6.refs_1_.refs_2_.refs_3_, bf16[416,768]{1,0:T(8,128)(2,1)S(1)} %collective-permute-done.6.refs_1_.refs_2_.refs_3_, ...), custom_call_target="tpu_custom_call" | custom-call | flops 1 | bytes 1 | tf_op jit(solution)/shard_map/attend/pallas_call | solution.py:313
  63.6 1.6 %collective-permute-start.10 = (bf16[384,1024]{1,0:T(8,128)(2,1)S(1)}, bf16[384,1024]{1,0:T(8,128)(2,1)S(1)}, u32[]{:S(2)}, u32[]{:S(2)}) collective-permute-start(bf16[384,1024]{1,0:T(8,128)(2,1)S(1)} %pad_maximum_fusion.1), channel_id=1, source_target_pairs={{0,16},{16,0},{1,17},{17,1},{2,18},{18,2},{3,19},{19,3},{4,20},{20... | collective-permute-start | bytes 2359304 | tf_op jit(solution)/shard_map/ppermute | solution.py:36
  65.2 2.1 %collective-permute-done.11.refs_0_.refs_1_ = bf16[208,768]{1,0:T(8,128)(2,1)S(1)} collective-permute-done((bf16[208,768]{1,0:T(8,128)(2,1)S(1)}, bf16[208,768]{1,0:T(8,128)(2,1)S(1)}, u32[]{:S(2)}, u32[]{:S(2)}) %collective-permute-start.11) | collective-permute-done | bytes 319520 | tf_op jit(solution)/shard_map/ppermute | solution.py:44
  67.3 1.3 %collective-permute-done.8.refs_0_ = bf16[144,1024]{1,0:T(8,128)(2,1)S(1)} collective-permute-done((bf16[144,1024]{1,0:T(8,128)(2,1)S(1)}, bf16[144,1024]{1,0:T(8,128)(2,1)S(1)}, u32[]{:S(2)}, u32[]{:S(2)}) %collective-permute-start.8) | collective-permute-done | bytes 294944 | tf_op jit(solution)/shard_map/ppermute | solution.py:36
  68.8 1.6 %collective-permute-start.17 = (bf16[416,768]{1,0:T(8,128)(2,1)S(1)}, bf16[416,768]{1,0:T(8,128)(2,1)S(1)}, u32[]{:S(2)}, u32[]{:S(2)}) collective-permute-start(bf16[416,768]{1,0:T(8,128)(2,1)S(1)} %join.15), channel_id=1, source_target_pairs={{0,2},{1,3},{2,0},{3,1},{4,6},{5,7},{6,4},{7,5},{8,10},{9,11},{10,... | collective-permute-start | bytes 1916936 | tf_op jit(solution)/shard_map/ppermute | solution.py:36
  71.1 1.2 %collective-permute-done.15.refs_4_.refs_5_.refs_6_.refs_7_ = bf16[832,256]{1,0:T(8,128)(2,1)S(1)} collective-permute-done((bf16[832,256]{1,0:T(8,128)(2,1)S(1)}, bf16[832,256]{1,0:T(8,128)(2,1)S(1)}, u32[]{:S(2)}, u32[]{:S(2)}) %collective-permute-start.15) | collective-permute-done | bytes 426016 | tf_op jit(solution)/shard_map/ppermute | solution.py:36
  72.3 4.0 %attend.11 = bf16[192,1024]{1,0:T(8,128)(2,1)S(1)} custom-call(bf16[208,512]{1,0:T(8,128)(2,1)S(1)} %copy-done.3, bf16[208,512]{1,0:T(8,128)(2,1)S(1)} %collective-permute-done.4.refs_0_.refs_1_, bf16[416,512]{1,0:T(8,128)(2,1)S(1)} %collective-permute-done.13.refs_1_.refs_2_.refs_3_, bf16[416,512]{1,0:T(8,128)(2,1)S(1)} %collective-permute-done.13.refs_1_.refs_2_.refs_3_, ...), custom_call_target="tpu_custom_call" | custom-call | flops 1 | bytes 1 | tf_op jit(solution)/shard_map/attend/pallas_call | solution.py:313
  76.3 4.0 %attend.12 = bf16[192,1024]{1,0:T(8,128)(2,1)S(1)} custom-call(bf16[208,512]{1,0:T(8,128)(2,1)S(1)} %copy-done.3, bf16[208,512]{1,0:T(8,128)(2,1)S(1)} %collective-permute-done.4.refs_0_.refs_1_, bf16[416,512]{1,0:T(8,128)(2,1)S(1)} %collective-permute-done.13.refs_1_.refs_2_.refs_3_, bf16[416,512]{1,0:T(8,128)(2,1)S(1)} %collective-permute-done.13.refs_1_.refs_2_.refs_3_, ...), custom_call_target="tpu_custom_call" | custom-call | flops 1 | bytes 1 | tf_op jit(solution)/shard_map/attend/pallas_call | solution.py:313
  80.9 4.5 %collective-permute-done.10 = bf16[384,1024]{1,0:T(8,128)(2,1)S(1)} collective-permute-done((bf16[384,1024]{1,0:T(8,128)(2,1)S(1)}, bf16[384,1024]{1,0:T(8,128)(2,1)S(1)}, u32[]{:S(2)}, u32[]{:S(2)}) %collective-permute-start.10) | collective-permute-done | bytes 786464 | tf_op jit(solution)/shard_map/ppermute | solution.py:36
  85.6 1.0 assemble.2.refs_0_
  87.9 4.3 %attend.13.refs_1_ = bf16[192,1024]{1,0:T(8,128)(2,1)S(1)} custom-call(bf16[208,768]{1,0:T(8,128)(2,1)S(1)} %unfold.1.refs_1_.refs_2_.refs_0_, bf16[208,768]{1,0:T(8,128)(2,1)S(1)} %collective-permute-done.11.refs_0_.refs_1_, bf16[416,768]{1,0:T(8,128)(2,1)S(1)} %collective-permute-done.17.refs_1_.refs_2_.refs_3_, ...), custom_call_target="tpu_custom_call" | custom-call | flops 1 | bytes 1 | tf_op jit(solution)/shard_map/attend/pallas_call | solution.py:313
  92.3 4.3 %attend.14.refs_2_ = bf16[192,1024]{1,0:T(8,128)(2,1)S(1)} custom-call(bf16[208,768]{1,0:T(8,128)(2,1)S(1)} %unfold.1.refs_1_.refs_2_.refs_0_, bf16[208,768]{1,0:T(8,128)(2,1)S(1)} %collective-permute-done.11.refs_0_.refs_1_, bf16[416,768]{1,0:T(8,128)(2,1)S(1)} %collective-permute-done.17.refs_1_.refs_2_.refs_3_, ...), custom_call_target="tpu_custom_call" | custom-call | flops 1 | bytes 1 | tf_op jit(solution)/shard_map/attend/pallas_call | solution.py:313
  96.6 4.3 %attend.15.refs_3_ = bf16[192,1024]{1,0:T(8,128)(2,1)S(1)} custom-call(bf16[208,768]{1,0:T(8,128)(2,1)S(1)} %unfold.1.refs_1_.refs_2_.refs_0_, bf16[208,768]{1,0:T(8,128)(2,1)S(1)} %collective-permute-done.11.refs_0_.refs_1_, bf16[416,768]{1,0:T(8,128)(2,1)S(1)} %collective-permute-done.17.refs_1_.refs_2_.refs_3_, ...), custom_call_target="tpu_custom_call" | custom-call | flops 1 | bytes 1 | tf_op jit(solution)/shard_map/attend/pallas_call | solution.py:313
  100.9 2.3 %collective-permute-done.20 = bf16[432,1024]{1,0:T(8,128)(2,1)S(1)} collective-permute-done((bf16[432,1024]{1,0:T(8,128)(2,1)S(1)}, bf16[432,1024]{1,0:T(8,128)(2,1)S(1)}, u32[]{:S(2)}, u32[]{:S(2)}) %collective-permute-start.20) | collective-permute-done | bytes 884768 | tf_op jit(solution)/shard_map/ppermute | solution.py:36
  103.3 1.4 %assemble.3 = bf16[192,8192]{1,0:T(8,128)(2,1)} custom-call(bf16[192,8192]{1,0:T(8,128)(2,1)} %assemble.2.refs_0_, bf16[192,1024]{1,0:T(8,128)(2,1)S(1)} %attend.13.refs_1_, bf16[192,1024]{1,0:T(8,128)(2,1)S(1)} %attend.14.refs_2_, bf16[192,1024]{1,0:T(8,128)(2,1)S(1)} %attend.15.refs_3_, ...), custom_call_target="tpu_custom_call", output_to_operand_aliasing={{}: (0, {})} | custom-call | flops 1 | bytes 1 | tf_op jit(solution)/shard_map/assemble/pallas_call | solution.py:355
  (55 shorter events, 5.7 us)
Async XLA Ops:
  1.0 27.8 %collective-permute-start.3 = (bf16[192,1024]{1,0:T(8,128)(2,1)S(1)}, bf16[192,1024]{1,0:T(8,128)(2,1)S(1)}, u32[]{:S(2)}, u32[]{:S(2)}) collective-permute-start(bf16[192,1024]{1,0:T(8,128)(2,1)S(1)} %slice.44), channel_id=1, source_target_pairs={{0,16},{16,0},{1,17},{17,1},{2,18},{18,2},{3,19},{19,3},{4,20},{20... | collective-permute-start | bytes 1179656 | tf_op jit(solution)/shard_map/ppermute | solution.py:36
  3.7 25.1 %collective-permute-start.2 = (bf16[160,1024]{1,0:T(8,128)(2,1)}, bf16[160,1024]{1,0:T(8,128)(2,1)S(1)}, u32[]{:S(2)}, u32[]{:S(2)}) collective-permute-start(bf16[160,1024]{1,0:T(8,128)(2,1)} %get-tuple-element.39), channel_id=1, source_target_pairs={{0,16},{16,0},{1,17},{17,1},{2,18},{18,2},{3,19},{19,3},{4,20},{20... | collective-permute-start | bytes 983048 | tf_op jit(solution)/shard_map/ppermute | solution.py:36
  5.3 13.7 %collective-permute-start.1 = (bf16[208,768]{1,0:T(8,128)(2,1)}, bf16[208,768]{1,0:T(8,128)(2,1)S(1)}, u32[]{:S(2)}, u32[]{:S(2)}) collective-permute-start(bf16[208,768]{1,0:T(8,128)(2,1)} %get-tuple-element.47.refs_1_.refs_2_.refs_0_), channel_id=1, source_target_pairs={{0,8},{1,9},{2,10},{3,11},{4,12},{5,13},{6,14},{7,15},{8,0},{9,1},... | collective-permute-start | bytes 958472 | tf_op jit(solution)/shard_map/ppermute | solution.py:44
  5.6 23.2 %collective-permute-start = (bf16[208,768]{1,0:T(8,128)(2,1)}, bf16[208,768]{1,0:T(8,128)(2,1)S(1)}, u32[]{:S(2)}, u32[]{:S(2)}) collective-permute-start(bf16[208,768]{1,0:T(8,128)(2,1)} %get-tuple-element.47.refs_1_.refs_2_.refs_0_), channel_id=1, source_target_pairs={{0,4},{1,5},{2,6},{3,7},{4,8},{5,9},{6,10},{7,11},{8,12},{9,13},{1... | collective-permute-start | bytes 958472 | tf_op jit(solution)/shard_map/ppermute | solution.py:44
  9.1 19.8 %copy-start.2 = (bf16[208,768]{1,0:T(8,128)(2,1)S(1)}, bf16[208,768]{1,0:T(8,128)(2,1)}, u32[]{:S(2)}) copy-start(bf16[208,768]{1,0:T(8,128)(2,1)} %get-tuple-element.47.refs_1_.refs_2_.refs_0_) | copy-start | bytes 958468
  9.1 21.4 %copy-start.3 = (bf16[208,512]{1,0:T(8,128)(2,1)S(1)}, bf16[208,512]{1,0:T(8,128)(2,1)}, u32[]{:S(2)}) copy-start(bf16[208,512]{1,0:T(8,128)(2,1)} %get-tuple-element.55.refs_1_.refs_2_.refs_0_) | copy-start | bytes 638980
  12.0 55.3 %collective-permute-start.14 = (bf16[960,1024]{1,0:T(8,128)(2,1)}, bf16[960,1024]{1,0:T(8,128)(2,1)S(1)}, u32[]{:S(2)}, u32[]{:S(2)}) collective-permute-start(bf16[960,1024]{1,0:T(8,128)(2,1)} %pack_wide.1), channel_id=1, source_target_pairs={{0,16},{16,0},{1,17},{17,1},{2,18},{18,2},{3,19},{19,3},{4,20},{20... | collective-permute-start | bytes 5898248 | tf_op jit(solution)/shard_map/ppermute | solution.py:36
  28.9 21.9 %copy-start.1 = (bf16[1,192,8192]{2,1,0:T(8,128)(2,1)S(1)}, bf16[1,192,8192]{2,1,0:T(8,128)(2,1)}, u32[]{:S(2)}) copy-start(bf16[1,192,8192]{2,1,0:T(8,128)(2,1)} %param.5) | copy-start | bytes 9437188
  28.9 16.4 %collective-permute-start.6 = (bf16[416,768]{1,0:T(8,128)(2,1)S(1)}, bf16[416,768]{1,0:T(8,128)(2,1)S(1)}, u32[]{:S(2)}, u32[]{:S(2)}) collective-permute-start(bf16[416,768]{1,0:T(8,128)(2,1)S(1)} %join.9), channel_id=1, source_target_pairs={{0,2},{1,3},{2,0},{3,1},{4,6},{5,7},{6,4},{7,5},{8,10},{9,11},{10,... | collective-permute-start | bytes 1916936 | tf_op jit(solution)/shard_map/ppermute | solution.py:36
  30.5 9.3 %collective-permute-start.5 = (bf16[208,512]{1,0:T(8,128)(2,1)S(1)}, bf16[208,512]{1,0:T(8,128)(2,1)S(1)}, u32[]{:S(2)}, u32[]{:S(2)}) collective-permute-start(bf16[208,512]{1,0:T(8,128)(2,1)S(1)} %copy-done.3), channel_id=1, source_target_pairs={{0,8},{1,9},{2,10},{3,11},{4,12},{5,13},{6,14},{7,15},{8,0},{9,1},... | collective-permute-start | bytes 638984 | tf_op jit(solution)/shard_map/ppermute | solution.py:44
  30.5 13.9 %collective-permute-start.4 = (bf16[208,512]{1,0:T(8,128)(2,1)S(1)}, bf16[208,512]{1,0:T(8,128)(2,1)S(1)}, u32[]{:S(2)}, u32[]{:S(2)}) collective-permute-start(bf16[208,512]{1,0:T(8,128)(2,1)S(1)} %copy-done.3), channel_id=1, source_target_pairs={{0,4},{1,5},{2,6},{3,7},{4,8},{5,9},{6,10},{7,11},{8,12},{9,13},{1... | collective-permute-start | bytes 638984 | tf_op jit(solution)/shard_map/ppermute | solution.py:44
  45.4 5.4 %copy-start = (bf16[1,192,8192]{2,1,0:T(8,128)(2,1)S(1)}, bf16[1,192,8192]{2,1,0:T(8,128)(2,1)}, u32[]{:S(2)}) copy-start(bf16[1,192,8192]{2,1,0:T(8,128)(2,1)} %param.6) | copy-start | bytes 9437188
  45.4 2.4 %collective-permute-start.7 = (bf16[832,512]{1,0:T(8,128)(2,1)S(1)}, bf16[832,512]{1,0:T(8,128)(2,1)S(1)}, u32[]{:S(2)}, u32[]{:S(2)}) collective-permute-start(bf16[832,512]{1,0:T(8,128)(2,1)S(1)} %join.10), channel_id=1, source_target_pairs={{0,1},{1,0},{2,3},{3,2},{4,5},{5,4},{6,7},{7,6},{8,9},{9,8},{10,11... | collective-permute-start | bytes 2555912 | tf_op jit(solution)/shard_map/ppermute | solution.py:36
  45.5 9.4 %collective-permute-start.9 = (bf16[832,256]{1,0:T(8,128)(2,1)S(1)}, bf16[832,256]{1,0:T(8,128)(2,1)S(1)}, u32[]{:S(2)}, u32[]{:S(2)}) collective-permute-start(bf16[832,256]{1,0:T(8,128)(2,1)S(1)} %join.11), channel_id=1, source_target_pairs={{0,1},{1,0},{2,3},{3,2},{4,5},{5,4},{6,7},{7,6},{8,9},{9,8},{10,11... | collective-permute-start | bytes 1277960 | tf_op jit(solution)/shard_map/ppermute | solution.py:36
  46.1 17.5 %collective-permute-start.12 = (bf16[208,768]{1,0:T(8,128)(2,1)S(1)}, bf16[208,768]{1,0:T(8,128)(2,1)S(1)}, u32[]{:S(2)}, u32[]{:S(2)}) collective-permute-start(bf16[208,768]{1,0:T(8,128)(2,1)S(1)} %unfold.1.refs_1_.refs_2_.refs_0_), channel_id=1, source_target_pairs={{0,8},{1,9},{2,10},{3,11},{4,12},{5,13},{6,14},{7,15},{8,0},{9,1},... | collective-permute-start | bytes 958472 | tf_op jit(solution)/shard_map/ppermute | solution.py:44
  46.2 21.1 %collective-permute-start.13 = (bf16[416,512]{1,0:T(8,128)(2,1)S(1)}, bf16[416,512]{1,0:T(8,128)(2,1)S(1)}, u32[]{:S(2)}, u32[]{:S(2)}) collective-permute-start(bf16[416,512]{1,0:T(8,128)(2,1)S(1)} %join.12), channel_id=1, source_target_pairs={{0,2},{1,3},{2,0},{3,1},{4,6},{5,7},{6,4},{7,5},{8,10},{9,11},{10,... | collective-permute-start | bytes 1277960 | tf_op jit(solution)/shard_map/ppermute | solution.py:36
  47.8 19.4 %collective-permute-start.11 = (bf16[208,768]{1,0:T(8,128)(2,1)S(1)}, bf16[208,768]{1,0:T(8,128)(2,1)S(1)}, u32[]{:S(2)}, u32[]{:S(2)}) collective-permute-start(bf16[208,768]{1,0:T(8,128)(2,1)S(1)} %unfold.1.refs_1_.refs_2_.refs_0_), channel_id=1, source_target_pairs={{0,4},{1,5},{2,6},{3,7},{4,8},{5,9},{6,10},{7,11},{8,12},{9,13},{1... | collective-permute-start | bytes 958472 | tf_op jit(solution)/shard_map/ppermute | solution.py:44
  54.9 13.7 %collective-permute-start.8 = (bf16[144,1024]{1,0:T(8,128)(2,1)S(1)}, bf16[144,1024]{1,0:T(8,128)(2,1)S(1)}, u32[]{:S(2)}, u32[]{:S(2)}) collective-permute-start(bf16[144,1024]{1,0:T(8,128)(2,1)S(1)} %slice.45), channel_id=1, source_target_pairs={{0,16},{16,0},{1,17},{17,1},{2,18},{18,2},{3,19},{19,3},{4,20},{20... | collective-permute-start | bytes 884744 | tf_op jit(solution)/shard_map/ppermute | solution.py:36
  63.5 7.6 %copy-start.4 = (bf16[192,1024]{1,0:T(8,128)(2,1)}, bf16[192,1024]{1,0:T(8,128)(2,1)S(1)}, u32[]{:S(2)}) copy-start(bf16[192,1024]{1,0:T(8,128)(2,1)S(1)} %attend.10) | copy-start | bytes 1179652
  63.6 21.8 %collective-permute-start.10 = (bf16[384,1024]{1,0:T(8,128)(2,1)S(1)}, bf16[384,1024]{1,0:T(8,128)(2,1)S(1)}, u32[]{:S(2)}, u32[]{:S(2)}) collective-permute-start(bf16[384,1024]{1,0:T(8,128)(2,1)S(1)} %pad_maximum_fusion.1), channel_id=1, source_target_pairs={{0,16},{16,0},{1,17},{17,1},{2,18},{18,2},{3,19},{19,3},{4,20},{20... | collective-permute-start | bytes 2359304 | tf_op jit(solution)/shard_map/ppermute | solution.py:36
  68.8 16.6 %collective-permute-start.17 = (bf16[416,768]{1,0:T(8,128)(2,1)S(1)}, bf16[416,768]{1,0:T(8,128)(2,1)S(1)}, u32[]{:S(2)}, u32[]{:S(2)}) collective-permute-start(bf16[416,768]{1,0:T(8,128)(2,1)S(1)} %join.15), channel_id=1, source_target_pairs={{0,2},{1,3},{2,0},{3,1},{4,6},{5,7},{6,4},{7,5},{8,10},{9,11},{10,... | collective-permute-start | bytes 1916936 | tf_op jit(solution)/shard_map/ppermute | solution.py:36
  70.4 1.8 %collective-permute-start.15 = (bf16[832,256]{1,0:T(8,128)(2,1)S(1)}, bf16[832,256]{1,0:T(8,128)(2,1)S(1)}, u32[]{:S(2)}, u32[]{:S(2)}) collective-permute-start(bf16[832,256]{1,0:T(8,128)(2,1)S(1)} %join.13), channel_id=1, source_target_pairs={{0,1},{1,0},{2,3},{3,2},{4,5},{5,4},{6,7},{7,6},{8,9},{9,8},{10,11... | collective-permute-start | bytes 1277960 | tf_op jit(solution)/shard_map/ppermute | solution.py:36
  70.5 5.7 %collective-permute-start.16 = (bf16[832,256]{1,0:T(8,128)(2,1)S(1)}, bf16[832,256]{1,0:T(8,128)(2,1)S(1)}, u32[]{:S(2)}, u32[]{:S(2)}) collective-permute-start(bf16[832,256]{1,0:T(8,128)(2,1)S(1)} %join.14), channel_id=1, source_target_pairs={{0,1},{1,0},{2,3},{3,2},{4,5},{5,4},{6,7},{7,6},{8,9},{9,8},{10,11... | collective-permute-start | bytes 1277960 | tf_op jit(solution)/shard_map/ppermute | solution.py:36
  76.2 4.0 %slice-start = ((bf16[192,1024]{1,0:T(8,128)(2,1)}), bf16[48,1024]{1,0:T(8,128)(2,1)S(1)}, s32[]{:S(2)}) async-start(bf16[192,1024]{1,0:T(8,128)(2,1)} %copy-done.4), calls=%async_computation | async-start | bytes 196608 | tf_op jit(solution)/shard_map/slice | solution.py:413
  80.3 22.9 %collective-permute-start.20 = (bf16[432,1024]{1,0:T(8,128)(2,1)S(1)}, bf16[432,1024]{1,0:T(8,128)(2,1)S(1)}, u32[]{:S(2)}, u32[]{:S(2)}) collective-permute-start(bf16[432,1024]{1,0:T(8,128)(2,1)S(1)} %pad_maximum_fusion), channel_id=1, source_target_pairs={{0,16},{16,0},{1,17},{17,1},{2,18},{18,2},{3,19},{19,3},{4,20},{20... | collective-permute-start | bytes 2654216 | tf_op jit(solution)/shard_map/ppermute | solution.py:36
  85.5 2.4 %collective-permute-start.18 = (bf16[832,512]{1,0:T(8,128)(2,1)S(1)}, bf16[832,512]{1,0:T(8,128)(2,1)S(1)}, u32[]{:S(2)}, u32[]{:S(2)}) collective-permute-start(bf16[832,512]{1,0:T(8,128)(2,1)S(1)} %join.16), channel_id=1, source_target_pairs={{0,1},{1,0},{2,3},{3,2},{4,5},{5,4},{6,7},{7,6},{8,9},{9,8},{10,11... | collective-permute-start | bytes 2555912 | tf_op jit(solution)/shard_map/ppermute | solution.py:36
  86.9 9.7 %collective-permute-start.19 = (bf16[832,256]{1,0:T(8,128)(2,1)S(1)}, bf16[832,256]{1,0:T(8,128)(2,1)S(1)}, u32[]{:S(2)}, u32[]{:S(2)}) collective-permute-start(bf16[832,256]{1,0:T(8,128)(2,1)S(1)} %join.17), channel_id=1, source_target_pairs={{0,1},{1,0},{2,3},{3,2},{4,5},{5,4},{6,7},{7,6},{8,9},{9,8},{10,11... | collective-permute-start | bytes 1277960 | tf_op jit(solution)/shard_map/ppermute | solution.py:36

commit v7 on v6

--- a/solution.py
+++ b/solution.py
@@ -104,26 +104,12 @@
         out[tokens : tokens + 1, n * PAIR : n * PAIR + tokens] = row
 
 
-def fold_places(rows, size):
-    per_row = WIDTH // PAIR
-    tiles = [(n, r) for n in range(size) for r in range(rows // SEG_ROWS)]
-    return [
-        (r * SEG_ROWS, n * PAIR, t // per_row * SEG_ROWS, t % per_row * PAIR)
-        for t, (n, r) in enumerate(tiles)
-    ]
-
-
-def pack_first_kernel(chunks, passed, keys_in, values_in, seg_in, *refs):
-    *blocks, out, block, keys, values, seg, sems = refs
-    tokens = keys_in.shape[0]
+def pack_first_kernel(chunks, keys_in, values_in, seg_in, *refs):
+    *blocks, keys, values, seg, sems = refs
     copies = [
         pltpu.make_async_copy(source, target, sems.at[n])
         for n, (source, target) in enumerate(
-            (
-                (keys_in, keys),
-                (values_in, values),
-                (seg_in, seg),
-            )
+            ((keys_in, keys), (values_in, values), (seg_in, seg))
         )
     ]
     for copy in copies:
@@ -131,27 +117,18 @@
     for copy in copies:
         copy.wait()
     for target, chunk in zip(blocks, chunks):
-        fill_block(target, tokens, chunk, keys, values, seg)
-    fill_block(block, tokens, passed, keys, values, seg)
-    for row, column, to_row, to_column in fold_places(block.shape[0], passed[1]):
-        out[to_row : to_row + SEG_ROWS, to_column : to_column + PAIR] = block[
-            row : row + SEG_ROWS, column : column + PAIR
-        ]
-
-
-def pack_first(keys, values, segments, chunks, passed):
-    tokens = keys.shape[0]
-    block = lambda chunk: (tokens + SEG_ROWS, chunk[1] * PAIR)
-    folded = max(place[2] for place in fold_places(tokens + SEG_ROWS, passed[1])) + SEG_ROWS
-    shapes = [block(chunk) for chunk in chunks] + [(folded, WIDTH)]
+        fill_block(target, keys.shape[0], chunk, keys, values, seg)
+
+
+def pack_first(keys, values, segments, chunks):
+    shapes = [(keys.shape[0] + SEG_ROWS, size * PAIR) for _, size in chunks]
     vmem = pl.BlockSpec(memory_space=pltpu.VMEM)
     return pl.pallas_call(
-        functools.partial(pack_first_kernel, chunks, passed),
+        functools.partial(pack_first_kernel, chunks),
         in_specs=[pl.BlockSpec(memory_space=pltpu.HBM)] * 3,
         out_specs=[vmem] * len(shapes),
         out_shape=[jax.ShapeDtypeStruct(shape, jnp.bfloat16) for shape in shapes],
         scratch_shapes=[
-            pltpu.VMEM(block(passed), jnp.bfloat16),
             pltpu.VMEM(keys.shape, jnp.bfloat16),
             pltpu.VMEM(values.shape, jnp.bfloat16),
             pltpu.VMEM(segments.shape, segments.dtype),
@@ -190,26 +167,6 @@
         compiler_params=pltpu.CompilerParams(vmem_limit_bytes=56 * 2**20),
         name="pack_wide",
     )(queries, stream)
-
-
-def unfold_kernel(base, size, wide, out):
-    for row, column, at_row, at_column in fold_places(out.shape[0], size):
-        out[row : row + SEG_ROWS, column : column + PAIR] = wide[
-            base + at_row : base + at_row + SEG_ROWS, at_column : at_column + PAIR
-        ]
-
-
-def unfold(wide, base, tokens, chunk):
-    vmem = pl.BlockSpec(memory_space=pltpu.VMEM)
-    return pl.pallas_call(
-        functools.partial(unfold_kernel, base, chunk[1]),
-        in_specs=[vmem],
-        out_specs=vmem,
-        out_shape=jax.ShapeDtypeStruct((tokens + SEG_ROWS, chunk[1] * PAIR), jnp.bfloat16),
-        cost_estimate=LIGHT,
-        compiler_params=pltpu.CompilerParams(vmem_limit_bytes=8 * 2**20),
-        name="unfold",
-    )(wide)
 
 
 def attend_kernel(tokens, column, query_row, stream_row, *refs):
@@ -385,12 +342,11 @@
     query_5 = queries[:, 5 * WIDTH : 6 * WIDTH]
     keys = gate(keys, query_5)
     query_5 = relay(query_5)
-    block_a, block_b, wide_a = pack_first(keys, values, segments, (chunk_a, chunk_b), chunk_f)
-    wide_a = relay(wide_a)
+    block_a, block_b, block_f = pack_first(keys, values, segments, (chunk_a, chunk_b, chunk_f))
+    block_f = relay(block_f)
     behind_a = gather_behind(block_a)
     wide_b = pack_wide(gate(queries, block_a), stream, ((1, 5), (0, 6), (1, 6), (0, 7), (1, 7)))
-    wide_b, behind_a = relay(wide_b), gate(behind_a, wide_a, query_5)
-    block_f = unfold(wide_a, 0, tokens, chunk_f)
+    wide_b, behind_a = relay(wide_b), gate(behind_a, block_f, query_5)
     behind_b = gather_behind(gate(block_b, behind_a))
     y_a = over_y(block_a, behind_a, whole(chunk_a))
     behind_f = gather_behind(gate(block_f, behind_b, y_a))
@@ -426,16 +382,19 @@
     piece_5 = passed(full_f, 0, core_f, 0, query_5, 0, 0)
     piece_6 = passed(gate(full_f, piece_5), 1, core_f, 1, wide_b, tokens, 2 * tokens)
     piece_7 = passed(gate(full_f, piece_6), 2, core_7, 0, wide_b, 3 * tokens, 4 * tokens)
-    recv_2 = gate(recv_2, piece_7)
     late = [
         (piece_5, (0, 5 * WIDTH)),
         (piece_6, (0, 6 * WIDTH)),
         (piece_7, (0, 7 * WIDTH)),
+    ]
+    out = assemble(out, late, queries.shape, LIGHT)
+    recv_2 = gate(recv_2, out)
+    last = [
         (recv_2[:rest], (cut, 2 * WIDTH)),
         (recv_2[rest : rest + tokens], (0, 3 * WIDTH)),
         (recv_2[rest + tokens :], (0, 4 * WIDTH)),
     ]
-    return assemble(out, late, queries.shape, LIGHT)[None]
+    return assemble(out, last, queries.shape, LIGHT)[None]
 
 
 def solution(mesh):

time: 106 us -> 106 us (level)
    ppermute x6, waiting for transfers between devices: 29.3 us -> 22 us  [from_groups_behind(): return lax.ppermute(value, 'ctx', pairs)]
    ppermute x15, waiting for transfers between devices: 10.6 us -> 16.9 us  [exchange(): lax.ppermute(value, axis, [(i, i ^ bit) for i in range(lax.axis_size(axis...]
    pallas_call x2 -> x3, Pallas kernels: 2.36 us -> 2.98 us  [assemble(): pl.pallas_call(functools.partial(assemble_kernel, places), in_specs=[pl.B...]
    pallas_call x2 -> x1, Pallas kernels: 2.13 us -> 2.11 us  [pack_first(): pl.pallas_call(functools.partial(pack_first_kernel, chunks), in_specs=[pl...]
  transfers between devices with their start and end apart: 21 -> 21, of which waited for: 11 -> 12; matrix products, arithmetic and copies ran while one was open for 0% -> 0% of each run, Pallas kernels for 38% -> 39%
where the time goes in v7:
time: 106 us; the launch traced here: 104 us
  Pallas kernels  41.6 us (39%)
  waiting for transfers between devices  38.9 us (37%)
  starting transfers between devices  21.8 us (21%)
  local copies, waits for them, and re-layouts  1.21 us (1%)
    pallas_call x8, Pallas kernels, attend(): pl.pallas_call(functools.partial(attend_kernel, tokens, column, query_row...  32.9 us
    ppermute x6, waiting for transfers between devices, from_groups_behind(): return lax.ppermute(value, 'ctx', pairs)  22 us
    ppermute x15, waiting for transfers between devices, exchange(): lax.ppermute(value, axis, [(i, i ^ bit) for i in range(lax.axis_size(axis...  16.9 us
    ppermute x15, starting transfers between devices, exchange(): lax.ppermute(value, axis, [(i, i ^ bit) for i in range(lax.axis_size(axis...  12.1 us
    ppermute x6, starting transfers between devices, from_groups_behind(): return lax.ppermute(value, 'ctx', pairs)  9.67 us
    pallas_call x3, Pallas kernels, assemble(): pl.pallas_call(functools.partial(assemble_kernel, places), in_specs=[pl.B...  2.98 us
    pallas_call x1, Pallas kernels, pack_wide(): pl.pallas_call(functools.partial(pack_wide_kernel, parts), in_specs=[pl.B...  2.85 us
  transfers between devices with their start and end apart: 21, of which 12 were waited for; matrix products, arithmetic and copies ran while one was open for 0% of the time, Pallas kernels for 39%

profile of v7, /device:TPU:18, one launch (start us, length us, event | category | flops | bytes accessed | tf_op | source)
XLA Modules:
  0.0 104.2 jit_solution(18376468452764749341)
XLA Ops:
  0.0 1.0 slice.44
  1.6 2.1 %pack_first.1 = (bf16[208,768]{1,0:T(8,128)(2,1)}, bf16[208,512]{1,0:T(8,128)(2,1)}, bf16[208,768]{1,0:T(8,128)(2,1)}) custom-call(bf16[192,1024]{1,0:T(8,128)(2,1)} %bitcast.18, bf16[192,1024]{1,0:T(8,128)(2,1)} %bitcast.19, s32[1,192]{1,0:T(1,128)} %seg_in.1), custom_call_target="tpu_custom_call" | custom-call | flops 1 | bytes 1 | tf_op jit(solution)/shard_map/pack_first/pallas_call | solution.py:126
  3.7 1.6 %collective-permute-start.2 = (bf16[208,768]{1,0:T(8,128)(2,1)}, bf16[208,768]{1,0:T(8,128)(2,1)S(1)}, u32[]{:S(2)}, u32[]{:S(2)}) collective-permute-start(bf16[208,768]{1,0:T(8,128)(2,1)} %get-tuple-element.39), channel_id=1, source_target_pairs={{0,16},{16,0},{1,17},{17,1},{2,18},{18,2},{3,19},{19,3},{4,20},{20... | collective-permute-start | bytes 958472 | tf_op jit(solution)/shard_map/ppermute | solution.py:36
  5.6 3.5 %collective-permute-start = (bf16[208,768]{1,0:T(8,128)(2,1)}, bf16[208,768]{1,0:T(8,128)(2,1)S(1)}, u32[]{:S(2)}, u32[]{:S(2)}) collective-permute-start(bf16[208,768]{1,0:T(8,128)(2,1)} %get-tuple-element.47.refs_1_.refs_2_.refs_0_), channel_id=1, source_target_pairs={{0,4},{1,5},{2,6},{3,7},{4,8},{5,9},{6,10},{7,11},{8,12},{9,13},{1... | collective-permute-start | bytes 958472 | tf_op jit(solution)/shard_map/ppermute | solution.py:44
  9.1 2.8 %pack_wide.1 = bf16[960,1024]{1,0:T(8,128)(2,1)} custom-call(bf16[192,8192]{1,0:T(8,128)(2,1)} %bitcast.6, bf16[192,8192]{1,0:T(8,128)(2,1)} %bitcast.12), custom_call_target="tpu_custom_call" | custom-call | flops 1 | bytes 1 | tf_op jit(solution)/shard_map/pack_wide/pallas_call | solution.py:160
  12.6 7.3 %collective-permute-done.2.refs_1_.refs_2_.refs_0_ = bf16[208,768]{1,0:T(8,128)(2,1)S(1)} collective-permute-done((bf16[208,768]{1,0:T(8,128)(2,1)}, bf16[208,768]{1,0:T(8,128)(2,1)S(1)}, u32[]{:S(2)}, u32[]{:S(2)}) %collective-permute-start.2) | collective-permute-done | bytes 319520 | tf_op jit(solution)/shard_map/ppermute | solution.py:36
  19.9 8.9 %collective-permute-done.refs_0_.refs_1_ = bf16[208,768]{1,0:T(8,128)(2,1)S(1)} collective-permute-done((bf16[208,768]{1,0:T(8,128)(2,1)}, bf16[208,768]{1,0:T(8,128)(2,1)S(1)}, u32[]{:S(2)}, u32[]{:S(2)}) %collective-permute-start) | collective-permute-done | bytes 319520 | tf_op jit(solution)/shard_map/ppermute | solution.py:44
  28.9 1.6 %collective-permute-start.6 = (bf16[416,768]{1,0:T(8,128)(2,1)S(1)}, bf16[416,768]{1,0:T(8,128)(2,1)S(1)}, u32[]{:S(2)}, u32[]{:S(2)}) collective-permute-start(bf16[416,768]{1,0:T(8,128)(2,1)S(1)} %join.9), channel_id=1, source_target_pairs={{0,2},{1,3},{2,0},{3,1},{4,6},{5,7},{6,4},{7,5},{8,10},{9,11},{10,... | collective-permute-start | bytes 1916936 | tf_op jit(solution)/shard_map/ppermute | solution.py:36
  30.5 3.0 %collective-permute-start.4 = (bf16[208,512]{1,0:T(8,128)(2,1)S(1)}, bf16[208,512]{1,0:T(8,128)(2,1)S(1)}, u32[]{:S(2)}, u32[]{:S(2)}) collective-permute-start(bf16[208,512]{1,0:T(8,128)(2,1)S(1)} %copy-done.3), channel_id=1, source_target_pairs={{0,4},{1,5},{2,6},{3,7},{4,8},{5,9},{6,10},{7,11},{8,12},{9,13},{1... | collective-permute-start | bytes 638984 | tf_op jit(solution)/shard_map/ppermute | solution.py:44
  33.5 6.3 %collective-permute-done.5.refs_2_.refs_3_ = bf16[208,512]{1,0:T(8,128)(2,1)S(1)} collective-permute-done((bf16[208,512]{1,0:T(8,128)(2,1)S(1)}, bf16[208,512]{1,0:T(8,128)(2,1)S(1)}, u32[]{:S(2)}, u32[]{:S(2)}) %collective-permute-start.5) | collective-permute-done | bytes 213024 | tf_op jit(solution)/shard_map/ppermute | solution.py:44
  39.8 4.7 %collective-permute-done.4.refs_0_.refs_1_ = bf16[208,512]{1,0:T(8,128)(2,1)S(1)} collective-permute-done((bf16[208,512]{1,0:T(8,128)(2,1)S(1)}, bf16[208,512]{1,0:T(8,128)(2,1)S(1)}, u32[]{:S(2)}, u32[]{:S(2)}) %collective-permute-start.4) | collective-permute-done | bytes 213024 | tf_op jit(solution)/shard_map/ppermute | solution.py:44
  44.4 0.9 collective-permute-done.6.refs_1_.refs_2_.refs_3_
  46.1 1.6 %collective-permute-start.13 = (bf16[416,512]{1,0:T(8,128)(2,1)S(1)}, bf16[416,512]{1,0:T(8,128)(2,1)S(1)}, u32[]{:S(2)}, u32[]{:S(2)}) collective-permute-start(bf16[416,512]{1,0:T(8,128)(2,1)S(1)} %join.12), channel_id=1, source_target_pairs={{0,2},{1,3},{2,0},{3,1},{4,6},{5,7},{6,4},{7,5},{8,10},{9,11},{10,... | collective-permute-start | bytes 1277960 | tf_op jit(solution)/shard_map/ppermute | solution.py:36
  47.8 2.9 %collective-permute-start.11 = (bf16[208,768]{1,0:T(8,128)(2,1)S(1)}, bf16[208,768]{1,0:T(8,128)(2,1)S(1)}, u32[]{:S(2)}, u32[]{:S(2)}) collective-permute-start(bf16[208,768]{1,0:T(8,128)(2,1)S(1)} %collective-permute-done.2.refs_1_.refs_2_.refs_0_), channel_id=1, source_target_pairs={{0,4},{1,5},{2,6},{3,7},{4,8},{5,9},{6,10},{7,11},{8,12},{9,13},{1... | collective-permute-start | bytes 958472 | tf_op jit(solution)/shard_map/ppermute | solution.py:44
  50.7 4.0 %attend.8 = bf16[192,1024]{1,0:T(8,128)(2,1)S(1)} custom-call(bf16[208,768]{1,0:T(8,128)(2,1)S(1)} %copy-done.2, bf16[208,768]{1,0:T(8,128)(2,1)S(1)} %collective-permute-done.refs_0_.refs_1_, bf16[416,768]{1,0:T(8,128)(2,1)S(1)} %collective-permute-done.6.refs_1_.refs_2_.refs_3_, bf16[416,768]{1,0:T(8,128)(2,1)S(1)} %collective-permute-done.6.refs_1_.refs_2_.refs_3_, ...), custom_call_target="tpu_custom_call" | custom-call | flops 1 | bytes 1 | tf_op jit(solution)/shard_map/attend/pallas_call | solution.py:270
  55.4 4.0 %attend.9 = bf16[192,1024]{1,0:T(8,128)(2,1)S(1)} custom-call(bf16[208,768]{1,0:T(8,128)(2,1)S(1)} %copy-done.2, bf16[208,768]{1,0:T(8,128)(2,1)S(1)} %collective-permute-done.refs_0_.refs_1_, bf16[416,768]{1,0:T(8,128)(2,1)S(1)} %collective-permute-done.6.refs_1_.refs_2_.refs_3_, bf16[416,768]{1,0:T(8,128)(2,1)S(1)} %collective-permute-done.6.refs_1_.refs_2_.refs_3_, ...), custom_call_target="tpu_custom_call" | custom-call | flops 1 | bytes 1 | tf_op jit(solution)/shard_map/attend/pallas_call | solution.py:270
  59.4 4.0 %attend.10 = bf16[192,1024]{1,0:T(8,128)(2,1)S(1)} custom-call(bf16[208,768]{1,0:T(8,128)(2,1)S(1)} %copy-done.2, bf16[208,768]{1,0:T(8,128)(2,1)S(1)} %collective-permute-done.refs_0_.refs_1_, bf16[416,768]{1,0:T(8,128)(2,1)S(1)} %collective-permute-done.6.refs_1_.refs_2_.refs_3_, bf16[416,768]{1,0:T(8,128)(2,1)S(1)} %collective-permute-done.6.refs_1_.refs_2_.refs_3_, ...), custom_call_target="tpu_custom_call" | custom-call | flops 1 | bytes 1 | tf_op jit(solution)/shard_map/attend/pallas_call | solution.py:270
  63.5 1.6 %collective-permute-start.10 = (bf16[384,1024]{1,0:T(8,128)(2,1)S(1)}, bf16[384,1024]{1,0:T(8,128)(2,1)S(1)}, u32[]{:S(2)}, u32[]{:S(2)}) collective-permute-start(bf16[384,1024]{1,0:T(8,128)(2,1)S(1)} %pad_maximum_fusion.1), channel_id=1, source_target_pairs={{0,16},{16,0},{1,17},{17,1},{2,18},{18,2},{3,19},{19,3},{4,20},{20... | collective-permute-start | bytes 2359304 | tf_op jit(solution)/shard_map/ppermute | solution.py:36
  65.0 2.2 %collective-permute-done.11.refs_0_.refs_1_ = bf16[208,768]{1,0:T(8,128)(2,1)S(1)} collective-permute-done((bf16[208,768]{1,0:T(8,128)(2,1)S(1)}, bf16[208,768]{1,0:T(8,128)(2,1)S(1)}, u32[]{:S(2)}, u32[]{:S(2)}) %collective-permute-start.11) | collective-permute-done | bytes 319520 | tf_op jit(solution)/shard_map/ppermute | solution.py:44
  67.2 1.2 %collective-permute-done.8.refs_0_ = bf16[144,1024]{1,0:T(8,128)(2,1)S(1)} collective-permute-done((bf16[144,1024]{1,0:T(8,128)(2,1)S(1)}, bf16[144,1024]{1,0:T(8,128)(2,1)S(1)}, u32[]{:S(2)}, u32[]{:S(2)}) %collective-permute-start.8) | collective-permute-done | bytes 294944 | tf_op jit(solution)/shard_map/ppermute | solution.py:36
  68.6 1.6 %collective-permute-start.17 = (bf16[416,768]{1,0:T(8,128)(2,1)S(1)}, bf16[416,768]{1,0:T(8,128)(2,1)S(1)}, u32[]{:S(2)}, u32[]{:S(2)}) collective-permute-start(bf16[416,768]{1,0:T(8,128)(2,1)S(1)} %join.15), channel_id=1, source_target_pairs={{0,2},{1,3},{2,0},{3,1},{4,6},{5,7},{6,4},{7,5},{8,10},{9,11},{10,... | collective-permute-start | bytes 1916936 | tf_op jit(solution)/shard_map/ppermute | solution.py:36
  70.9 1.2 %collective-permute-done.15.refs_4_.refs_5_.refs_6_.refs_7_ = bf16[832,256]{1,0:T(8,128)(2,1)S(1)} collective-permute-done((bf16[832,256]{1,0:T(8,128)(2,1)S(1)}, bf16[832,256]{1,0:T(8,128)(2,1)S(1)}, u32[]{:S(2)}, u32[]{:S(2)}) %collective-permute-start.15) | collective-permute-done | bytes 426016 | tf_op jit(solution)/shard_map/ppermute | solution.py:36
  72.1 4.0 %attend.11 = bf16[192,1024]{1,0:T(8,128)(2,1)S(1)} custom-call(bf16[208,512]{1,0:T(8,128)(2,1)S(1)} %copy-done.3, bf16[208,512]{1,0:T(8,128)(2,1)S(1)} %collective-permute-done.4.refs_0_.refs_1_, bf16[416,512]{1,0:T(8,128)(2,1)S(1)} %collective-permute-done.13.refs_1_.refs_2_.refs_3_, bf16[416,512]{1,0:T(8,128)(2,1)S(1)} %collective-permute-done.13.refs_1_.refs_2_.refs_3_, ...), custom_call_target="tpu_custom_call" | custom-call | flops 1 | bytes 1 | tf_op jit(solution)/shard_map/attend/pallas_call | solution.py:270
  76.1 4.0 %attend.12 = bf16[192,1024]{1,0:T(8,128)(2,1)S(1)} custom-call(bf16[208,512]{1,0:T(8,128)(2,1)S(1)} %copy-done.3, bf16[208,512]{1,0:T(8,128)(2,1)S(1)} %collective-permute-done.4.refs_0_.refs_1_, bf16[416,512]{1,0:T(8,128)(2,1)S(1)} %collective-permute-done.13.refs_1_.refs_2_.refs_3_, bf16[416,512]{1,0:T(8,128)(2,1)S(1)} %collective-permute-done.13.refs_1_.refs_2_.refs_3_, ...), custom_call_target="tpu_custom_call" | custom-call | flops 1 | bytes 1 | tf_op jit(solution)/shard_map/attend/pallas_call | solution.py:270
  80.8 4.4 %collective-permute-done.10 = bf16[384,1024]{1,0:T(8,128)(2,1)S(1)} collective-permute-done((bf16[384,1024]{1,0:T(8,128)(2,1)S(1)}, bf16[384,1024]{1,0:T(8,128)(2,1)S(1)}, u32[]{:S(2)}, u32[]{:S(2)}) %collective-permute-start.10) | collective-permute-done | bytes 786464 | tf_op jit(solution)/shard_map/ppermute | solution.py:36
  85.4 1.0 assemble.3.refs_0_
  87.7 4.3 %attend.13.refs_1_ = bf16[192,1024]{1,0:T(8,128)(2,1)S(1)} custom-call(bf16[208,768]{1,0:T(8,128)(2,1)S(1)} %collective-permute-done.2.refs_1_.refs_2_.refs_0_, bf16[208,768]{1,0:T(8,128)(2,1)S(1)} %collective-permute-done.11.refs_0_.refs_1_, bf16[416,768]{1,0:T(8,128)(2,1)S(1)} %collective-permute-done.17.refs_1_.refs_2_.refs_3_, ...), custom_call_target="tpu_custom_call" | custom-call | flops 1 | bytes 1 | tf_op jit(solution)/shard_map/attend/pallas_call | solution.py:270
  92.0 4.3 %attend.14.refs_2_ = bf16[192,1024]{1,0:T(8,128)(2,1)S(1)} custom-call(bf16[208,768]{1,0:T(8,128)(2,1)S(1)} %collective-permute-done.2.refs_1_.refs_2_.refs_0_, bf16[208,768]{1,0:T(8,128)(2,1)S(1)} %collective-permute-done.11.refs_0_.refs_1_, bf16[416,768]{1,0:T(8,128)(2,1)S(1)} %collective-permute-done.17.refs_1_.refs_2_.refs_3_, ...), custom_call_target="tpu_custom_call" | custom-call | flops 1 | bytes 1 | tf_op jit(solution)/shard_map/attend/pallas_call | solution.py:270
  96.4 4.3 %attend.15.refs_3_ = bf16[192,1024]{1,0:T(8,128)(2,1)S(1)} custom-call(bf16[208,768]{1,0:T(8,128)(2,1)S(1)} %collective-permute-done.2.refs_1_.refs_2_.refs_0_, bf16[208,768]{1,0:T(8,128)(2,1)S(1)} %collective-permute-done.11.refs_0_.refs_1_, bf16[416,768]{1,0:T(8,128)(2,1)S(1)} %collective-permute-done.17.refs_1_.refs_2_.refs_3_, ...), custom_call_target="tpu_custom_call" | custom-call | flops 1 | bytes 1 | tf_op jit(solution)/shard_map/attend/pallas_call | solution.py:270
  100.7 1.0 assemble.4.refs_0_
  101.7 1.3 %collective-permute-done.20 = bf16[432,1024]{1,0:T(8,128)(2,1)S(1)} collective-permute-done((bf16[432,1024]{1,0:T(8,128)(2,1)S(1)}, bf16[432,1024]{1,0:T(8,128)(2,1)S(1)}, u32[]{:S(2)}, u32[]{:S(2)}) %collective-permute-start.20) | collective-permute-done | bytes 884768 | tf_op jit(solution)/shard_map/ppermute | solution.py:36
  103.1 0.9 assemble.5
  (55 shorter events, 6.3 us)
Async XLA Ops:
  1.0 27.8 %collective-permute-start.3 = (bf16[192,1024]{1,0:T(8,128)(2,1)S(1)}, bf16[192,1024]{1,0:T(8,128)(2,1)S(1)}, u32[]{:S(2)}, u32[]{:S(2)}) collective-permute-start(bf16[192,1024]{1,0:T(8,128)(2,1)S(1)} %slice.44), channel_id=1, source_target_pairs={{0,16},{16,0},{1,17},{17,1},{2,18},{18,2},{3,19},{19,3},{4,20},{20... | collective-permute-start | bytes 1179656 | tf_op jit(solution)/shard_map/ppermute | solution.py:36
  3.7 16.2 %collective-permute-start.2 = (bf16[208,768]{1,0:T(8,128)(2,1)}, bf16[208,768]{1,0:T(8,128)(2,1)S(1)}, u32[]{:S(2)}, u32[]{:S(2)}) collective-permute-start(bf16[208,768]{1,0:T(8,128)(2,1)} %get-tuple-element.39), channel_id=1, source_target_pairs={{0,16},{16,0},{1,17},{17,1},{2,18},{18,2},{3,19},{19,3},{4,20},{20... | collective-permute-start | bytes 958472 | tf_op jit(solution)/shard_map/ppermute | solution.py:36
  5.3 14.6 %collective-permute-start.1 = (bf16[208,768]{1,0:T(8,128)(2,1)}, bf16[208,768]{1,0:T(8,128)(2,1)S(1)}, u32[]{:S(2)}, u32[]{:S(2)}) collective-permute-start(bf16[208,768]{1,0:T(8,128)(2,1)} %get-tuple-element.47.refs_1_.refs_2_.refs_0_), channel_id=1, source_target_pairs={{0,8},{1,9},{2,10},{3,11},{4,12},{5,13},{6,14},{7,15},{8,0},{9,1},... | collective-permute-start | bytes 958472 | tf_op jit(solution)/shard_map/ppermute | solution.py:44
  5.6 23.2 %collective-permute-start = (bf16[208,768]{1,0:T(8,128)(2,1)}, bf16[208,768]{1,0:T(8,128)(2,1)S(1)}, u32[]{:S(2)}, u32[]{:S(2)}) collective-permute-start(bf16[208,768]{1,0:T(8,128)(2,1)} %get-tuple-element.47.refs_1_.refs_2_.refs_0_), channel_id=1, source_target_pairs={{0,4},{1,5},{2,6},{3,7},{4,8},{5,9},{6,10},{7,11},{8,12},{9,13},{1... | collective-permute-start | bytes 958472 | tf_op jit(solution)/shard_map/ppermute | solution.py:44
  9.1 19.8 %copy-start.2 = (bf16[208,768]{1,0:T(8,128)(2,1)S(1)}, bf16[208,768]{1,0:T(8,128)(2,1)}, u32[]{:S(2)}) copy-start(bf16[208,768]{1,0:T(8,128)(2,1)} %get-tuple-element.47.refs_1_.refs_2_.refs_0_) | copy-start | bytes 958468
  9.1 21.4 %copy-start.3 = (bf16[208,512]{1,0:T(8,128)(2,1)S(1)}, bf16[208,512]{1,0:T(8,128)(2,1)}, u32[]{:S(2)}) copy-start(bf16[208,512]{1,0:T(8,128)(2,1)} %get-tuple-element.55.refs_1_.refs_2_.refs_0_) | copy-start | bytes 638980
  12.0 55.2 %collective-permute-start.14 = (bf16[960,1024]{1,0:T(8,128)(2,1)}, bf16[960,1024]{1,0:T(8,128)(2,1)S(1)}, u32[]{:S(2)}, u32[]{:S(2)}) collective-permute-start(bf16[960,1024]{1,0:T(8,128)(2,1)} %pack_wide.1), channel_id=1, source_target_pairs={{0,16},{16,0},{1,17},{17,1},{2,18},{18,2},{3,19},{19,3},{4,20},{20... | collective-permute-start | bytes 5898248 | tf_op jit(solution)/shard_map/ppermute | solution.py:36
  28.9 21.8 %copy-start.1 = (bf16[1,192,8192]{2,1,0:T(8,128)(2,1)S(1)}, bf16[1,192,8192]{2,1,0:T(8,128)(2,1)}, u32[]{:S(2)}) copy-start(bf16[1,192,8192]{2,1,0:T(8,128)(2,1)} %param.5) | copy-start | bytes 9437188
  28.9 16.4 %collective-permute-start.6 = (bf16[416,768]{1,0:T(8,128)(2,1)S(1)}, bf16[416,768]{1,0:T(8,128)(2,1)S(1)}, u32[]{:S(2)}, u32[]{:S(2)}) collective-permute-start(bf16[416,768]{1,0:T(8,128)(2,1)S(1)} %join.9), channel_id=1, source_target_pairs={{0,2},{1,3},{2,0},{3,1},{4,6},{5,7},{6,4},{7,5},{8,10},{9,11},{10,... | collective-permute-start | bytes 1916936 | tf_op jit(solution)/shard_map/ppermute | solution.py:36
  30.5 9.3 %collective-permute-start.5 = (bf16[208,512]{1,0:T(8,128)(2,1)S(1)}, bf16[208,512]{1,0:T(8,128)(2,1)S(1)}, u32[]{:S(2)}, u32[]{:S(2)}) collective-permute-start(bf16[208,512]{1,0:T(8,128)(2,1)S(1)} %copy-done.3), channel_id=1, source_target_pairs={{0,8},{1,9},{2,10},{3,11},{4,12},{5,13},{6,14},{7,15},{8,0},{9,1},... | collective-permute-start | bytes 638984 | tf_op jit(solution)/shard_map/ppermute | solution.py:44
  30.5 13.9 %collective-permute-start.4 = (bf16[208,512]{1,0:T(8,128)(2,1)S(1)}, bf16[208,512]{1,0:T(8,128)(2,1)S(1)}, u32[]{:S(2)}, u32[]{:S(2)}) collective-permute-start(bf16[208,512]{1,0:T(8,128)(2,1)S(1)} %copy-done.3), channel_id=1, source_target_pairs={{0,4},{1,5},{2,6},{3,7},{4,8},{5,9},{6,10},{7,11},{8,12},{9,13},{1... | collective-permute-start | bytes 638984 | tf_op jit(solution)/shard_map/ppermute | solution.py:44
  45.3 5.4 %copy-start = (bf16[1,192,8192]{2,1,0:T(8,128)(2,1)S(1)}, bf16[1,192,8192]{2,1,0:T(8,128)(2,1)}, u32[]{:S(2)}) copy-start(bf16[1,192,8192]{2,1,0:T(8,128)(2,1)} %param.6) | copy-start | bytes 9437188
  45.4 2.4 %collective-permute-start.7 = (bf16[832,512]{1,0:T(8,128)(2,1)S(1)}, bf16[832,512]{1,0:T(8,128)(2,1)S(1)}, u32[]{:S(2)}, u32[]{:S(2)}) collective-permute-start(bf16[832,512]{1,0:T(8,128)(2,1)S(1)} %join.10), channel_id=1, source_target_pairs={{0,1},{1,0},{2,3},{3,2},{4,5},{5,4},{6,7},{7,6},{8,9},{9,8},{10,11... | collective-permute-start | bytes 2555912 | tf_op jit(solution)/shard_map/ppermute | solution.py:36
  45.5 9.3 %collective-permute-start.9 = (bf16[832,256]{1,0:T(8,128)(2,1)S(1)}, bf16[832,256]{1,0:T(8,128)(2,1)S(1)}, u32[]{:S(2)}, u32[]{:S(2)}) collective-permute-start(bf16[832,256]{1,0:T(8,128)(2,1)S(1)} %join.11), channel_id=1, source_target_pairs={{0,1},{1,0},{2,3},{3,2},{4,5},{5,4},{6,7},{7,6},{8,9},{9,8},{10,11... | collective-permute-start | bytes 1277960 | tf_op jit(solution)/shard_map/ppermute | solution.py:36
  46.0 17.4 %collective-permute-start.12 = (bf16[208,768]{1,0:T(8,128)(2,1)S(1)}, bf16[208,768]{1,0:T(8,128)(2,1)S(1)}, u32[]{:S(2)}, u32[]{:S(2)}) collective-permute-start(bf16[208,768]{1,0:T(8,128)(2,1)S(1)} %collective-permute-done.2.refs_1_.refs_2_.refs_0_), channel_id=1, source_target_pairs={{0,8},{1,9},{2,10},{3,11},{4,12},{5,13},{6,14},{7,15},{8,0},{9,1},... | collective-permute-start | bytes 958472 | tf_op jit(solution)/shard_map/ppermute | solution.py:44
  46.1 21.1 %collective-permute-start.13 = (bf16[416,512]{1,0:T(8,128)(2,1)S(1)}, bf16[416,512]{1,0:T(8,128)(2,1)S(1)}, u32[]{:S(2)}, u32[]{:S(2)}) collective-permute-start(bf16[416,512]{1,0:T(8,128)(2,1)S(1)} %join.12), channel_id=1, source_target_pairs={{0,2},{1,3},{2,0},{3,1},{4,6},{5,7},{6,4},{7,5},{8,10},{9,11},{10,... | collective-permute-start | bytes 1277960 | tf_op jit(solution)/shard_map/ppermute | solution.py:36
  47.8 19.4 %collective-permute-start.11 = (bf16[208,768]{1,0:T(8,128)(2,1)S(1)}, bf16[208,768]{1,0:T(8,128)(2,1)S(1)}, u32[]{:S(2)}, u32[]{:S(2)}) collective-permute-start(bf16[208,768]{1,0:T(8,128)(2,1)S(1)} %collective-permute-done.2.refs_1_.refs_2_.refs_0_), channel_id=1, source_target_pairs={{0,4},{1,5},{2,6},{3,7},{4,8},{5,9},{6,10},{7,11},{8,12},{9,13},{1... | collective-permute-start | bytes 958472 | tf_op jit(solution)/shard_map/ppermute | solution.py:44
  54.8 13.6 %collective-permute-start.8 = (bf16[144,1024]{1,0:T(8,128)(2,1)S(1)}, bf16[144,1024]{1,0:T(8,128)(2,1)S(1)}, u32[]{:S(2)}, u32[]{:S(2)}) collective-permute-start(bf16[144,1024]{1,0:T(8,128)(2,1)S(1)} %slice.45), channel_id=1, source_target_pairs={{0,16},{16,0},{1,17},{17,1},{2,18},{18,2},{3,19},{19,3},{4,20},{20... | collective-permute-start | bytes 884744 | tf_op jit(solution)/shard_map/ppermute | solution.py:36
  63.4 7.6 %copy-start.4 = (bf16[192,1024]{1,0:T(8,128)(2,1)}, bf16[192,1024]{1,0:T(8,128)(2,1)S(1)}, u32[]{:S(2)}) copy-start(bf16[192,1024]{1,0:T(8,128)(2,1)S(1)} %attend.10) | copy-start | bytes 1179652
  63.5 21.7 %collective-permute-start.10 = (bf16[384,1024]{1,0:T(8,128)(2,1)S(1)}, bf16[384,1024]{1,0:T(8,128)(2,1)S(1)}, u32[]{:S(2)}, u32[]{:S(2)}) collective-permute-start(bf16[384,1024]{1,0:T(8,128)(2,1)S(1)} %pad_maximum_fusion.1), channel_id=1, source_target_pairs={{0,16},{16,0},{1,17},{17,1},{2,18},{18,2},{3,19},{19,3},{4,20},{20... | collective-permute-start | bytes 2359304 | tf_op jit(solution)/shard_map/ppermute | solution.py:36
  68.6 16.6 %collective-permute-start.17 = (bf16[416,768]{1,0:T(8,128)(2,1)S(1)}, bf16[416,768]{1,0:T(8,128)(2,1)S(1)}, u32[]{:S(2)}, u32[]{:S(2)}) collective-permute-start(bf16[416,768]{1,0:T(8,128)(2,1)S(1)} %join.15), channel_id=1, source_target_pairs={{0,2},{1,3},{2,0},{3,1},{4,6},{5,7},{6,4},{7,5},{8,10},{9,11},{10,... | collective-permute-start | bytes 1916936 | tf_op jit(solution)/shard_map/ppermute | solution.py:36
  70.2 1.8 %collective-permute-start.15 = (bf16[832,256]{1,0:T(8,128)(2,1)S(1)}, bf16[832,256]{1,0:T(8,128)(2,1)S(1)}, u32[]{:S(2)}, u32[]{:S(2)}) collective-permute-start(bf16[832,256]{1,0:T(8,128)(2,1)S(1)} %join.13), channel_id=1, source_target_pairs={{0,1},{1,0},{2,3},{3,2},{4,5},{5,4},{6,7},{7,6},{8,9},{9,8},{10,11... | collective-permute-start | bytes 1277960 | tf_op jit(solution)/shard_map/ppermute | solution.py:36
  70.4 5.7 %collective-permute-start.16 = (bf16[832,256]{1,0:T(8,128)(2,1)S(1)}, bf16[832,256]{1,0:T(8,128)(2,1)S(1)}, u32[]{:S(2)}, u32[]{:S(2)}) collective-permute-start(bf16[832,256]{1,0:T(8,128)(2,1)S(1)} %join.14), channel_id=1, source_target_pairs={{0,1},{1,0},{2,3},{3,2},{4,5},{5,4},{6,7},{7,6},{8,9},{9,8},{10,11... | collective-permute-start | bytes 1277960 | tf_op jit(solution)/shard_map/ppermute | solution.py:36
  76.1 4.0 %slice-start = ((bf16[192,1024]{1,0:T(8,128)(2,1)}), bf16[48,1024]{1,0:T(8,128)(2,1)S(1)}, s32[]{:S(2)}) async-start(bf16[192,1024]{1,0:T(8,128)(2,1)} %copy-done.4), calls=%async_computation | async-start | bytes 196608 | tf_op jit(solution)/shard_map/slice | solution.py:369
  80.2 22.9 %collective-permute-start.20 = (bf16[432,1024]{1,0:T(8,128)(2,1)S(1)}, bf16[432,1024]{1,0:T(8,128)(2,1)S(1)}, u32[]{:S(2)}, u32[]{:S(2)}) collective-permute-start(bf16[432,1024]{1,0:T(8,128)(2,1)S(1)} %pad_maximum_fusion), channel_id=1, source_target_pairs={{0,16},{16,0},{1,17},{17,1},{2,18},{18,2},{3,19},{19,3},{4,20},{20... | collective-permute-start | bytes 2654216 | tf_op jit(solution)/shard_map/ppermute | solution.py:36
  85.2 2.4 %collective-permute-start.18 = (bf16[832,512]{1,0:T(8,128)(2,1)S(1)}, bf16[832,512]{1,0:T(8,128)(2,1)S(1)}, u32[]{:S(2)}, u32[]{:S(2)}) collective-permute-start(bf16[832,512]{1,0:T(8,128)(2,1)S(1)} %join.16), channel_id=1, source_target_pairs={{0,1},{1,0},{2,3},{3,2},{4,5},{5,4},{6,7},{7,6},{8,9},{9,8},{10,11... | collective-permute-start | bytes 2555912 | tf_op jit(solution)/shard_map/ppermute | solution.py:36
  86.7 9.7 %collective-permute-start.19 = (bf16[832,256]{1,0:T(8,128)(2,1)S(1)}, bf16[832,256]{1,0:T(8,128)(2,1)S(1)}, u32[]{:S(2)}, u32[]{:S(2)}) collective-permute-start(bf16[832,256]{1,0:T(8,128)(2,1)S(1)} %join.17), channel_id=1, source_target_pairs={{0,1},{1,0},{2,3},{3,2},{4,5},{5,4},{6,7},{7,6},{8,9},{9,8},{10,11... | collective-permute-start | bytes 1277960 | tf_op jit(solution)/shard_map/ppermute | solution.py:36
